TPU v7x, 512 devices: a whole 4x8x8 slice. The times are simulated.
512 devices in a mesh: grp: 4 (over x), dom: 128 (over y, z, core).
Axes of the slice: x: 4, y: 8, z: 8, core: 2. Of those that a mesh axis runs over, the one named last changes fastest.
Arguments:
- positions: float32 [3, 2097152], P(None, ('grp', 'dom')), may hold values from -6 to 6
- velocities: float32 [3, 2097152], P(None, ('grp', 'dom')), may hold values from -6 to 6
- particle_volume: float32 [2097152], P(('grp', 'dom')), may hold values from 0.5 to 2
- drag_coef: float32 [2097152], P(('grp', 'dom')), may hold values from 0.2 to 5
- gas_at_particle: float32 [3, 2097152], P(None, ('grp', 'dom')), may hold values from -6 to 6
- pair_first: int32 [65536], P(('grp', 'dom')), may hold values from 0 to 31
- pair_second: int32 [65536], P(('grp', 'dom')), may hold values from 0 to 35
- ghost_list: int32 [2, 1024], P(None, ('grp', 'dom')), may hold values from 0 to 31
- block_owner: int32 [16384, 1], P(('grp', 'dom')), may hold values from 0 to 127; in each aligned block of 32 rows (0 to 31, 32 to 63, ...) at most 2 rows name the same one
- cell_map: int32 [2097152], P(('grp', 'dom')), may hold values from 0 to 511
- gas_velocity: float32 [3, 262144], P(None, ('grp', 'dom')), may hold values from -6 to 6
Outputs:
- positions_out: float32 [3, 2097152], P(None, ('grp', 'dom'))
- velocities_out: float32 [3, 2097152], P(None, ('grp', 'dom'))
- gas_out: float32 [3, 262144], P(None, ('grp', 'dom'))
- void_out: float32 [262144], P(('grp', 'dom'))
- particle_gas: float32 [3, 2097152], P(None, ('grp', 'dom'))
Inputs may be any that keep to these rules, and one draw needn't show every extreme that they name: `block_owner`: in the 32 blocks of one device no owner is named by more than 2 blocks, a bound that some block reaches. `pair_second`: values 32 to 33 name ghosts from the previous device, the next 2 those from the next device.
All inputs are finite; a program needn't handle non-finite values.
Results may differ from a plain program's by a relative error of at most 0.0003.
Values sent between devices are 32-bit elements; how exact they have to be, the bound alone decides.
No kernel may reach another device: no remote copies, remote signals or barrier semaphores. Data moves between devices by JAX's collectives and lax.ppermute only.
A program may use at most 128 MiB of HBM per device.

v0:
```python
import jax
import jax.numpy as jnp
from jax import lax
from jax.sharding import PartitionSpec as P

BP = 128
K = 5
SUBSTEPS = 4
SWEEPS = 4


SLAB = 4.0
SOFT = 0.01
STIFF = 20.0
NORMAL_DAMP = 2.0
TANGENT_DAMP = 1.0
STEP = 0.01
GRAVITY_Z = -1.0
RADIUS_FACTOR = 0.62
CELL_VOLUME = 16.0
RHO_STEP = 2.0
VISCOSITY = 1.0


def from_behind(value, axis, steps):
    count = lax.axis_size(axis)
    pairs = [(source, (source + steps) % count) for source in range(count)]
    return lax.ppermute(value, axis, pairs)


def padded_2(block, sides, width):
    for axis, dim in sides:
        count = lax.axis_size(axis)
        forward = [(i, i + 1) for i in range(count - 1)]
        forward.append((count - 1, 0))
        backward = [(target, source) for source, target in forward]
        low = lax.ppermute(
            lax.slice_in_dim(block, block.shape[dim] - width, None, axis=dim), axis, forward
        )
        high = lax.ppermute(lax.slice_in_dim(block, 0, width, axis=dim), axis, backward)
        block = jnp.concatenate([low, block, high], axis=dim)
    return block


def pair_force(xi, vi, ri, xj, vj, rj):
    delta_vec = xi[:, :, :, None] - xj[:, :, None, :]
    dist = jnp.sqrt(jnp.sum(delta_vec * delta_vec, axis=0) + SOFT)
    normal = delta_vec / dist[None]
    intersection = jnp.maximum(ri[:, :, None] + rj[:, None, :] - dist, 0.0)
    root = jnp.sqrt(intersection)
    relative = vi[:, :, :, None] - vj[:, :, None, :]
    speed_n = jnp.sum(relative * normal, axis=0)
    push = STIFF * intersection * root - NORMAL_DAMP * root * speed_n
    force = push[None] * normal - TANGENT_DAMP * root[None] * (relative - speed_n[None] * normal)
    return jnp.sum(force, axis=3)


def contact_forces(extended, first, second, nblocks):
    width = extended.shape[2]
    xi = extended[0:3][:, first]
    vi = extended[3:6][:, first]
    ri = extended[6][first]
    xj = extended[0:3][:, second]
    vj = extended[3:6][:, second]
    rj = extended[6][second]
    groups = first.shape[0] // 8

    def contact_one_group(k):
        start = k * 8
        return pair_force(
            lax.dynamic_slice_in_dim(xi, start, 8, 1),
            lax.dynamic_slice_in_dim(vi, start, 8, 1),
            lax.dynamic_slice_in_dim(ri, start, 8, 0),
            lax.dynamic_slice_in_dim(xj, start, 8, 1),
            lax.dynamic_slice_in_dim(vj, start, 8, 1),
            lax.dynamic_slice_in_dim(rj, start, 8, 0),
        )

    per_pair = lax.map(contact_one_group, jnp.arange(groups, dtype=jnp.int32))
    per_pair = jnp.moveaxis(per_pair, 0, 1).reshape(3, groups * 8, width)
    onehot = (first[None, :] == jnp.arange(nblocks, dtype=jnp.int32)[:, None]).astype(jnp.float32)
    return jnp.einsum("bp,cpq->cbq", onehot, per_pair, precision=lax.Precision.HIGHEST)


def advance(pos, vel, force, gas_seen, beta, mass):
    gravity = jnp.array([0.0, 0.0, GRAVITY_Z], dtype=jnp.float32)[:, None, None]
    beta3 = jnp.expand_dims(beta, -3)
    mass3 = jnp.expand_dims(mass, -3)
    accel = (force + beta3 * (gas_seen - vel)) / mass3 + gravity
    vel = vel + STEP * accel
    pos = pos + STEP * vel
    return (pos, vel)


def deposit_cells(amounts, cells, ncells):
    count = cells.shape[0]

    def deposit_one_group(k):
        part = lax.dynamic_slice_in_dim(amounts, k * 8, 8, 0)
        where = lax.dynamic_slice_in_dim(cells, k * 8, 8, 0)
        onehot = (where[:, :, None] == jnp.arange(ncells, dtype=jnp.int32)[None, None, :]).astype(
            jnp.float32
        )
        return jnp.einsum("bkp,bpc->bkc", part, onehot, precision=lax.Precision.HIGHEST)

    result = lax.map(deposit_one_group, jnp.arange(count // 8, dtype=jnp.int32))
    return result.reshape(count, amounts.shape[1], ncells)


def body(
    positions,
    velocities,
    particle_volume,
    drag_coef,
    gas_at_particle,
    pair_first,
    pair_second,
    ghost_list,
    block_owner,
    cell_map,
    gas_velocity,
):
    width = BP
    nblocks = positions.shape[1] // width
    ncells = gas_velocity.shape[1]
    ndom = lax.axis_size("dom")
    pos = positions.reshape(3, nblocks, width)
    vel = velocities.reshape(3, nblocks, width)
    gas_seen = gas_at_particle.reshape(3, nblocks, width)
    mass = particle_volume.reshape(nblocks, width)
    beta = drag_coef.reshape(nblocks, width)
    radius = RADIUS_FACTOR * mass ** (1.0 / 3.0)
    shift_vec = jnp.array([SLAB, 0.0, 0.0, 0.0, 0.0, 0.0, 0.0], dtype=jnp.float32)[:, None, None]
    for step in range(SUBSTEPS):
        payload = jnp.concatenate([pos, vel, radius[None]], axis=0)
        below = from_behind(payload[:, ghost_list[0]], ("grp", "dom"), 1) - shift_vec
        above = from_behind(payload[:, ghost_list[1]], ("grp", "dom"), -1) + shift_vec
        extended = jnp.concatenate([payload, below, above], axis=1)
        force = contact_forces(extended, pair_first, pair_second, nblocks)
        pos, vel = advance(pos, vel, force, gas_seen, beta, mass)
    owner = block_owner[:, 0]
    cells = cell_map.reshape(nblocks, width)
    amounts = jnp.concatenate([mass[None], beta[None], beta[None] * vel], axis=0).transpose(1, 0, 2)
    owner_range = jnp.arange(ndom, dtype=jnp.int32)
    per_block = deposit_cells(amounts, cells, ncells)
    owner_hot = (owner[:, None] == owner_range[None, :]).astype(jnp.float32)
    buffer = jnp.einsum("bo,bkc->koc", owner_hot, per_block, precision=lax.Precision.HIGHEST)
    mine = lax.psum_scatter(
        buffer.reshape(K, ndom * ncells), "dom", scatter_dimension=1, tiled=True
    )
    void_out = CELL_VOLUME / (CELL_VOLUME + mine[0])
    inertia = RHO_STEP * void_out
    drag_sum = mine[1] / CELL_VOLUME
    drag_mom = mine[2:5] / CELL_VOLUME
    diag = inertia + drag_sum + 2.0 * VISCOSITY
    known = inertia[None] * gas_velocity + drag_mom
    gas = gas_velocity
    for sweep in range(SWEEPS):
        padded = padded_2(gas, ((("grp", "dom"), 1),), 1)
        gas = (known + VISCOSITY * (padded[:, :-2] + padded[:, 2:])) / diag[None]
    table = lax.all_gather(gas, "dom", axis=1, tiled=True)
    index = (owner[:, None] * ncells + cells).reshape(-1)
    particle_gas = table[:, index]
    return (pos.reshape(3, -1), vel.reshape(3, -1), gas, void_out, particle_gas)


def solution(mesh):
    return jax.shard_map(
        body,
        mesh=mesh,
        in_specs=(
            P(None, ("grp", "dom")),
            P(None, ("grp", "dom")),
            P(("grp", "dom")),
            P(("grp", "dom")),
            P(None, ("grp", "dom")),
            P(("grp", "dom")),
            P(("grp", "dom")),
            P(None, ("grp", "dom")),
            P(("grp", "dom"), None),
            P(("grp", "dom")),
            P(None, ("grp", "dom")),
        ),
        out_specs=(
            P(None, ("grp", "dom")),
            P(None, ("grp", "dom")),
            P(None, ("grp", "dom")),
            P(("grp", "dom")),
            P(None, ("grp", "dom")),
        ),
        check_vma=False,
    )
```

profile of v0, /device:TPU:7, one launch (start us, length us, event | category | flops | bytes accessed | tf_op | source)
XLA Modules:
  0.0 749.2 jit_solution(7288193689247809356)
XLA Ops:
  10.3 4.6 collective-permute-start
  15.4 1.9 collective-permute-start.1
  25.7 79.0 %while.50 = (s32[]{:T(128)}, f32[16,3,8,128]{3,2,0,1:T(8,128)S(1)}, s32[16]{0:T(128)S(1)}, f32[128,128]{1,0:T(8,128)S(1)}, f32[128,128]{1,0:T(8,128)S(1)}, /*ind...) while((s32[]{:T(128)}, f32[16,3,8,128]{3,2,0,1:T(8,128)S(1)}, ...), condition=%wide.region_4.5_spmd, body=%wide.region_0.4_spmd.sunk | while | flops 7730182 | bytes 7098567 | solution.py:79
  48.9 1.5 fusion.123
  53.8 1.5 fusion.123
  58.8 1.5 fusion.123
  93.3 1.5 fusion.123
  98.3 1.5 fusion.123
  105.7 2.7 collective-permute-start.2
  108.9 9.9 %collective-permute-start.3 = (f32[7,2,128]{2,1,0:T(2,128)S(1)}, f32[7,2,128]{2,1,0:T(2,128)S(1)}, u32[]{:S(2)}, u32[]{:S(2)}) collective-permute-start(f32[7,2,128]{2,1,0:T(2,128)S(1)} %bitcast.305), channel_id=1, source_target_pairs={{0,511},{1,0},{2,1},{3,2},{4,3},{5,4},{6,5},{7,6},{8,7},{9,8},{10,... | collective-permute-start | bytes 21512 | tf_op jit(solution)/shard_map/ppermute | solution.py:28
  124.2 79.1 %while.51 = (s32[]{:T(128)}, f32[16,3,8,128]{3,2,0,1:T(8,128)S(1)}, s32[16]{0:T(128)S(1)}, f32[128,128]{1,0:T(8,128)S(1)}, f32[128,128]{1,0:T(8,128)S(1)}, /*ind...) while((s32[]{:T(128)}, f32[16,3,8,128]{3,2,0,1:T(8,128)S(1)}, ...), condition=%wide.region_9.10_spmd, body=%wide.region_5.9_spmd.sunk | while | flops 7730182 | bytes 7098567 | solution.py:79
  127.6 1.5 fusion.126
  132.6 1.5 fusion.126
  137.5 1.5 fusion.126
  142.5 1.5 fusion.126
  147.4 1.5 fusion.126
  152.4 1.5 fusion.126
  157.3 1.5 fusion.126
  162.3 1.5 fusion.126
  167.2 1.5 fusion.126
  172.2 1.5 fusion.126
  177.1 1.5 fusion.126
  182.1 1.5 fusion.126
  187.0 1.5 fusion.126
  192.0 1.5 fusion.126
  196.9 1.5 fusion.126
  201.9 1.5 fusion.126
  204.3 1.9 collective-permute-start.4
  206.8 8.6 %collective-permute-start.5 = (f32[7,2,128]{2,1,0:T(2,128)S(1)}, f32[7,2,128]{2,1,0:T(2,128)S(1)}, u32[]{:S(2)}, u32[]{:S(2)}) collective-permute-start(f32[7,2,128]{2,1,0:T(2,128)S(1)} %bitcast.306), channel_id=1, source_target_pairs={{0,511},{1,0},{2,1},{3,2},{4,3},{5,4},{6,5},{7,6},{8,7},{9,8},{10,... | collective-permute-start | bytes 21512 | tf_op jit(solution)/shard_map/ppermute | solution.py:28
  220.6 79.0 %while.52 = (s32[]{:T(128)}, f32[16,3,8,128]{3,2,0,1:T(8,128)S(1)}, s32[16]{0:T(128)S(1)}, f32[128,128]{1,0:T(8,128)S(1)}, f32[128,128]{1,0:T(8,128)S(1)}, /*ind...) while((s32[]{:T(128)}, f32[16,3,8,128]{3,2,0,1:T(8,128)S(1)}, ...), condition=%wide.region_14.15_spmd, body=%wide.region_10.14_spmd.sunk | while | flops 7730182 | bytes 7098567 | solution.py:79
  300.5 1.9 collective-permute-start.6
  303.0 8.4 %collective-permute-start.7 = (f32[7,2,128]{2,1,0:T(2,128)S(1)}, f32[7,2,128]{2,1,0:T(2,128)S(1)}, u32[]{:S(2)}, u32[]{:S(2)}) collective-permute-start(f32[7,2,128]{2,1,0:T(2,128)S(1)} %bitcast.304), channel_id=1, source_target_pairs={{0,511},{1,0},{2,1},{3,2},{4,3},{5,4},{6,5},{7,6},{8,7},{9,8},{10,... | collective-permute-start | bytes 21512 | tf_op jit(solution)/shard_map/ppermute | solution.py:28
  316.9 79.1 %while.53 = (s32[]{:T(128)}, f32[16,3,8,128]{3,2,0,1:T(8,128)S(1)}, s32[16]{0:T(128)S(1)}, f32[128,128]{1,0:T(8,128)S(1)}, f32[128,128]{1,0:T(8,128)S(1)}, /*ind...) while((s32[]{:T(128)}, f32[16,3,8,128]{3,2,0,1:T(8,128)S(1)}, ...), condition=%wide.region_19.20_spmd, body=%wide.region_15.19_spmd.sunk | while | flops 7730182 | bytes 7098567 | solution.py:79
  396.2 8.4 %while.54 = (s32[]{:T(128)}, f32[4,8,5,512]{3,2,1,0:T(8,128)S(1)}, s32[4]{0:T(128)S(1)}, f32[32,5,128]{2,0,1:T(8,128)S(1)}, s32[32,128]{1,0:T(8,128)S(1)}, /*index=5*/s32[]{:T(128)}, s32[1]{0:T(128)}, s32[]{:T(128)}, s32[]{:T(128)}) while((s32[]{:T(128)}, f32[4,8,5,512]{3,2,1,0:T(8,128)S(1)}, s32[4]{0:T(128)S(1)}, ...), condition=%wide.region_21.22_spmd, body=%wide.region_20.21_spmd.sunk | while | flops 31981572 | bytes 204963 | solution.py:106
  406.2 2.2 copy.346
  409.2 1.9 collective-permute-start.8
  411.1 8.4 %collective-permute-start.9 = (f32[3,1]{1,0:T(4,128)S(1)}, f32[3,1]{1,0:T(4,128)S(1)}, u32[]{:S(2)}, u32[]{:S(2)}) collective-permute-start(f32[3,1]{1,0:T(4,128)S(1)} %get-tuple-element.554), channel_id=1, source_target_pairs={{1,0},{2,1},{3,2},{4,3},{5,4},{6,5},{7,6},{8,7},{9,8},{10,9},{11,1... | collective-permute-start | bytes 44 | tf_op jit(solution)/shard_map/ppermute | solution.py:40
  420.9 188.4 %reduce-scatter.2.cloned.1.call-done = f32[5,512]{1,0:T(8,128)} async-done(((f32[5,65536]{1,0:T(8,128)}), f32[5,512]{1,0:T(8,128)}) %reduce-scatter.2.cloned.1.call-update) | async-done | bytes 10256 | tf_op jit(solution)/shard_map/reduce_scatter | solution.py:148
  611.1 7.5 %collective-permute-start.10 = (f32[3,1]{1,0:T(4,128)S(1)}, f32[3,1]{1,0:T(4,128)S(1)}, u32[]{:S(2)}, u32[]{:S(2)}) collective-permute-start(f32[3,1]{1,0:T(4,128)S(1)} %get-tuple-element.551), channel_id=1, source_target_pairs={{0,1},{1,2},{2,3},{3,4},{4,5},{5,6},{6,7},{7,8},{8,9},{9,10},{10,1... | collective-permute-start | bytes 44 | tf_op jit(solution)/shard_map/ppermute | solution.py:37
  618.6 1.9 collective-permute-start.11
  620.5 3.3 collective-permute-done.11
  623.9 1.9 collective-permute-start.12
  625.9 5.7 collective-permute-start.13
  632.5 1.9 collective-permute-start.14
  634.4 8.3 %collective-permute-start.15 = (f32[3,1]{1,0:T(4,128)S(1)}, f32[3,1]{1,0:T(4,128)S(1)}, u32[]{:S(2)}, u32[]{:S(2)}) collective-permute-start(f32[3,1]{1,0:T(4,128)S(1)} %get-tuple-element.548), channel_id=1, source_target_pairs={{1,0},{2,1},{3,2},{4,3},{5,4},{6,5},{7,6},{8,7},{9,8},{10,9},{11,1... | collective-permute-start | bytes 44 | tf_op jit(solution)/shard_map/ppermute | solution.py:40
  643.7 60.1 %all_gather.3 = f32[3,65536]{1,0:T(4,128)S(1)} all-gather(f32[3,512]{1,0:T(4,128)S(1)} %fusion.76), channel_id=1, replica_groups=mesh['grp'=4,'dom'=128] {'dom'}, dimensions={1}, use_global_device_ids=true | all-gather | bytes 792576 | tf_op jit(solution)/shard_map/all_gather | solution.py:161
  703.8 15.9 %copy.330 = f32[3,65536]{0,1:T(8,128)} copy(f32[3,65536]{1,0:T(4,128)S(1)} %all_gather.3) | data formatting | bytes 1572864 | tf_op jit(solution)/shard_map/all_gather | solution.py:161
  719.7 21.3 %gather_fusion.32 = f32[4096,3]{1,0:T(8,128)S(1)} fusion(f32[3,65536]{0,1:T(8,128)} %copy.330, s32[4096]{0:T(1024)S(1)} %fusion.66), kind=kCustom, calls=%fused_computation.32 | custom fusion | bytes 114688 | tf_op jit(solution)/shard_map/gather | solution.py:163
  (809 shorter events, 284.2 us)
Async XLA Ops:
  7.2 602.2 %reduce-scatter.2.cloned.1.call-start = ((), (), s32[]{:S(2)}) async-start(), calls=%async_computation.1 | async-start | bytes 2113536 | tf_op jit(solution)/shard_map/reduce_scatter | solution.py:148
  10.3 8.4 %collective-permute-start = (f32[7,2,128]{2,1,0:T(2,128)S(1)}, f32[7,2,128]{2,1,0:T(2,128)S(1)}, u32[]{:S(2)}, u32[]{:S(2)}) collective-permute-start(f32[7,2,128]{2,1,0:T(2,128)S(1)} %bitcast.299), channel_id=1, source_target_pairs={{0,1},{1,2},{2,3},{3,4},{4,5},{5,6},{6,7},{7,8},{8,9},{9,10},{10,1... | collective-permute-start | bytes 21512 | tf_op jit(solution)/shard_map/ppermute | solution.py:28
  15.4 5.0 collective-permute-start.1
  25.6 79.1 %copy-start = (f32[3,4096]{1,0:T(4,128)S(1)}, f32[3,4096]{1,0:T(4,128)}, u32[]{:S(2)}) copy-start(f32[3,4096]{1,0:T(4,128)} %param.30) | copy-start | bytes 147460
  25.7 79.1 %copy-start.1 = (f32[4096]{0:T(1024)S(1)}, f32[4096]{0:T(1024)}, u32[]{:S(2)}) copy-start(f32[4096]{0:T(1024)} %param.28) | copy-start | bytes 49156
  25.7 79.1 %copy-start.2 = (f32[4096]{0:T(1024)S(1)}, f32[4096]{0:T(1024)}, u32[]{:S(2)}) copy-start(f32[4096]{0:T(1024)} %param.29) | copy-start | bytes 49156
  25.7 79.1 %copy-start.9 = (s32[128]{0:T(128)S(1)}, s32[128]{0:T(128)}, u32[]{:S(2)}) copy-start(s32[128]{0:T(128)} %param.31) | copy-start | bytes 1540
  25.7 79.1 %copy-start.10 = (f32[3]{0:T(128)S(1)}, f32[3]{0:T(128)}, u32[]{:S(2)}) copy-start(f32[3]{0:T(128)} %constant.133.clone) | copy-start | bytes 40
  25.7 93.1 %copy-start.8 = (f32[7]{0:T(128)S(1)}, f32[7]{0:T(128)}, u32[]{:S(2)}) copy-start(f32[7]{0:T(128)} %constant.138) | copy-start | bytes 88
  25.7 93.9 %copy-start.7 = (f32[7]{0:T(128)S(1)}, f32[7]{0:T(128)}, u32[]{:S(2)}) copy-start(f32[7]{0:T(128)} %constant.132.clone) | copy-start | bytes 88
  105.7 13.1 %collective-permute-start.2 = (f32[7,2,128]{2,1,0:T(2,128)S(1)}, f32[7,2,128]{2,1,0:T(2,128)S(1)}, u32[]{:S(2)}, u32[]{:S(2)}) collective-permute-start(f32[7,2,128]{2,1,0:T(2,128)S(1)} %bitcast.302), channel_id=1, source_target_pairs={{0,1},{1,2},{2,3},{3,4},{4,5},{5,6},{6,7},{7,8},{8,9},{9,10},{10,1... | collective-permute-start | bytes 21512 | tf_op jit(solution)/shard_map/ppermute | solution.py:28
  108.9 10.7 %collective-permute-start.3 = (f32[7,2,128]{2,1,0:T(2,128)S(1)}, f32[7,2,128]{2,1,0:T(2,128)S(1)}, u32[]{:S(2)}, u32[]{:S(2)}) collective-permute-start(f32[7,2,128]{2,1,0:T(2,128)S(1)} %bitcast.305), channel_id=1, source_target_pairs={{0,511},{1,0},{2,1},{3,2},{4,3},{5,4},{6,5},{7,6},{8,7},{9,8},{10,... | collective-permute-start | bytes 21512 | tf_op jit(solution)/shard_map/ppermute | solution.py:28
  204.3 11.1 %collective-permute-start.4 = (f32[7,2,128]{2,1,0:T(2,128)S(1)}, f32[7,2,128]{2,1,0:T(2,128)S(1)}, u32[]{:S(2)}, u32[]{:S(2)}) collective-permute-start(f32[7,2,128]{2,1,0:T(2,128)S(1)} %bitcast.303), channel_id=1, source_target_pairs={{0,1},{1,2},{2,3},{3,4},{4,5},{5,6},{6,7},{7,8},{8,9},{9,10},{10,1... | collective-permute-start | bytes 21512 | tf_op jit(solution)/shard_map/ppermute | solution.py:28
  206.8 9.2 %collective-permute-start.5 = (f32[7,2,128]{2,1,0:T(2,128)S(1)}, f32[7,2,128]{2,1,0:T(2,128)S(1)}, u32[]{:S(2)}, u32[]{:S(2)}) collective-permute-start(f32[7,2,128]{2,1,0:T(2,128)S(1)} %bitcast.306), channel_id=1, source_target_pairs={{0,511},{1,0},{2,1},{3,2},{4,3},{5,4},{6,5},{7,6},{8,7},{9,8},{10,... | collective-permute-start | bytes 21512 | tf_op jit(solution)/shard_map/ppermute | solution.py:28
  300.5 10.9 %collective-permute-start.6 = (f32[7,2,128]{2,1,0:T(2,128)S(1)}, f32[7,2,128]{2,1,0:T(2,128)S(1)}, u32[]{:S(2)}, u32[]{:S(2)}) collective-permute-start(f32[7,2,128]{2,1,0:T(2,128)S(1)} %bitcast.301), channel_id=1, source_target_pairs={{0,1},{1,2},{2,3},{3,4},{4,5},{5,6},{6,7},{7,8},{8,9},{9,10},{10,1... | collective-permute-start | bytes 21512 | tf_op jit(solution)/shard_map/ppermute | solution.py:28
  303.0 9.2 %collective-permute-start.7 = (f32[7,2,128]{2,1,0:T(2,128)S(1)}, f32[7,2,128]{2,1,0:T(2,128)S(1)}, u32[]{:S(2)}, u32[]{:S(2)}) collective-permute-start(f32[7,2,128]{2,1,0:T(2,128)S(1)} %bitcast.304), channel_id=1, source_target_pairs={{0,511},{1,0},{2,1},{3,2},{4,3},{5,4},{6,5},{7,6},{8,7},{9,8},{10,... | collective-permute-start | bytes 21512 | tf_op jit(solution)/shard_map/ppermute | solution.py:28
  316.9 79.4 %copy-start.3 = (s32[4096]{0:T(1024)S(1)}, s32[4096]{0:T(1024)}, u32[]{:S(2)}) copy-start(s32[4096]{0:T(1024)} %param.35) | copy-start | bytes 49156
  396.2 8.4 %copy-start.11 = (s32[32,1]{0,1:T(1,128)S(1)}, s32[32,1]{0,1:T(1,128)}, u32[]{:S(2)}) copy-start(s32[32,1]{0,1:T(1,128)} %param.34) | copy-start | bytes 388
  408.4 0.7 copy-start.5
  409.2 201.0 %collective-permute-start.8 = (f32[3,1]{1,0:T(4,128)S(1)}, f32[3,1]{1,0:T(4,128)S(1)}, u32[]{:S(2)}, u32[]{:S(2)}) collective-permute-start(f32[3,1]{1,0:T(4,128)S(1)} %get-tuple-element.553), channel_id=1, source_target_pairs={{0,1},{1,2},{2,3},{3,4},{4,5},{5,6},{6,7},{7,8},{8,9},{9,10},{10,1... | collective-permute-start | bytes 44 | tf_op jit(solution)/shard_map/ppermute | solution.py:37
  411.1 199.1 %collective-permute-start.9 = (f32[3,1]{1,0:T(4,128)S(1)}, f32[3,1]{1,0:T(4,128)S(1)}, u32[]{:S(2)}, u32[]{:S(2)}) collective-permute-start(f32[3,1]{1,0:T(4,128)S(1)} %get-tuple-element.554), channel_id=1, source_target_pairs={{1,0},{2,1},{3,2},{4,3},{5,4},{6,5},{7,6},{8,7},{9,8},{10,9},{11,1... | collective-permute-start | bytes 44 | tf_op jit(solution)/shard_map/ppermute | solution.py:40
  610.1 109.6 %copy-start.6 = (f32[1,512]{1,0:T(1,128)}, f32[1,512]{1,0:T(1,128)S(1)}, u32[]{:S(2)}) copy-start(f32[1,512]{1,0:T(1,128)S(1)} %get-tuple-element.504) | copy-start | bytes 6148
  611.1 9.4 %collective-permute-start.10 = (f32[3,1]{1,0:T(4,128)S(1)}, f32[3,1]{1,0:T(4,128)S(1)}, u32[]{:S(2)}, u32[]{:S(2)}) collective-permute-start(f32[3,1]{1,0:T(4,128)S(1)} %get-tuple-element.551), channel_id=1, source_target_pairs={{0,1},{1,2},{2,3},{3,4},{4,5},{5,6},{6,7},{7,8},{8,9},{9,10},{10,1... | collective-permute-start | bytes 44 | tf_op jit(solution)/shard_map/ppermute | solution.py:37
  618.6 5.2 collective-permute-start.11
  623.9 7.6 %collective-permute-start.12 = (f32[3,1]{1,0:T(4,128)S(1)}, f32[3,1]{1,0:T(4,128)S(1)}, u32[]{:S(2)}, u32[]{:S(2)}) collective-permute-start(f32[3,1]{1,0:T(4,128)S(1)} %get-tuple-element.549), channel_id=1, source_target_pairs={{0,1},{1,2},{2,3},{3,4},{4,5},{5,6},{6,7},{7,8},{8,9},{9,10},{10,1... | collective-permute-start | bytes 44 | tf_op jit(solution)/shard_map/ppermute | solution.py:37
  625.9 6.5 collective-permute-start.13
  632.5 10.3 %collective-permute-start.14 = (f32[3,1]{1,0:T(4,128)S(1)}, f32[3,1]{1,0:T(4,128)S(1)}, u32[]{:S(2)}, u32[]{:S(2)}) collective-permute-start(f32[3,1]{1,0:T(4,128)S(1)} %get-tuple-element.547), channel_id=1, source_target_pairs={{0,1},{1,2},{2,3},{3,4},{4,5},{5,6},{6,7},{7,8},{8,9},{9,10},{10,1... | collective-permute-start | bytes 44 | tf_op jit(solution)/shard_map/ppermute | solution.py:37
  634.4 9.2 %collective-permute-start.15 = (f32[3,1]{1,0:T(4,128)S(1)}, f32[3,1]{1,0:T(4,128)S(1)}, u32[]{:S(2)}, u32[]{:S(2)}) collective-permute-start(f32[3,1]{1,0:T(4,128)S(1)} %get-tuple-element.548), channel_id=1, source_target_pairs={{1,0},{2,1},{3,2},{4,3},{5,4},{6,5},{7,6},{8,7},{9,8},{10,9},{11,1... | collective-permute-start | bytes 44 | tf_op jit(solution)/shard_map/ppermute | solution.py:40
  643.7 76.1 %copy-start.4 = (f32[3,512]{1,0:T(4,128)}, f32[3,512]{1,0:T(4,128)S(1)}, u32[]{:S(2)}) copy-start(f32[3,512]{1,0:T(4,128)S(1)} %fusion.76) | copy-start | bytes 18436
Sparse Core Ops, SparseCore 0:
  408.6 200.7 reduce-scatter.1
where the time goes:
time: 751 us; the launch traced here: 749 us
  other arithmetic  235 us (31%)
  waiting for transfers between devices  196 us (26%)
  local copies, waits for them, and re-layouts  110 us (15%)
  starting transfers between devices  77.5 us (10%)
  blocking collectives  60.1 us (8%)
  loops' own time  49.9 us (7%)
  between operations  15.1 us (2%)
    reduce_scatter x1, waiting for transfers between devices, body(): lax.psum_scatter(buffer.reshape(K, ndom * ncells), 'dom', scatter_dimensi...  188 us
    reduce_sum x64, other arithmetic, pair_force(): return jnp.sum(force, axis=3)  95.4 us
    reduce_sum x64, other arithmetic, pair_force(): speed_n = jnp.sum(relative * normal, axis=0)  65.3 us
    all_gather x1, blocking collectives, body(): table = lax.all_gather(gas, 'dom', axis=1, tiled=True)  60.1 us
    another operation x4, loops' own time, contact_forces(): per_pair = lax.map(contact_one_group, jnp.arange(groups, dtype=jnp.int32))  47.2 us
    ppermute x8, starting transfers between devices, from_behind(): return lax.ppermute(value, axis, pairs)  39.8 us
    dynamic_slice x64, local copies, waits for them, and re-layouts, contact_forces(): per_pair = lax.map(contact_one_group, jnp.arange(groups, dtype=jnp.int32))  37.5 us
    reduce_sum x64, other arithmetic, pair_force(): dist = jnp.sqrt(jnp.sum(delta_vec * delta_vec, axis=0) + SOFT)  30.2 us
  transfers between devices with their start and end apart: 17, of which 8 were waited for; matrix products, arithmetic and copies ran while one was open for 1% of the time, Pallas kernels for 0%

commit v1 on v0

v1 whole, which is shorter than its diff:
```python
import functools

import jax
import jax.numpy as jnp
from jax import lax
from jax.experimental import pallas as pl
from jax.experimental.pallas import tpu as pltpu
from jax.sharding import PartitionSpec as P

NB = 32
BP = 128
NG = 2
NEXT = NB + 2 * NG
NPAIR = 128
GROUP = 8
SUBSTEPS = 4
SWEEPS = 4
K = 5
CHUNKS = 4
DEPROWS = 24
GASROWS = 12

SLAB = 4.0
SOFT = 0.01
STIFF = 20.0
STEP = 0.01
GRAVITY_Z = -1.0
RADIUS_FACTOR = 0.62
CELL_VOLUME = 16.0
RHO_STEP = 2.0
VISCOSITY = 1.0
TINY = 1e-36

F32 = jnp.float32
BF16 = jnp.bfloat16
VMEM = pl.BlockSpec(memory_space=pltpu.VMEM)
SMEM = pl.BlockSpec(memory_space=pltpu.SMEM)
PARAMS = pltpu.CompilerParams(vmem_limit_bytes=40 * 1024 * 1024)


def cost(flops, nbytes, transcendentals=0):
    return pl.CostEstimate(flops=flops, bytes_accessed=nbytes, transcendentals=transcendentals)


def parts3(value):
    high = value.astype(BF16).astype(F32)
    rest = value - high
    mid = rest.astype(BF16).astype(F32)
    low = (rest - mid).astype(BF16).astype(F32)
    return high, mid, low


def swap3(tile):
    return jnp.concatenate([tile[:, 3:6], tile[:, 0:3], tile[:, 6:8]], axis=1)


def fill_sends(par_ref, ghost_ref, state_ref, near_ref, far_ref):
    par = par_ref[0]
    for s in range(NG):
        near_ref[s] = state_ref[ghost_ref[par, s]]
        far_ref[s] = state_ref[ghost_ref[1 - par, s]]


def prepare_kernel(par_ref, ghost_ref, pos_ref, vel_ref, gas_ref, mass_ref, beta_ref, state_ref, aux_ref, near_ref, far_ref):
    radius = RADIUS_FACTOR * jnp.exp(jnp.log(mass_ref[...]) * (1.0 / 3.0))
    zero3 = jnp.zeros((3, BP), F32)
    for b in range(NB):
        lanes = slice(b * BP, (b + 1) * BP)
        rows = slice(b, b + 1)
        state_ref[b] = jnp.concatenate(
            [pos_ref[:, lanes], vel_ref[:, lanes], radius[rows], jnp.zeros((1, BP), F32)], axis=0
        )
        aux_ref[b] = jnp.concatenate([zero3, gas_ref[:, lanes], beta_ref[rows], mass_ref[rows]], axis=0)
    fill_sends(par_ref, ghost_ref, state_ref, near_ref, far_ref)


def prepare(par, ghost_list, pos, vel, gas_seen, mass, beta):
    tile = jax.ShapeDtypeStruct((NB, 8, BP), F32)
    send = jax.ShapeDtypeStruct((NG, 8, BP), F32)
    return pl.pallas_call(
        prepare_kernel,
        in_specs=[SMEM] * 2 + [VMEM] * 5,
        out_shape=(tile, tile, send, send),
        out_specs=(VMEM,) * 4,
        compiler_params=PARAMS,
        cost_estimate=cost(100000, 600000),
        name="prepare",
    )(par, ghost_list, pos, vel, gas_seen, mass, beta)


def pair_body(a, b, ext_ref, jt_ref, g_ref, a_ref, rb_ref):
    both = jnp.dot(jt_ref[b], g_ref[a], preferred_element_type=F32)
    dist2 = both[:, :BP]
    slide = both[:, BP:]
    inv = lax.rsqrt(dist2)
    overlap = (rb_ref[b] + ext_ref[a, 6:7, :]) - dist2 * inv
    delta = jnp.maximum(overlap, 0.0)
    root = delta * lax.rsqrt(jnp.maximum(overlap, TINY))
    push = (root * inv) * (delta - slide * inv)
    push_high = push.astype(BF16)
    push_low = (push - push_high.astype(F32)).astype(BF16)
    root_high = root.astype(BF16)
    root_low = (root - root_high.astype(F32)).astype(BF16)
    weights = jnp.concatenate([push_high, push_low, root_high, root_low], axis=0)
    left_x = a_ref[b, :, :BP]
    left_v = a_ref[b, :, BP:]
    left = jnp.concatenate([left_x, left_x, left_v, left_v], axis=1)
    sums = jnp.dot(left, weights, preferred_element_type=F32)
    return sums[0:8] + sums[8:16] + sums[16:24]


def step_kernel(last, *refs):
    (par_ref, ghost_ref, first_ref, second_ref, owner_ref, cell_ref, state_ref, near_in, far_in, aux_ref), refs = refs[:10], refs[10:]
    if last:
        (pos_out, vel_out, dep_ref), scratch = refs[:3], refs[3:]
    else:
        (new_ref, near_out, far_out), scratch = refs[:3], refs[3:]
    ext_ref, jt_ref, g_ref, a_ref, rb_ref, acc_ref = scratch
    par = par_ref[0]
    row = lax.broadcasted_iota(jnp.int32, (8, BP), 0)[None]

    ext_ref[0:NB] = state_ref[...]
    sign = 1.0 - 2.0 * par.astype(F32)
    shift = jnp.where(row[0] == 0, SLAB * sign, 0.0)
    for s in range(NG):
        ext_ref[NB + NG * (1 - par) + s] = near_in[s] + shift
        ext_ref[NB + NG * par + s] = far_in[s] - shift
    for s in range(NEXT, ext_ref.shape[0]):
        ext_ref[s] = jnp.zeros((8, BP), F32)

    radius = jnp.transpose(ext_ref[:, 6, :])
    for b in range(NEXT):
        rb_ref[b] = jnp.broadcast_to(radius[:, b : b + 1], (BP, BP))

    def features(start, count):
        tile = ext_ref[pl.ds(start, count)]
        swapped = swap3(tile)
        norm = jnp.sum(jnp.where(row < 3, tile * tile, 0.0), axis=1, keepdims=True)
        cross = jnp.sum(jnp.where(row < 3, tile * swapped, 0.0), axis=1, keepdims=True) * (1.0 / STIFF)
        return tile, swapped, norm, cross

    ones = jnp.ones((8, BP), F32)
    zeros = jnp.zeros((8, BP), F32)

    def partner_side(k, carry):
        base = k * 4
        tile, swapped, norm, cross = features(base, 4)
        full = jnp.where(row < 6, tile, jnp.where(row == 6, norm, cross))
        high, mid, low = parts3(full)
        for s in range(4):
            h, m, l = high[s], mid[s], low[s]
            stack = jnp.concatenate([h, h, h, m, m, l, ones, zeros], axis=0)
            jt_ref[base + s] = jnp.transpose(stack).astype(BF16)
            r = row[0]
            by_x = jnp.concatenate(
                [
                    jnp.where(r < 3, h, jnp.where(r == 6, 1.0, 0.0)),
                    jnp.where(r < 3, m, 0.0),
                    jnp.where(r < 3, l, 0.0),
                    zeros,
                ],
                axis=0,
            )
            is_v = (r >= 3) & (r < 6)
            by_v = jnp.concatenate(
                [
                    jnp.where(is_v, h, jnp.where(r == 7, 1.0, 0.0)),
                    jnp.where(is_v, m, 0.0),
                    jnp.where(is_v, l, 0.0),
                    zeros,
                ],
                axis=0,
            )
            a_ref[base + s] = jnp.concatenate([by_x, by_v], axis=1).astype(BF16)
        return carry

    lax.fori_loop(0, NEXT // 4, partner_side, 0)

    def own_side(k, carry):
        base = k * 4
        tile, swapped, norm, cross = features(base, 4)
        xh, xm, xl = parts3(jnp.where(row < 3, -2.0 * tile, 0.0))
        xh = jnp.where(row == 6, 1.0, xh)
        vh, vm, vl = parts3(jnp.where(row < 6, swapped * (-1.0 / STIFF), 0.0))
        vh = jnp.where(row == 7, 1.0, vh)
        nh, nm, nl = parts3(norm + SOFT)
        ch, cm, cl = parts3(cross)
        own_n = jnp.where(row == 0, nh, jnp.where(row == 1, nm, jnp.where(row == 2, nl, 0.0)))
        own_c = jnp.where(row == 0, ch, jnp.where(row == 1, cm, jnp.where(row == 2, cl, 0.0)))
        for s in range(4):
            left = jnp.concatenate([xh[s], xm[s], xl[s], xh[s], xm[s], xh[s], own_n[s], zeros], axis=0)
            right = jnp.concatenate([vh[s], vm[s], vl[s], vh[s], vm[s], vh[s], own_c[s], zeros], axis=0)
            g_ref[base + s] = jnp.concatenate([left, right], axis=1).astype(BF16)
        return carry

    lax.fori_loop(0, NB // 4, own_side, 0)

    acc_ref[...] = jnp.zeros(acc_ref.shape, F32)

    def group(k, carry):
        start = k * GROUP
        firsts = [first_ref[start + s] for s in range(GROUP)]
        seconds = [second_ref[start + s] for s in range(GROUP)]
        sums = [pair_body(a, b, ext_ref, jt_ref, g_ref, a_ref, rb_ref) for a, b in zip(firsts, seconds)]
        for a, value in zip(firsts, sums):
            acc_ref[a] += value
        return carry

    lax.fori_loop(0, NPAIR // GROUP, group, 0)

    tile = state_ref[...]
    acc = acc_ref[...]
    aux = aux_ref[...]
    by_x = STIFF * (tile * acc[:, 6:7] - acc)
    by_v = acc - tile * acc[:, 7:8]
    force = swap3(by_x) + by_v
    beta = aux[:, 6:7]
    mass = aux[:, 7:8]
    gravity = jnp.where(row == 5, GRAVITY_Z, 0.0)
    velocity = tile + STEP * ((force + beta * (aux - tile)) / mass + gravity)
    place = tile + STEP * swap3(velocity)
    moved = jnp.where(row < 3, place, jnp.where(row < 6, velocity, tile))

    if not last:
        new_ref[...] = moved
        fill_sends(par_ref, ghost_ref, new_ref, near_out, far_out)
        return

    for b in range(NB):
        lanes = slice(b * BP, (b + 1) * BP)
        pos_out[:, lanes] = moved[b, 0:3]
        vel_out[:, lanes] = moved[b, 3:6]

    dep_ref[...] = jnp.zeros(dep_ref.shape, F32)
    drag = beta * moved
    quarter = lax.broadcasted_iota(jnp.int32, (DEPROWS, BP), 0) % CHUNKS
    place_of = lax.broadcasted_iota(jnp.int32, (BP, BP), 0)
    tail = jnp.zeros((DEPROWS - CHUNKS * K, BP), F32)
    for b in range(NB):
        cell = cell_ref[b : b + 1, :]
        chunk = cell // BP
        hot = jnp.where(place_of == cell % BP, 1.0, 0.0).astype(BF16)
        values = [mass[b], beta[b], drag[b, 3:4], drag[b, 4:5], drag[b, 5:6]]
        amounts = jnp.concatenate([jnp.broadcast_to(v, (CHUNKS, BP)) for v in values] + [tail], axis=0)
        amounts = jnp.where(quarter == chunk, amounts, 0.0)
        stacked = jnp.concatenate(list(parts3(amounts)) + [zeros], axis=0).astype(BF16)
        spread = lax.dot_general(stacked, hot, (((1,), (1,)), ((), ())), preferred_element_type=F32)
        owner = owner_ref[b]
        dep_ref[owner] += spread[0:DEPROWS] + spread[DEPROWS : 2 * DEPROWS] + spread[2 * DEPROWS : 3 * DEPROWS]


def contact_step(last, ndom, scalars, cells, state, near, far, aux):
    tile = jax.ShapeDtypeStruct((NB, 8, BP), F32)
    send = jax.ShapeDtypeStruct((NG, 8, BP), F32)
    if last:
        flat = jax.ShapeDtypeStruct((3, NB * BP), F32)
        outs = (flat, flat, jax.ShapeDtypeStruct((ndom, DEPROWS, BP), F32))
    else:
        outs = (tile, send, send)
    return pl.pallas_call(
        functools.partial(step_kernel, last),
        in_specs=[SMEM] * 5 + [VMEM] * 5,
        out_shape=outs,
        out_specs=(VMEM,) * 3,
        scratch_shapes=[
            pltpu.VMEM((40, 8, BP), F32),
            pltpu.VMEM((NEXT, BP, 64), BF16),
            pltpu.VMEM((NB, 64, 2 * BP), BF16),
            pltpu.VMEM((NEXT, 32, 2 * BP), BF16),
            pltpu.VMEM((NEXT, BP, BP), F32),
            pltpu.VMEM((NB, 8, BP), F32),
        ],
        compiler_params=PARAMS,
        cost_estimate=cost(1500000000, 2000000, 4000000),
        name="contact_last" if last else "contact",
    )(*scalars, cells, state, near, far, aux)


def known_kernel(dep_ref, gas_ref, void_ref, known_ref, low_ref, high_ref):
    dep = jnp.sum(dep_ref[...], axis=0)
    void = CELL_VOLUME / (CELL_VOLUME + dep[0:4])
    inertia = RHO_STEP * void
    void_ref[...] = void
    rows = [gas_ref[c : c + 1, s * BP : (s + 1) * BP] for c in range(3) for s in range(CHUNKS)]
    gas = [jnp.concatenate(rows[c * CHUNKS : (c + 1) * CHUNKS], axis=0) for c in range(3)]
    diag = inertia + dep[4:8] / CELL_VOLUME + 2.0 * VISCOSITY
    known = [inertia * gas[c] + dep[8 + 4 * c : 12 + 4 * c] / CELL_VOLUME for c in range(3)]
    for s in range(CHUNKS):
        one = slice(s, s + 1)
        tile = jnp.concatenate(
            [g[one] for g in gas] + [k[one] for k in known] + [diag[one], diag[one]], axis=0
        )
        known_ref[s] = tile
    low_ref[...] = known_ref[0]
    high_ref[...] = known_ref[CHUNKS - 1]


def sweeps_kernel(par_ref, near_ref, far_ref, known_ref, gas_out, table_ref):
    odd = par_ref[0] == 1
    below = jnp.where(odd, near_ref[...], far_ref[...])
    above = jnp.where(odd, far_ref[...], near_ref[...])
    full = jnp.concatenate([below] + [known_ref[s] for s in range(CHUNKS)] + [above], axis=1)
    width = full.shape[1]
    inverse = 1.0 / full[6:7]
    known = full[3:6]
    gas = full[0:3]
    pad = jnp.zeros((5, width), F32)
    gas8 = jnp.concatenate([gas, pad], axis=0)
    known8 = jnp.concatenate([known, pad], axis=0)
    for sweep in range(SWEEPS):
        sides = pltpu.roll(gas8, 1, 1) + pltpu.roll(gas8, width - 1, 1)
        gas8 = (known8 + VISCOSITY * sides) * inverse
    gas_out[...] = gas8[0:3, BP : BP + CHUNKS * BP]
    for c in range(3):
        for s in range(CHUNKS):
            table_ref[c * CHUNKS + s : c * CHUNKS + s + 1, :] = gas8[c : c + 1, (s + 1) * BP : (s + 2) * BP]


def pick_kernel(owner_ref, cell_ref, table_ref, out_ref):
    place_of = lax.broadcasted_iota(jnp.int32, (BP, BP), 0)
    quarter = lax.broadcasted_iota(jnp.int32, (CHUNKS, BP), 0)
    pad = jnp.zeros((4, BP), F32)
    for b in range(NB):
        cell = cell_ref[b : b + 1, :]
        chunk = cell // BP
        hot = jnp.where(place_of == cell % BP, 1.0, 0.0).astype(BF16)
        rows = jnp.concatenate([table_ref[owner_ref[b]], pad], axis=0)
        stacked = jnp.concatenate(parts3(rows), axis=0).astype(BF16)
        found = jnp.dot(stacked, hot, preferred_element_type=F32)
        found = found[0:16] + found[16:32] + found[32:48]
        mine = quarter == chunk
        out_ref[:, b * BP : (b + 1) * BP] = jnp.concatenate(
            [
                jnp.sum(jnp.where(mine, found[4 * c : 4 * c + 4], 0.0), axis=0, keepdims=True)
                for c in range(3)
            ],
            axis=0,
        )


def swap_pairs(count):
    near = [(d, d ^ 1) for d in range(count)]
    far = [(d, (d + 1) % count if d % 2 else (d - 1) % count) for d in range(count)]
    return near, far


def body(
    positions,
    velocities,
    particle_volume,
    drag_coef,
    gas_at_particle,
    pair_first,
    pair_second,
    ghost_list,
    block_owner,
    cell_map,
    gas_velocity,
):
    axes = ("grp", "dom")
    ndom = lax.axis_size("dom")
    near_pairs, far_pairs = swap_pairs(lax.axis_size("grp") * ndom)

    def exchange(near, far):
        far = lax.ppermute(far, axes, far_pairs)
        near = lax.ppermute(near, axes, near_pairs)
        return near, far

    par = (lax.axis_index("dom") % 2).astype(jnp.int32).reshape(1)
    mass = particle_volume.reshape(NB, BP)
    beta = drag_coef.reshape(NB, BP)
    cells = cell_map.reshape(NB, BP)
    owner = block_owner.reshape(NB)
    scalars = (par, ghost_list, pair_first, pair_second, owner)

    state, aux, near, far = prepare(par, ghost_list, positions, velocities, gas_at_particle, mass, beta)
    for step in range(SUBSTEPS):
        near, far = exchange(near, far)
        last = step == SUBSTEPS - 1
        state, near, far = contact_step(last, ndom, scalars, cells, state, near, far, aux)
    pos_out, vel_out, dep = state, near, far

    dep = lax.all_to_all(dep, "dom", 0, 0, tiled=True)

    tile = jax.ShapeDtypeStruct((8, BP), F32)
    void, known, low, high = pl.pallas_call(
        known_kernel,
        in_specs=[VMEM] * 2,
        out_shape=(
            jax.ShapeDtypeStruct((CHUNKS, BP), F32),
            jax.ShapeDtypeStruct((CHUNKS, 8, BP), F32),
            tile,
            tile,
        ),
        out_specs=(VMEM,) * 4,
        compiler_params=PARAMS,
        cost_estimate=cost(400000, 1600000),
        name="known",
    )(dep, gas_velocity)
    odd = par[0] == 1
    near, far = exchange(jnp.where(odd, low, high), jnp.where(odd, high, low))
    gas, table = pl.pallas_call(
        sweeps_kernel,
        in_specs=[SMEM] + [VMEM] * 3,
        out_shape=(
            jax.ShapeDtypeStruct((3, CHUNKS * BP), F32),
            jax.ShapeDtypeStruct((GASROWS, BP), F32),
        ),
        out_specs=(VMEM,) * 2,
        compiler_params=PARAMS,
        cost_estimate=cost(40000, 50000),
        name="sweeps",
    )(par, near, far, known)
    table = jnp.broadcast_to(table[None], (ndom, GASROWS, BP))
    table = lax.all_to_all(table, "dom", 0, 0, tiled=True)
    particle_gas = pl.pallas_call(
        pick_kernel,
        in_specs=[SMEM] + [VMEM] * 2,
        out_shape=jax.ShapeDtypeStruct((3, NB * BP), F32),
        out_specs=VMEM,
        compiler_params=PARAMS,
        cost_estimate=cost(60000000, 1200000),
        name="pick",
    )(owner, cells, table)
    return (pos_out, vel_out, gas, void.reshape(-1), particle_gas)


def solution(mesh):
    both = ("grp", "dom")
    return jax.shard_map(
        body,
        mesh=mesh,
        in_specs=(
            P(None, both),
            P(None, both),
            P(both),
            P(both),
            P(None, both),
            P(both),
            P(both),
            P(None, both),
            P(both, None),
            P(both),
            P(None, both),
        ),
        out_specs=(
            P(None, both),
            P(None, both),
            P(None, both),
            P(both),
            P(None, both),
        ),
        check_vma=False,
    )
```

time: 751 us -> 221 us (0.29)
  other arithmetic: 235 us -> 0.01 us
  waiting for transfers between devices: 196 us -> 53.6 us
  local copies, waits for them, and re-layouts: 110 us -> 7.39 us
  Pallas kernels: 0 us -> 57.1 us
  loops' own time: 49.9 us -> 0 us
  blocking collectives: 60.1 us -> 39.9 us
  starting transfers between devices: 77.5 us -> 60.4 us
  between operations: 15.1 us -> 0.83 us
    reduce_sum x192 -> x0, other arithmetic: 191 us -> none  [the longest x64 95.4 us: pair_force(): return jnp.sum(force, axis=3)]
    reduce_scatter x1 -> x0, waiting for transfers between devices: 188 us -> none  [body(): lax.psum_scatter(buffer.reshape(K, ndom * ncells), 'dom', scatter_dimensi...]
    all_gather x1 -> x0, blocking collectives: 60.1 us -> none  [body(): table = lax.all_gather(gas, 'dom', axis=1, tiled=True)]
    pallas_call x0 -> x8, Pallas kernels: none -> 57.1 us  [the longest x4 53.1 us: contact_step(): pl.pallas_call(functools.partial(step_kernel, last), in_specs=[SMEM] * 5...]
    another operation x5 -> x0, loops' own time: 49.9 us -> none  [the longest x4 47.2 us: contact_forces(): per_pair = lax.map(contact_one_group, jnp.arange(groups, dtype=jnp.int32))]
    gather x41 -> x0, local copies, waits for them, and re-layouts: 43 us -> none  [the longest x1 21.3 us: body(): particle_gas = table[:, index]]
    dynamic_slice x268 -> x0, local copies, waits for them, and re-layouts: 42.4 us -> none  [the longest x64 37.5 us: contact_forces(): per_pair = lax.map(contact_one_group, jnp.arange(groups, dtype=jnp.int32))]
    all_to_all x0 -> x1, waiting for transfers between devices: none -> 41.1 us  [body(): dep = lax.all_to_all(dep, 'dom', 0, 0, tiled=True)]
  transfers between devices with their start and end apart: 17 -> 11, of which waited for: 8 -> 6; matrix products, arithmetic and copies ran while one was open for 1% -> 0% of each run, Pallas kernels for 0% -> 0%
where the time goes in v1:
time: 221 us; the launch traced here: 219 us
  starting transfers between devices  60.4 us (27%)
  Pallas kernels  57.1 us (26%)
  waiting for transfers between devices  53.6 us (24%)
  blocking collectives  39.9 us (18%)
  local copies, waits for them, and re-layouts  7.39 us (3%)
    pallas_call x4, Pallas kernels, contact_step(): pl.pallas_call(functools.partial(step_kernel, last), in_specs=[SMEM] * 5...  53.1 us
    all_to_all x1, waiting for transfers between devices, body(): dep = lax.all_to_all(dep, 'dom', 0, 0, tiled=True)  41.1 us
    all_to_all x1, blocking collectives, body(): table = lax.all_to_all(table, 'dom', 0, 0, tiled=True)  39.9 us
    ppermute x5, starting transfers between devices, exchange(): near = lax.ppermute(near, axes, near_pairs)  30.4 us
    all_to_all x1, starting transfers between devices, body(): dep = lax.all_to_all(dep, 'dom', 0, 0, tiled=True)  17.5 us
    ppermute x5, waiting for transfers between devices, exchange(): far = lax.ppermute(far, axes, far_pairs)  12.5 us
    ppermute x5, starting transfers between devices, exchange(): far = lax.ppermute(far, axes, far_pairs)  12.5 us
    unnamed x30, local copies, waits for them, and re-layouts  7.32 us
  transfers between devices with their start and end apart: 11, of which 6 were waited for; matrix products, arithmetic and copies ran while one was open for 0% of the time, Pallas kernels for 0%

profile of v1, /device:TPU:7, one launch (start us, length us, event | category | flops | bytes accessed | tf_op | source)
XLA Modules:
  0.0 219.1 jit_solution(11386610006667580290)
XLA Ops:
  0.6 0.0 copy-start
  0.7 0.8 copy-done
  1.5 0.8 copy-done.1
  2.3 0.8 copy-done.2
  3.2 0.7 copy-done.5
  3.9 0.7 copy-done.6
  4.6 0.7 copy-done.8
  5.3 0.6 prepare.1
  5.9 2.6 %collective-permute-start = (f32[2,8,128]{2,1,0:T(8,128)S(1)}, f32[2,8,128]{2,1,0:T(8,128)S(1)}, u32[]{:S(2)}, u32[]{:S(2)}) collective-permute-start(f32[2,8,128]{2,1,0:T(8,128)S(1)} %get-tuple-element.28), channel_id=1, source_target_pairs={{0,1},{1,0},{2,3},{3,2},{4,5},{5,4},{6,7},{7,6},{8,9},{9,8},{10,11... | collective-permute-start | bytes 24584 | tf_op jit(solution)/shard_map/ppermute | solution.py:366
  8.5 3.9 %collective-permute-start.1 = (f32[2,8,128]{2,1,0:T(8,128)S(1)}, f32[2,8,128]{2,1,0:T(8,128)S(1)}, u32[]{:S(2)}, u32[]{:S(2)}) collective-permute-start(f32[2,8,128]{2,1,0:T(8,128)S(1)} %get-tuple-element.29), channel_id=1, source_target_pairs={{0,511},{1,2},{2,1},{3,4},{4,3},{5,6},{6,5},{7,8},{8,7},{9,10},{10... | collective-permute-start | bytes 24584 | tf_op jit(solution)/shard_map/ppermute | solution.py:365
  12.4 0.0 collective-permute-done.refs_7_
  12.4 1.3 collective-permute-done.1.refs_8_
  13.7 0.7 copy-done.3
  14.4 0.7 copy-done.9
  15.1 0.7 copy-done.11
  15.7 0.7 copy-done.13
  16.4 12.8 %contact.3 = (f32[32,8,128]{2,1,0:T(8,128)S(1)}, f32[2,8,128]{2,1,0:T(8,128)S(1)}, f32[2,8,128]{2,1,0:T(8,128)S(1)}) custom-call(s32[1]{0:T(128)} %bitcast.par_ref.refs_0_, s32[2,2]{1,0:T(2,128)S(1)} %copy-done.8, s32[128]{0:T(128)S(1)} %copy-done.11, s32[128]{0:T(128)S(1)} %copy-done.13, s32[32]{0:T(128)S(1)} %bitcast.13, s32[32,128]{1,0:T(8,128)S(1)} %bitcast.6, ...), custom_call_target="tpu_custom_call" | custom-call | flops 1500000000 | bytes 2000000 | tf_op jit(solution)/shard_map/contact/pallas_call | solution.py:260
  29.2 12.3 %collective-permute-start.2 = (f32[2,8,128]{2,1,0:T(8,128)S(1)}, f32[2,8,128]{2,1,0:T(8,128)S(1)}, u32[]{:S(2)}, u32[]{:S(2)}) collective-permute-start(f32[2,8,128]{2,1,0:T(8,128)S(1)} %get-tuple-element.32), channel_id=1, source_target_pairs={{0,1},{1,0},{2,3},{3,2},{4,5},{5,4},{6,7},{7,6},{8,9},{9,8},{10,11... | collective-permute-start | bytes 24584 | tf_op jit(solution)/shard_map/ppermute | solution.py:366
  41.5 1.9 collective-permute-start.3
  43.4 0.0 collective-permute-done.2.refs_7_
  43.4 3.0 %collective-permute-done.3.refs_8_ = f32[2,8,128]{2,1,0:T(8,128)S(1)} collective-permute-done((f32[2,8,128]{2,1,0:T(8,128)S(1)}, f32[2,8,128]{2,1,0:T(8,128)S(1)}, u32[]{:S(2)}, u32[]{:S(2)}) %collective-permute-start.3) | collective-permute-done | bytes 8224 | tf_op jit(solution)/shard_map/ppermute | solution.py:365
  46.4 0.0 copy-done.4
  46.4 0.0 copy-done.10
  46.4 12.8 %contact.4 = (f32[32,8,128]{2,1,0:T(8,128)S(1)}, f32[2,8,128]{2,1,0:T(8,128)S(1)}, f32[2,8,128]{2,1,0:T(8,128)S(1)}) custom-call(s32[1]{0:T(128)} %bitcast.par_ref.refs_0_, s32[2,2]{1,0:T(2,128)S(1)} %copy-done.8, s32[128]{0:T(128)S(1)} %copy-done.11, s32[128]{0:T(128)S(1)} %copy-done.13, s32[32]{0:T(128)S(1)} %bitcast.14, s32[32,128]{1,0:T(8,128)S(1)} %bitcast.7, ...), custom_call_target="tpu_custom_call" | custom-call | flops 1500000000 | bytes 2000000 | tf_op jit(solution)/shard_map/contact/pallas_call | solution.py:260
  59.2 6.1 %collective-permute-start.4 = (f32[2,8,128]{2,1,0:T(8,128)S(1)}, f32[2,8,128]{2,1,0:T(8,128)S(1)}, u32[]{:S(2)}, u32[]{:S(2)}) collective-permute-start(f32[2,8,128]{2,1,0:T(8,128)S(1)} %get-tuple-element.35), channel_id=1, source_target_pairs={{0,1},{1,0},{2,3},{3,2},{4,5},{5,4},{6,7},{7,6},{8,9},{9,8},{10,11... | collective-permute-start | bytes 24584 | tf_op jit(solution)/shard_map/ppermute | solution.py:366
  65.4 1.9 collective-permute-start.5
  67.3 0.0 collective-permute-done.4.refs_7_
  67.3 3.0 %collective-permute-done.5.refs_8_ = f32[2,8,128]{2,1,0:T(8,128)S(1)} collective-permute-done((f32[2,8,128]{2,1,0:T(8,128)S(1)}, f32[2,8,128]{2,1,0:T(8,128)S(1)}, u32[]{:S(2)}, u32[]{:S(2)}) %collective-permute-start.5) | collective-permute-done | bytes 8224 | tf_op jit(solution)/shard_map/ppermute | solution.py:365
  70.3 12.8 %contact.5 = (f32[32,8,128]{2,1,0:T(8,128)S(1)}, f32[2,8,128]{2,1,0:T(8,128)S(1)}, f32[2,8,128]{2,1,0:T(8,128)S(1)}) custom-call(s32[1]{0:T(128)} %bitcast.par_ref.refs_0_, s32[2,2]{1,0:T(2,128)S(1)} %copy-done.8, s32[128]{0:T(128)S(1)} %copy-done.11, s32[128]{0:T(128)S(1)} %copy-done.13, s32[32]{0:T(128)S(1)} %bitcast.15, s32[32,128]{1,0:T(8,128)S(1)} %bitcast.8, ...), custom_call_target="tpu_custom_call" | custom-call | flops 1500000000 | bytes 2000000 | tf_op jit(solution)/shard_map/contact/pallas_call | solution.py:260
  83.1 6.1 %collective-permute-start.6 = (f32[2,8,128]{2,1,0:T(8,128)S(1)}, f32[2,8,128]{2,1,0:T(8,128)S(1)}, u32[]{:S(2)}, u32[]{:S(2)}) collective-permute-start(f32[2,8,128]{2,1,0:T(8,128)S(1)} %get-tuple-element.38), channel_id=1, source_target_pairs={{0,1},{1,0},{2,3},{3,2},{4,5},{5,4},{6,7},{7,6},{8,9},{9,8},{10,11... | collective-permute-start | bytes 24584 | tf_op jit(solution)/shard_map/ppermute | solution.py:366
  89.3 1.9 collective-permute-start.7
  91.2 0.0 collective-permute-done.6.refs_7_
  91.2 3.0 %collective-permute-done.7.refs_8_ = f32[2,8,128]{2,1,0:T(8,128)S(1)} collective-permute-done((f32[2,8,128]{2,1,0:T(8,128)S(1)}, f32[2,8,128]{2,1,0:T(8,128)S(1)}, u32[]{:S(2)}, u32[]{:S(2)}) %collective-permute-start.7) | collective-permute-done | bytes 8224 | tf_op jit(solution)/shard_map/ppermute | solution.py:365
  94.2 0.0 copy-done.12
  94.2 0.0 copy-done.14
  94.3 14.7 %contact_last.1 = (f32[3,4096]{1,0:T(4,128)}, f32[3,4096]{1,0:T(4,128)}, f32[128,24,128]{2,1,0:T(8,128)}) custom-call(s32[1]{0:T(128)} %bitcast.par_ref.refs_0_, s32[2,2]{1,0:T(2,128)S(1)} %copy-done.8, s32[128]{0:T(128)S(1)} %copy-done.12, s32[128]{0:T(128)S(1)} %copy-done.14, s32[32]{0:T(128)S(1)} %bitcast.16, s32[32,128]{1,0:T(8,128)S(1)} %bitcast.9, ...), custom_call_target="tpu_custom_call" | custom-call | flops 1500000000 | bytes 2000000 | tf_op jit(solution)/shard_map/contact_last/pallas_call | solution.py:260
  109.0 17.5 %all-to-all-start = ((f32[128,24,128]{2,1,0:T(8,128)}), f32[128,24,128]{2,1,0:T(8,128)S(1)}, u32[]{:S(2)}, u32[]{:S(2)}) async-start(f32[128,24,128]{2,1,0:T(8,128)} %get-tuple-element.42), calls=%async_computation | async-start | bytes 3145728 | tf_op jit(solution)/shard_map/all_to_all | solution.py:383
  126.5 41.1 %all-to-all-done.dep_ref = f32[128,24,128]{2,1,0:T(8,128)S(1)} async-done(((f32[128,24,128]{2,1,0:T(8,128)}), f32[128,24,128]{2,1,0:T(8,128)S(1)}, u32[]{:S(2)}, u32[]{:S(2)}) %all-to-all-start) | async-done | bytes 1572896 | tf_op jit(solution)/shard_map/all_to_all | solution.py:383
  167.6 0.0 copy-done.7
  167.6 0.7 known.1
  168.3 3.3 %collective-permute-start.8 = (f32[8,128]{1,0:T(8,128)S(1)}, f32[8,128]{1,0:T(8,128)S(1)}, u32[]{:S(2)}, u32[]{:S(2)}) collective-permute-start(f32[8,128]{1,0:T(8,128)S(1)} %get-tuple-element.50), channel_id=1, source_target_pairs={{0,1},{1,0},{2,3},{3,2},{4,5},{5,4},{6,7},{7,6},{8,9},{9,8},{10,11... | collective-permute-start | bytes 12296 | tf_op jit(solution)/shard_map/ppermute | solution.py:366
  171.6 2.8 %collective-permute-start.9 = (f32[8,128]{1,0:T(8,128)S(1)}, f32[8,128]{1,0:T(8,128)S(1)}, u32[]{:S(2)}, u32[]{:S(2)}) collective-permute-start(f32[8,128]{1,0:T(8,128)S(1)} %get-tuple-element.49), channel_id=1, source_target_pairs={{0,511},{1,2},{2,1},{3,4},{4,3},{5,6},{6,5},{7,8},{8,7},{9,10},{10... | collective-permute-start | bytes 12296 | tf_op jit(solution)/shard_map/ppermute | solution.py:365
  174.4 0.0 collective-permute-done.8.near_ref
  174.4 2.1 collective-permute-done.9.far_ref
  176.5 0.9 sweeps.1
  177.5 0.1 broadcast_in_dim.2
  177.5 39.9 %all_to_all.10.table_ref = f32[128,12,128]{2,1,0:T(8,128)S(1)} all-to-all(f32[128,12,128]{2,1,0:T(8,128)S(1)} %broadcast_in_dim.2), channel_id=1, replica_groups=mesh['grp'=4,'dom'=128] {'dom'}, dimensions={0} | all-to-all | bytes 1572864 | tf_op jit(solution)/shard_map/all_to_all | solution.py:415
  217.4 1.7 pick.1
  (15 shorter events, 0.0 us)
Async XLA Ops:
  0.6 0.8 copy-start
  1.5 0.8 copy-start.1
  2.3 0.8 copy-start.2
  3.2 0.7 copy-start.5
  3.9 0.7 copy-start.6
  4.6 0.7 copy-start.8
  5.9 6.5 %collective-permute-start = (f32[2,8,128]{2,1,0:T(8,128)S(1)}, f32[2,8,128]{2,1,0:T(8,128)S(1)}, u32[]{:S(2)}, u32[]{:S(2)}) collective-permute-start(f32[2,8,128]{2,1,0:T(8,128)S(1)} %get-tuple-element.28), channel_id=1, source_target_pairs={{0,1},{1,0},{2,3},{3,2},{4,5},{5,4},{6,7},{7,6},{8,9},{9,8},{10,11... | collective-permute-start | bytes 24584 | tf_op jit(solution)/shard_map/ppermute | solution.py:366
  8.5 5.2 %collective-permute-start.1 = (f32[2,8,128]{2,1,0:T(8,128)S(1)}, f32[2,8,128]{2,1,0:T(8,128)S(1)}, u32[]{:S(2)}, u32[]{:S(2)}) collective-permute-start(f32[2,8,128]{2,1,0:T(8,128)S(1)} %get-tuple-element.29), channel_id=1, source_target_pairs={{0,511},{1,2},{2,1},{3,4},{4,3},{5,6},{6,5},{7,8},{8,7},{9,10},{10... | collective-permute-start | bytes 24584 | tf_op jit(solution)/shard_map/ppermute | solution.py:365
  13.7 0.7 copy-start.3
  14.4 0.7 copy-start.9
  15.1 0.7 copy-start.11
  15.7 0.7 copy-start.13
  16.4 30.0 %copy-start.4 = (s32[4096]{0:T(1024)S(1)}, s32[4096]{0:T(1024)}, u32[]{:S(2)}) copy-start(s32[4096]{0:T(1024)} %param.20) | copy-start | bytes 49156
  16.4 30.0 %copy-start.10 = (s32[32,1]{0,1:T(1,128)S(1)}, s32[32,1]{0,1:T(1,128)}, u32[]{:S(2)}) copy-start(s32[32,1]{0,1:T(1,128)} %param.19) | copy-start | bytes 388
  29.2 14.2 %collective-permute-start.2 = (f32[2,8,128]{2,1,0:T(8,128)S(1)}, f32[2,8,128]{2,1,0:T(8,128)S(1)}, u32[]{:S(2)}, u32[]{:S(2)}) collective-permute-start(f32[2,8,128]{2,1,0:T(8,128)S(1)} %get-tuple-element.32), channel_id=1, source_target_pairs={{0,1},{1,0},{2,3},{3,2},{4,5},{5,4},{6,7},{7,6},{8,9},{9,8},{10,11... | collective-permute-start | bytes 24584 | tf_op jit(solution)/shard_map/ppermute | solution.py:366
  41.5 5.0 %collective-permute-start.3 = (f32[2,8,128]{2,1,0:T(8,128)S(1)}, f32[2,8,128]{2,1,0:T(8,128)S(1)}, u32[]{:S(2)}, u32[]{:S(2)}) collective-permute-start(f32[2,8,128]{2,1,0:T(8,128)S(1)} %get-tuple-element.33), channel_id=1, source_target_pairs={{0,511},{1,2},{2,1},{3,4},{4,3},{5,6},{6,5},{7,8},{8,7},{9,10},{10... | collective-permute-start | bytes 24584 | tf_op jit(solution)/shard_map/ppermute | solution.py:365
  59.2 8.1 %collective-permute-start.4 = (f32[2,8,128]{2,1,0:T(8,128)S(1)}, f32[2,8,128]{2,1,0:T(8,128)S(1)}, u32[]{:S(2)}, u32[]{:S(2)}) collective-permute-start(f32[2,8,128]{2,1,0:T(8,128)S(1)} %get-tuple-element.35), channel_id=1, source_target_pairs={{0,1},{1,0},{2,3},{3,2},{4,5},{5,4},{6,7},{7,6},{8,9},{9,8},{10,11... | collective-permute-start | bytes 24584 | tf_op jit(solution)/shard_map/ppermute | solution.py:366
  65.4 5.0 %collective-permute-start.5 = (f32[2,8,128]{2,1,0:T(8,128)S(1)}, f32[2,8,128]{2,1,0:T(8,128)S(1)}, u32[]{:S(2)}, u32[]{:S(2)}) collective-permute-start(f32[2,8,128]{2,1,0:T(8,128)S(1)} %get-tuple-element.36), channel_id=1, source_target_pairs={{0,511},{1,2},{2,1},{3,4},{4,3},{5,6},{6,5},{7,8},{8,7},{9,10},{10... | collective-permute-start | bytes 24584 | tf_op jit(solution)/shard_map/ppermute | solution.py:365
  70.3 23.9 %copy-start.12 = (s32[128]{0:T(128)S(1)}, s32[128]{0:T(128)}, u32[]{:S(2)}) copy-start(s32[128]{0:T(128)} %refs_2_.7) | copy-start | bytes 1540
  70.3 23.9 %copy-start.14 = (s32[128]{0:T(128)S(1)}, s32[128]{0:T(128)}, u32[]{:S(2)}) copy-start(s32[128]{0:T(128)} %refs_3_.7) | copy-start | bytes 1540
  83.1 8.1 %collective-permute-start.6 = (f32[2,8,128]{2,1,0:T(8,128)S(1)}, f32[2,8,128]{2,1,0:T(8,128)S(1)}, u32[]{:S(2)}, u32[]{:S(2)}) collective-permute-start(f32[2,8,128]{2,1,0:T(8,128)S(1)} %get-tuple-element.38), channel_id=1, source_target_pairs={{0,1},{1,0},{2,3},{3,2},{4,5},{5,4},{6,7},{7,6},{8,9},{9,8},{10,11... | collective-permute-start | bytes 24584 | tf_op jit(solution)/shard_map/ppermute | solution.py:366
  89.3 5.0 %collective-permute-start.7 = (f32[2,8,128]{2,1,0:T(8,128)S(1)}, f32[2,8,128]{2,1,0:T(8,128)S(1)}, u32[]{:S(2)}, u32[]{:S(2)}) collective-permute-start(f32[2,8,128]{2,1,0:T(8,128)S(1)} %get-tuple-element.39), channel_id=1, source_target_pairs={{0,511},{1,2},{2,1},{3,4},{4,3},{5,6},{6,5},{7,8},{8,7},{9,10},{10... | collective-permute-start | bytes 24584 | tf_op jit(solution)/shard_map/ppermute | solution.py:365
  109.0 58.6 %copy-start.7 = (f32[3,512]{1,0:T(4,128)S(1)}, f32[3,512]{1,0:T(4,128)}, u32[]{:S(2)}) copy-start(f32[3,512]{1,0:T(4,128)} %gas_ref.3) | copy-start | bytes 18436
  109.0 58.6 %all-to-all-start = ((f32[128,24,128]{2,1,0:T(8,128)}), f32[128,24,128]{2,1,0:T(8,128)S(1)}, u32[]{:S(2)}, u32[]{:S(2)}) async-start(f32[128,24,128]{2,1,0:T(8,128)} %get-tuple-element.42), calls=%async_computation | async-start | bytes 3145728 | tf_op jit(solution)/shard_map/all_to_all | solution.py:383
  168.3 6.1 %collective-permute-start.8 = (f32[8,128]{1,0:T(8,128)S(1)}, f32[8,128]{1,0:T(8,128)S(1)}, u32[]{:S(2)}, u32[]{:S(2)}) collective-permute-start(f32[8,128]{1,0:T(8,128)S(1)} %get-tuple-element.50), channel_id=1, source_target_pairs={{0,1},{1,0},{2,3},{3,2},{4,5},{5,4},{6,7},{7,6},{8,9},{9,8},{10,11... | collective-permute-start | bytes 12296 | tf_op jit(solution)/shard_map/ppermute | solution.py:366
  171.6 4.9 %collective-permute-start.9 = (f32[8,128]{1,0:T(8,128)S(1)}, f32[8,128]{1,0:T(8,128)S(1)}, u32[]{:S(2)}, u32[]{:S(2)}) collective-permute-start(f32[8,128]{1,0:T(8,128)S(1)} %get-tuple-element.49), channel_id=1, source_target_pairs={{0,511},{1,2},{2,1},{3,4},{4,3},{5,6},{6,5},{7,8},{8,7},{9,10},{10... | collective-permute-start | bytes 12296 | tf_op jit(solution)/shard_map/ppermute | solution.py:365

commit v2 on v1

v2 whole, which is shorter than its diff:
```python
import functools

import jax
import jax.numpy as jnp
from jax import lax
from jax.experimental import pallas as pl
from jax.experimental.pallas import tpu as pltpu
from jax.sharding import PartitionSpec as P

NB = 32
BP = 128
NG = 2
NEXT = NB + 2 * NG
NPAIR = 128
GROUP = 8
SUBSTEPS = 4
SWEEPS = 4
K = 5
CHUNKS = 4
DEPROWS = 24
ROOM = NPAIR + GROUP
LISTS = 4 * ROOM + 8

SLAB = 4.0
SOFT = 0.01
STIFF = 20.0
STEP = 0.01
GRAVITY_Z = -1.0
RADIUS_FACTOR = 0.62
CELL_VOLUME = 16.0
RHO_STEP = 2.0
VISCOSITY = 1.0
TINY = 1e-36

F32 = jnp.float32
BF16 = jnp.bfloat16
VMEM = pl.BlockSpec(memory_space=pltpu.VMEM)
SMEM = pl.BlockSpec(memory_space=pltpu.SMEM)
PARAMS = pltpu.CompilerParams(vmem_limit_bytes=24 * 1024 * 1024)


def cost(flops, nbytes, transcendentals=0):
    return pl.CostEstimate(flops=flops, bytes_accessed=nbytes, transcendentals=transcendentals)


def parts3(value):
    high = value.astype(BF16).astype(F32)
    rest = value - high
    mid = rest.astype(BF16).astype(F32)
    low = (rest - mid).astype(BF16).astype(F32)
    return high, mid, low


def swap3(tile):
    return jnp.concatenate([tile[:, 3:6], tile[:, 0:3], tile[:, 6:8]], axis=1)


def fill_sends(par_ref, ghost_ref, state_ref, near_ref, far_ref):
    par = par_ref[0]
    for s in range(NG):
        near_ref[s] = state_ref[ghost_ref[par, s]]
        far_ref[s] = state_ref[ghost_ref[1 - par, s]]


def prepare_kernel(
    par_ref, ghost_hbm, pos_hbm, vel_hbm, gas_hbm, mass_hbm, beta_hbm, first_hbm, second_hbm,
    state_ref, aux_ref, rb_ref, near_ref, far_ref, list_ref,
    ghost_ref, pos_ref, vel_ref, gas_ref, mass_ref, beta_ref, first_ref, second_ref, sems,
):
    sources = (ghost_hbm, pos_hbm, vel_hbm, gas_hbm, mass_hbm, beta_hbm, first_hbm, second_hbm)
    targets = (ghost_ref, pos_ref, vel_ref, gas_ref, mass_ref, beta_ref, first_ref, second_ref)
    copies = [pltpu.make_async_copy(s, t, sems.at[i]) for i, (s, t) in enumerate(zip(sources, targets))]
    for copy in copies:
        copy.start()
    for copy in copies:
        copy.wait()
    radius = RADIUS_FACTOR * jnp.exp(jnp.log(mass_ref[...]) * (1.0 / 3.0))
    zero3 = jnp.zeros((3, BP), F32)
    for b in range(NB):
        lanes = slice(b * BP, (b + 1) * BP)
        rows = slice(b, b + 1)
        state_ref[b] = jnp.concatenate(
            [pos_ref[:, lanes], vel_ref[:, lanes], radius[rows], jnp.zeros((1, BP), F32)], axis=0
        )
        aux_ref[b] = jnp.concatenate([zero3, gas_ref[:, lanes], beta_ref[rows], mass_ref[rows]], axis=0)
    fill_sends(par_ref, ghost_ref, state_ref, near_ref, far_ref)
    column = jnp.transpose(radius)
    for b in range(NB):
        rb_ref[b] = jnp.broadcast_to(column[:, b : b + 1], (BP, BP))

    def sort_pair(p, counts):
        local, ghost = counts
        first = first_ref[p]
        second = second_ref[p]
        is_ghost = (second >= NB).astype(jnp.int32)
        slot = jnp.where(is_ghost == 1, 2 * ROOM + ghost, local)
        list_ref[slot] = first
        list_ref[ROOM + slot] = second
        return local + 1 - is_ghost, ghost + is_ghost

    local, ghost = lax.fori_loop(0, NPAIR, sort_pair, (jnp.int32(0), jnp.int32(0)))
    for s in range(GROUP):
        list_ref[local + s] = NB
        list_ref[ROOM + local + s] = 0
        list_ref[2 * ROOM + ghost + s] = NB
        list_ref[3 * ROOM + ghost + s] = NB
    list_ref[4 * ROOM] = (local + GROUP - 1) // GROUP
    list_ref[4 * ROOM + 1] = (ghost + GROUP - 1) // GROUP


def prepare(par, ghost_list, pos, vel, gas_seen, mass, beta, first, second):
    tile = jax.ShapeDtypeStruct((NB, 8, BP), F32)
    send = jax.ShapeDtypeStruct((NG, 8, BP), F32)
    wide = jax.ShapeDtypeStruct((NB, BP, BP), F32)
    lists = jax.ShapeDtypeStruct((LISTS,), jnp.int32)
    return pl.pallas_call(
        prepare_kernel,
        in_specs=[SMEM] + [pl.BlockSpec(memory_space=pl.ANY)] * 8,
        out_shape=(tile, tile, wide, send, send, lists),
        out_specs=(VMEM,) * 5 + (SMEM,),
        scratch_shapes=[
            pltpu.SMEM((2, NG), jnp.int32),
            pltpu.VMEM((3, NB * BP), F32),
            pltpu.VMEM((3, NB * BP), F32),
            pltpu.VMEM((3, NB * BP), F32),
            pltpu.VMEM((NB, BP), F32),
            pltpu.VMEM((NB, BP), F32),
            pltpu.SMEM((NPAIR,), jnp.int32),
            pltpu.SMEM((NPAIR,), jnp.int32),
            pltpu.SemaphoreType.DMA((8,)),
        ],
        compiler_params=pltpu.CompilerParams(vmem_limit_bytes=58 * 1024 * 1024),
        cost_estimate=cost(100000, 3000000),
        name="prepare",
    )(par, ghost_list, pos, vel, gas_seen, mass, beta, first, second)


def row_index():
    return lax.broadcasted_iota(jnp.int32, (8, BP), 0)[None]


def features(tile):
    row = row_index()
    swapped = swap3(tile)
    norm = jnp.sum(jnp.where(row < 3, tile * tile, 0.0), axis=1, keepdims=True)
    cross = jnp.sum(jnp.where(row < 3, tile * swapped, 0.0), axis=1, keepdims=True) * (1.0 / STIFF)
    return swapped, norm, cross


def partner_side(tile, base, jt_ref, a_ref):
    row = row_index()
    r = row[0]
    ones = jnp.ones((8, BP), F32)
    zeros = jnp.zeros((8, BP), F32)
    swapped, norm, cross = features(tile)
    full = jnp.where(row < 6, tile, jnp.where(row == 6, norm, cross))
    high, mid, low = parts3(full)
    is_v = (r >= 3) & (r < 6)
    for s in range(4):
        h, m, l = high[s], mid[s], low[s]
        stack = jnp.concatenate([h, h, h, m, m, l, ones, zeros], axis=0)
        jt_ref[base + s] = jnp.transpose(stack).astype(BF16)
        by_x = jnp.concatenate(
            [
                jnp.where(r < 3, h, jnp.where(r == 6, 1.0, 0.0)),
                jnp.where(r < 3, m, 0.0),
                jnp.where(r < 3, l, 0.0),
                zeros,
            ],
            axis=0,
        )
        by_v = jnp.concatenate(
            [
                jnp.where(is_v, h, jnp.where(r == 7, 1.0, 0.0)),
                jnp.where(is_v, m, 0.0),
                jnp.where(is_v, l, 0.0),
                zeros,
            ],
            axis=0,
        )
        a_ref[base + s] = jnp.concatenate([by_x, by_v], axis=1).astype(BF16)


def own_side(tile, base, g_ref):
    row = row_index()
    zeros = jnp.zeros((8, BP), F32)
    swapped, norm, cross = features(tile)
    xh, xm, xl = parts3(jnp.where(row < 3, -2.0 * tile, 0.0))
    xh = jnp.where(row == 6, 1.0, xh)
    vh, vm, vl = parts3(jnp.where(row < 6, swapped * (-1.0 / STIFF), 0.0))
    vh = jnp.where(row == 7, 1.0, vh)
    nh, nm, nl = parts3(norm + SOFT)
    ch, cm, cl = parts3(cross)
    own_n = jnp.where(row == 0, nh, jnp.where(row == 1, nm, jnp.where(row == 2, nl, 0.0)))
    own_c = jnp.where(row == 0, ch, jnp.where(row == 1, cm, jnp.where(row == 2, cl, 0.0)))
    for s in range(4):
        left = jnp.concatenate([xh[s], xm[s], xl[s], xh[s], xm[s], xh[s], own_n[s], zeros], axis=0)
        right = jnp.concatenate([vh[s], vm[s], vl[s], vh[s], vm[s], vh[s], own_c[s], zeros], axis=0)
        g_ref[base + s] = jnp.concatenate([left, right], axis=1).astype(BF16)


def pair_sums(a, b, state_ref, jt_ref, g_ref, a_ref, rb_ref):
    both = jnp.dot(jt_ref[b], g_ref[a], preferred_element_type=F32)
    dist2 = both[:, :BP]
    slide = both[:, BP:]
    inv = lax.rsqrt(dist2)
    overlap = (rb_ref[b] + state_ref[a, 6:7, :]) - dist2 * inv
    delta = jnp.maximum(overlap, 0.0)
    root = delta * lax.rsqrt(jnp.maximum(overlap, TINY))
    push = (root * inv) * (delta - slide * inv)
    push_high = push.astype(BF16)
    push_low = (push - push_high.astype(F32)).astype(BF16)
    root_high = root.astype(BF16)
    root_low = (root - root_high.astype(F32)).astype(BF16)
    weights = jnp.concatenate([push_high, push_low, root_high, root_low], axis=0)
    left_x = a_ref[b, :, :BP]
    left_v = a_ref[b, :, BP:]
    left = jnp.concatenate([left_x, left_x, left_v, left_v], axis=1)
    sums = jnp.dot(left, weights, preferred_element_type=F32)
    return sums[0:8] + sums[8:16] + sums[16:24]


def all_pairs(groups, offset, partner_base, list_ref, acc_ref, state_ref, jt_ref, g_ref, a_ref, rb_ref):
    def group(k, carry):
        start = offset + k * GROUP
        firsts = [list_ref[start + s] for s in range(GROUP)]
        seconds = [list_ref[start + ROOM + s] - partner_base for s in range(GROUP)]
        sums = [
            pair_sums(jnp.minimum(a, NB - 1), b, state_ref, jt_ref, g_ref, a_ref, rb_ref)
            for a, b in zip(firsts, seconds)
        ]
        for a, value in zip(firsts, sums):
            acc_ref[a] += value
        return carry

    lax.fori_loop(0, groups, group, 0)


def local_kernel(list_ref, state_ref, rb_ref, acc_ref, g_ref, jt_ref, a_ref):
    def blocks(k, carry):
        tile = state_ref[pl.ds(k * 4, 4)]
        partner_side(tile, k * 4, jt_ref, a_ref)
        own_side(tile, k * 4, g_ref)
        return carry

    lax.fori_loop(0, NB // 4, blocks, 0)
    acc_ref[...] = jnp.zeros(acc_ref.shape, F32)
    all_pairs(list_ref[4 * ROOM], 0, 0, list_ref, acc_ref, state_ref, jt_ref, g_ref, a_ref, rb_ref)


def local_pairs(lists, state, rb):
    return pl.pallas_call(
        local_kernel,
        in_specs=[SMEM] + [VMEM] * 2,
        out_shape=(
            jax.ShapeDtypeStruct((NB + 1, 8, BP), F32),
            jax.ShapeDtypeStruct((NB, 64, 2 * BP), BF16),
        ),
        out_specs=(VMEM,) * 2,
        scratch_shapes=[pltpu.VMEM((NB, BP, 64), BF16), pltpu.VMEM((NB, 32, 2 * BP), BF16)],
        compiler_params=PARAMS,
        cost_estimate=cost(10000000000, 3500000, 4000000),
        name="local_pairs",
    )(lists, state, rb)


def ghost_kernel(last, *refs):
    (par_ref, ghost_ref, list_ref, owner_ref), refs = refs[:4], refs[4:]
    (cell_ref, state_ref, near_in, far_in, aux_ref, part_ref, g_ref), refs = refs[:7], refs[7:]
    if last:
        (pos_out, vel_out, keep_ref, give_ref), scratch = refs[:4], refs[4:]
    else:
        (new_ref, near_out, far_out), scratch = refs[:3], refs[3:]
    ext_ref, jt_ref, a_ref, rb_ref, acc_ref = scratch
    par = par_ref[0]
    row = row_index()

    sign = 1.0 - 2.0 * par.astype(F32)
    shift = jnp.where(row[0] == 0, SLAB * sign, 0.0)
    for s in range(NG):
        ext_ref[NG * (1 - par) + s] = near_in[s] + shift
        ext_ref[NG * par + s] = far_in[s] - shift
    for s in range(2 * NG, 8):
        ext_ref[s] = jnp.zeros((8, BP), F32)
    column = jnp.transpose(ext_ref[:, 6, :])
    for b in range(2 * NG):
        rb_ref[b] = jnp.broadcast_to(column[:, b : b + 1], (BP, BP))
    partner_side(ext_ref[0:4], 0, jt_ref, a_ref)
    acc_ref[...] = part_ref[...]
    all_pairs(
        list_ref[4 * ROOM + 1], 2 * ROOM, NB, list_ref, acc_ref, state_ref, jt_ref, g_ref, a_ref, rb_ref
    )

    tile = state_ref[...]
    acc = acc_ref[0:NB]
    aux = aux_ref[...]
    by_x = STIFF * (tile * acc[:, 6:7] - acc)
    by_v = acc - tile * acc[:, 7:8]
    force = swap3(by_x) + by_v
    beta = aux[:, 6:7]
    mass = aux[:, 7:8]
    gravity = jnp.where(row == 5, GRAVITY_Z, 0.0)
    velocity = tile + STEP * ((force + beta * (aux - tile)) / mass + gravity)
    place = tile + STEP * swap3(velocity)
    moved = jnp.where(row < 3, place, jnp.where(row < 6, velocity, tile))

    if not last:
        new_ref[...] = moved
        fill_sends(par_ref, ghost_ref, new_ref, near_out, far_out)
        return

    for b in range(NB):
        lanes = slice(b * BP, (b + 1) * BP)
        pos_out[:, lanes] = moved[b, 0:3]
        vel_out[:, lanes] = moved[b, 3:6]

    keep_ref[...] = jnp.zeros(keep_ref.shape, F32)
    give_ref[...] = jnp.zeros(give_ref.shape, F32)
    drag = beta * moved
    quarter = lax.broadcasted_iota(jnp.int32, (DEPROWS, BP), 0) % CHUNKS
    place_of = lax.broadcasted_iota(jnp.int32, (BP, BP), 0)
    zeros = jnp.zeros((8, BP), F32)
    tail = jnp.zeros((DEPROWS - CHUNKS * K, BP), F32)
    for b in range(NB):
        cell = cell_ref[b : b + 1, :]
        chunk = cell // BP
        hot = jnp.where(place_of == cell % BP, 1.0, 0.0).astype(BF16)
        values = [mass[b], beta[b], drag[b, 3:4], drag[b, 4:5], drag[b, 5:6]]
        amounts = jnp.concatenate([jnp.broadcast_to(v, (CHUNKS, BP)) for v in values] + [tail], axis=0)
        amounts = jnp.where(quarter == chunk, amounts, 0.0)
        stacked = jnp.concatenate(list(parts3(amounts)) + [zeros], axis=0).astype(BF16)
        spread = lax.dot_general(stacked, hot, (((1,), (1,)), ((), ())), preferred_element_type=F32)
        spread = spread[0:DEPROWS] + spread[DEPROWS : 2 * DEPROWS] + spread[2 * DEPROWS : 3 * DEPROWS]
        owner = owner_ref[b]
        chip = owner // 2
        mine = owner % 2 == par

        def put(target, chip=chip, spread=spread):
            for q in range(K):
                target[chip, q] += spread[CHUNKS * q : CHUNKS * (q + 1)]

        pl.when(mine)(functools.partial(put, keep_ref))
        pl.when(jnp.logical_not(mine))(functools.partial(put, give_ref))


def ghost_pairs(last, chips, scalars, cells, state, near, far, aux, part, g):
    tile = jax.ShapeDtypeStruct((NB, 8, BP), F32)
    send = jax.ShapeDtypeStruct((NG, 8, BP), F32)
    if last:
        flat = jax.ShapeDtypeStruct((3, NB * BP), F32)
        dep = jax.ShapeDtypeStruct((chips, K, CHUNKS, BP), F32)
        outs = (flat, flat, dep, dep)
    else:
        outs = (tile, send, send)
    return pl.pallas_call(
        functools.partial(ghost_kernel, last),
        in_specs=[SMEM] * 4 + [VMEM] * 7,
        out_shape=outs,
        out_specs=(VMEM,) * len(outs),
        scratch_shapes=[
            pltpu.VMEM((8, 8, BP), F32),
            pltpu.VMEM((2 * NG, BP, 64), BF16),
            pltpu.VMEM((2 * NG, 32, 2 * BP), BF16),
            pltpu.VMEM((2 * NG, BP, BP), F32),
            pltpu.VMEM((NB + 1, 8, BP), F32),
        ],
        compiler_params=PARAMS,
        cost_estimate=cost(2000000000, 2000000, 500000),
        name="ghost_pairs_last" if last else "ghost_pairs",
    )(*scalars, cells, state, near, far, aux, part, g)


def known_kernel(dep_ref, gas_ref, void_ref, known_ref, low_ref, high_ref):
    dep = jnp.sum(dep_ref[...], axis=0)
    void = CELL_VOLUME / (CELL_VOLUME + dep[0])
    inertia = RHO_STEP * void
    void_ref[...] = void
    gas = [
        jnp.concatenate([gas_ref[c : c + 1, s * BP : (s + 1) * BP] for s in range(CHUNKS)], axis=0)
        for c in range(3)
    ]
    diag = inertia + dep[1] / CELL_VOLUME + 2.0 * VISCOSITY
    known = [inertia * gas[c] + dep[2 + c] / CELL_VOLUME for c in range(3)]
    for s in range(CHUNKS):
        one = slice(s, s + 1)
        known_ref[s] = jnp.concatenate(
            [g[one] for g in gas] + [k[one] for k in known] + [diag[one], diag[one]], axis=0
        )
    low_ref[...] = known_ref[0]
    high_ref[...] = known_ref[CHUNKS - 1]


def sweeps_kernel(par_ref, near_ref, far_ref, known_ref, gas_out, table_ref):
    odd = par_ref[0] == 1
    below = jnp.where(odd, near_ref[...], far_ref[...])
    above = jnp.where(odd, far_ref[...], near_ref[...])
    full = jnp.concatenate([below] + [known_ref[s] for s in range(CHUNKS)] + [above], axis=1)
    width = full.shape[1]
    inverse = 1.0 / full[6:7]
    pad = jnp.zeros((5, width), F32)
    gas = jnp.concatenate([full[0:3], pad], axis=0)
    known = jnp.concatenate([full[3:6], pad], axis=0)
    for sweep in range(SWEEPS):
        sides = pltpu.roll(gas, 1, 1) + pltpu.roll(gas, width - 1, 1)
        gas = (known + VISCOSITY * sides) * inverse
    gas_out[...] = gas[0:3, BP : BP + CHUNKS * BP]
    for c in range(3):
        for s in range(CHUNKS):
            table_ref[c, s : s + 1, :] = gas[c : c + 1, (s + 1) * BP : (s + 2) * BP]


def pick_kernel(par_ref, owner_ref, cell_ref, mine_ref, other_ref, out_ref):
    par = par_ref[0]
    place_of = lax.broadcasted_iota(jnp.int32, (BP, BP), 0)
    quarter = lax.broadcasted_iota(jnp.int32, (CHUNKS, BP), 0)
    pad = jnp.zeros((4, BP), F32)
    for b in range(NB):
        cell = cell_ref[b : b + 1, :]
        chunk = cell // BP
        hot = jnp.where(place_of == cell % BP, 1.0, 0.0).astype(BF16)
        owner = owner_ref[b]
        chip = owner // 2
        mine = owner % 2 == par
        rows = [jnp.where(mine, mine_ref[chip, c], other_ref[chip, c]) for c in range(3)]
        rows = jnp.concatenate(rows + [pad], axis=0)
        stacked = jnp.concatenate(parts3(rows), axis=0).astype(BF16)
        found = jnp.dot(stacked, hot, preferred_element_type=F32)
        found = found[0:16] + found[16:32] + found[32:48]
        here = quarter == chunk
        out_ref[:, b * BP : (b + 1) * BP] = jnp.concatenate(
            [
                jnp.sum(jnp.where(here, found[4 * c : 4 * c + 4], 0.0), axis=0, keepdims=True)
                for c in range(3)
            ],
            axis=0,
        )


def swap_pairs(count):
    near = [(d, d ^ 1) for d in range(count)]
    far = [(d, (d + 1) % count if d % 2 else (d - 1) % count) for d in range(count)]
    return near, far


def body(
    positions,
    velocities,
    particle_volume,
    drag_coef,
    gas_at_particle,
    pair_first,
    pair_second,
    ghost_list,
    block_owner,
    cell_map,
    gas_velocity,
):
    axes = ("grp", "dom")
    ndom = lax.axis_size("dom")
    near_pairs, far_pairs = swap_pairs(lax.axis_size("grp") * ndom)

    def exchange(near, far):
        far = lax.ppermute(far, axes, far_pairs)
        near = lax.ppermute(near, axes, near_pairs)
        return near, far

    par = (lax.axis_index("dom") & 1).astype(jnp.int32).reshape(1)
    chips = ndom // 2
    same_core = [list(range(core, ndom, 2)) for core in range(2)]
    mass = particle_volume.reshape(NB, BP)
    beta = drag_coef.reshape(NB, BP)
    cells = cell_map.reshape(NB, BP)
    owner = block_owner.reshape(NB)

    state, aux, rb, near, far, lists = prepare(
        par, ghost_list, positions, velocities, gas_at_particle, mass, beta, pair_first, pair_second
    )
    scalars = (par, ghost_list, lists, owner)
    for step in range(SUBSTEPS):
        near, far = exchange(near, far)
        part, g = local_pairs(lists, state, rb)
        last = step == SUBSTEPS - 1
        outs = ghost_pairs(last, chips, scalars, cells, state, near, far, aux, part, g)
        if not last:
            state, near, far = outs
    pos_out, vel_out, keep, give = outs

    dep = keep + lax.ppermute(give, axes, near_pairs)
    dep = lax.all_to_all(dep, "dom", 0, 0, axis_index_groups=same_core, tiled=True)

    tile = jax.ShapeDtypeStruct((8, BP), F32)
    void, known, low, high = pl.pallas_call(
        known_kernel,
        in_specs=[VMEM] * 2,
        out_shape=(
            jax.ShapeDtypeStruct((CHUNKS, BP), F32),
            jax.ShapeDtypeStruct((CHUNKS, 8, BP), F32),
            tile,
            tile,
        ),
        out_specs=(VMEM,) * 4,
        compiler_params=PARAMS,
        cost_estimate=cost(400000, 700000),
        name="known",
    )(dep, gas_velocity)
    odd = par[0] == 1
    near, far = exchange(jnp.where(odd, low, high), jnp.where(odd, high, low))
    gas, table = pl.pallas_call(
        sweeps_kernel,
        in_specs=[SMEM] + [VMEM] * 3,
        out_shape=(
            jax.ShapeDtypeStruct((3, CHUNKS * BP), F32),
            jax.ShapeDtypeStruct((3, CHUNKS, BP), F32),
        ),
        out_specs=(VMEM,) * 2,
        compiler_params=PARAMS,
        cost_estimate=cost(40000, 50000),
        name="sweeps",
    )(par, near, far, known)

    table = jnp.broadcast_to(table[None], (chips, 3, CHUNKS, BP))
    table = lax.all_to_all(table, "dom", 0, 0, axis_index_groups=same_core, tiled=True)
    other = lax.ppermute(table, axes, near_pairs)
    particle_gas = pl.pallas_call(
        pick_kernel,
        in_specs=[SMEM] * 2 + [VMEM] * 3,
        out_shape=jax.ShapeDtypeStruct((3, NB * BP), F32),
        out_specs=VMEM,
        compiler_params=PARAMS,
        cost_estimate=cost(60000000, 900000),
        name="pick",
    )(par, owner, cells, table, other)
    return (pos_out, vel_out, gas, void.reshape(-1), particle_gas)


def solution(mesh):
    both = ("grp", "dom")
    return jax.shard_map(
        body,
        mesh=mesh,
        in_specs=(
            P(None, both),
            P(None, both),
            P(both),
            P(both),
            P(None, both),
            P(both),
            P(both),
            P(None, both),
            P(both, None),
            P(both),
            P(None, both),
        ),
        out_specs=(
            P(None, both),
            P(None, both),
            P(None, both),
            P(both),
            P(None, both),
        ),
        check_vma=False,
    )
```

time: 221 us -> 178 us (0.81)
  waiting for transfers between devices: 53.6 us -> 23.5 us
  blocking collectives: 39.9 us -> 21.6 us
  Pallas kernels: 57.1 us -> 64.8 us
  local copies, waits for them, and re-layouts: 7.39 us -> 3.26 us
    all_to_all x1, waiting for transfers between devices: 41.1 us -> 19.3 us  [body(): lax.all_to_all(dep, 'dom', 0, 0, axis_index_groups=same_core, tiled=True)]
    all_to_all x1, blocking collectives: 39.9 us -> 21.6 us  [body(): lax.all_to_all(table, 'dom', 0, 0, axis_index_groups=same_core, tiled=True)]
    ppermute x5, waiting for transfers between devices: 12.5 us -> 0.01 us  [exchange(): far = lax.ppermute(far, axes, far_pairs)]
    ppermute x0 -> x2, starting transfers between devices: none -> 8.72 us  [the longest x1 5.42 us: body(): other = lax.ppermute(table, axes, near_pairs)]
    pallas_call x6 -> x10, Pallas kernels: 55.4 us -> 63.3 us  [the longest x4 41.3 us: local_pairs(): pl.pallas_call(local_kernel, in_specs=[SMEM] + [VMEM] * 2, out_shape=(jax...]
    all_to_all x1, starting transfers between devices: 17.5 us -> 9.74 us  [body(): lax.all_to_all(dep, 'dom', 0, 0, axis_index_groups=same_core, tiled=True)]
    unnamed x30 -> x22, local copies, waits for them, and re-layouts: 7.32 us -> 3.21 us
    ppermute x5, starting transfers between devices: 12.5 us -> 16.1 us  [exchange(): far = lax.ppermute(far, axes, far_pairs)]
  transfers between devices with their start and end apart: 11 -> 13, of which waited for: 6 -> 4; matrix products, arithmetic and copies ran while one was open for 0% -> 0% of each run, Pallas kernels for 0% -> 23%
where the time goes in v2:
time: 178 us; the launch traced here: 177 us
  Pallas kernels  64.8 us (36%)
  starting transfers between devices  61.8 us (35%)
  waiting for transfers between devices  23.5 us (13%)
  blocking collectives  21.6 us (12%)
  local copies, waits for them, and re-layouts  3.26 us (2%)
    pallas_call x4, Pallas kernels, local_pairs(): pl.pallas_call(local_kernel, in_specs=[SMEM] + [VMEM] * 2, out_shape=(jax...  41.3 us
    ppermute x5, starting transfers between devices, exchange(): near = lax.ppermute(near, axes, near_pairs)  27.3 us
    all_to_all x1, blocking collectives, body(): lax.all_to_all(table, 'dom', 0, 0, axis_index_groups=same_core, tiled=True)  21.6 us
    all_to_all x1, waiting for transfers between devices, body(): lax.all_to_all(dep, 'dom', 0, 0, axis_index_groups=same_core, tiled=True)  19.3 us
    ppermute x5, starting transfers between devices, exchange(): far = lax.ppermute(far, axes, far_pairs)  16.1 us
    pallas_call x4, Pallas kernels, ghost_pairs(): pl.pallas_call(functools.partial(ghost_kernel, last), in_specs=[SMEM] * 4...  15.9 us
    all_to_all x1, starting transfers between devices, body(): lax.all_to_all(dep, 'dom', 0, 0, axis_index_groups=same_core, tiled=True)  9.74 us
    ppermute x1, starting transfers between devices, body(): other = lax.ppermute(table, axes, near_pairs)  5.42 us
  transfers between devices with their start and end apart: 13, of which 4 were waited for; matrix products, arithmetic and copies ran while one was open for 0% of the time, Pallas kernels for 23%

profile of v2, /device:TPU:7, one launch (start us, length us, event | category | flops | bytes accessed | tf_op | source)
XLA Modules:
  0.0 177.0 jit_solution(2144731638985377273)
XLA Ops:
  0.6 4.4 %prepare.1 = (f32[32,8,128]{2,1,0:T(8,128)}, f32[32,8,128]{2,1,0:T(8,128)}, f32[32,128,128]{2,1,0:T(8,128)}, f32[2,8,128]{2,1,0:T(8,128)}, f32[2,8,128]{2,1,0:T(8,128)}, /*index=5*/s32[552]{0:T(1024)}) custom-call(s32[1]{0:T(128)} %bitcast.par_ref.refs_0_, s32[2,2]{1,0:T(2,128)} %refs_1_.7, f32[3,4096]{1,0:T(4,128)} %pos_hbm.1, f32[3,4096]{1,0:T(4,128)} %vel_hbm.1, ...), custom_call_target="tpu_custom_call" | custom-call | flops 100000 | bytes 3000000 | tf_op jit(solution)/shard_map/prepare/pallas_call | solution.py:116
  5.0 2.6 %collective-permute-start = (f32[2,8,128]{2,1,0:T(8,128)}, f32[2,8,128]{2,1,0:T(8,128)S(1)}, u32[]{:S(2)}, u32[]{:S(2)}) collective-permute-start(f32[2,8,128]{2,1,0:T(8,128)} %get-tuple-element.40), channel_id=1, source_target_pairs={{0,1},{1,0},{2,3},{3,2},{4,5},{5,4},{6,7},{7,6},{8,9},{9,8},{10,11... | collective-permute-start | bytes 24584 | tf_op jit(solution)/shard_map/ppermute | solution.py:464
  7.6 3.9 %collective-permute-start.1 = (f32[2,8,128]{2,1,0:T(8,128)}, f32[2,8,128]{2,1,0:T(8,128)S(1)}, u32[]{:S(2)}, u32[]{:S(2)}) collective-permute-start(f32[2,8,128]{2,1,0:T(8,128)} %get-tuple-element.41), channel_id=1, source_target_pairs={{0,511},{1,2},{2,1},{3,4},{4,3},{5,6},{6,5},{7,8},{8,7},{9,10},{10... | collective-permute-start | bytes 24584 | tf_op jit(solution)/shard_map/ppermute | solution.py:463
  11.5 0.0 copy-start.4
  11.5 1.6 copy-done.4
  13.1 0.9 copy-done.7
  14.0 0.7 copy-done.9
  14.7 0.0 copy-start.8
  14.7 10.3 %local_pairs.4 = (f32[33,8,128]{2,1,0:T(8,128)S(1)}, bf16[32,64,256]{2,1,0:T(8,128)(2,1)S(1)}) custom-call(s32[552]{0:T(1024)S(1)} %copy-done.9, f32[32,8,128]{2,1,0:T(8,128)S(1)} %copy-done.7, f32[32,128,128]{2,1,0:T(8,128)S(1)} %copy-done.4), custom_call_target="tpu_custom_call" | custom-call | flops 10000000000 | bytes 3500000 | tf_op jit(solution)/shard_map/local_pairs/pallas_call | solution.py:252
  25.0 0.0 collective-permute-done.refs_6_
  25.0 0.0 collective-permute-done.1.refs_7_
  25.0 0.0 copy-done
  25.1 0.0 copy-start.10
  25.1 2.3 %ghost_pairs.3 = (f32[32,8,128]{2,1,0:T(8,128)S(1)}, f32[2,8,128]{2,1,0:T(8,128)S(1)}, f32[2,8,128]{2,1,0:T(8,128)S(1)}) custom-call(s32[1]{0:T(128)} %bitcast.par_ref.refs_0_, s32[2,2]{1,0:T(2,128)S(1)} %copy-done.2, s32[552]{0:T(1024)S(1)} %copy-done.9, s32[32]{0:T(128)S(1)} %bitcast.11, s32[32,128]{1,0:T(8,128)S(1)} %bitcast.6, ...), custom_call_target="tpu_custom_call" | custom-call | flops 2000000000 | bytes 2000000 | tf_op jit(solution)/shard_map/ghost_pairs/pallas_call | solution.py:355
  27.4 12.9 %collective-permute-start.2 = (f32[2,8,128]{2,1,0:T(8,128)S(1)}, f32[2,8,128]{2,1,0:T(8,128)S(1)}, u32[]{:S(2)}, u32[]{:S(2)}) collective-permute-start(f32[2,8,128]{2,1,0:T(8,128)S(1)} %get-tuple-element.47), channel_id=1, source_target_pairs={{0,1},{1,0},{2,3},{3,2},{4,5},{5,4},{6,7},{7,6},{8,9},{9,8},{10,11... | collective-permute-start | bytes 24584 | tf_op jit(solution)/shard_map/ppermute | solution.py:464
  40.3 1.9 %collective-permute-start.3 = (f32[2,8,128]{2,1,0:T(8,128)S(1)}, f32[2,8,128]{2,1,0:T(8,128)S(1)}, u32[]{:S(2)}, u32[]{:S(2)}) collective-permute-start(f32[2,8,128]{2,1,0:T(8,128)S(1)} %get-tuple-element.48), channel_id=1, source_target_pairs={{0,511},{1,2},{2,1},{3,4},{4,3},{5,6},{6,5},{7,8},{8,7},{9,10},{10... | collective-permute-start | bytes 24584 | tf_op jit(solution)/shard_map/ppermute | solution.py:463
  42.3 10.3 %local_pairs.5 = (f32[33,8,128]{2,1,0:T(8,128)S(1)}, bf16[32,64,256]{2,1,0:T(8,128)(2,1)S(1)}) custom-call(s32[552]{0:T(1024)S(1)} %copy-done.10, f32[32,8,128]{2,1,0:T(8,128)S(1)} %get-tuple-element.46.state_ref.refs_5_, f32[32,128,128]{2,1,0:T(8,128)S(1)} %copy-done.5), custom_call_target="tpu_custom_call" | custom-call | flops 10000000000 | bytes 3500000 | tf_op jit(solution)/shard_map/local_pairs/pallas_call | solution.py:252
  52.6 0.0 collective-permute-done.2.refs_6_
  52.6 0.0 collective-permute-done.3.refs_7_
  52.6 2.3 %ghost_pairs.4 = (f32[32,8,128]{2,1,0:T(8,128)S(1)}, f32[2,8,128]{2,1,0:T(8,128)S(1)}, f32[2,8,128]{2,1,0:T(8,128)S(1)}) custom-call(s32[1]{0:T(128)} %bitcast.par_ref.refs_0_, s32[2,2]{1,0:T(2,128)S(1)} %copy-done.2, s32[552]{0:T(1024)S(1)} %copy-done.10, s32[32]{0:T(128)S(1)} %bitcast.12, s32[32,128]{1,0:T(8,128)S(1)} %bitcast.7, ...), custom_call_target="tpu_custom_call" | custom-call | flops 2000000000 | bytes 2000000 | tf_op jit(solution)/shard_map/ghost_pairs/pallas_call | solution.py:355
  55.0 3.2 %collective-permute-start.4 = (f32[2,8,128]{2,1,0:T(8,128)S(1)}, f32[2,8,128]{2,1,0:T(8,128)S(1)}, u32[]{:S(2)}, u32[]{:S(2)}) collective-permute-start(f32[2,8,128]{2,1,0:T(8,128)S(1)} %get-tuple-element.52), channel_id=1, source_target_pairs={{0,1},{1,0},{2,3},{3,2},{4,5},{5,4},{6,7},{7,6},{8,9},{9,8},{10,11... | collective-permute-start | bytes 24584 | tf_op jit(solution)/shard_map/ppermute | solution.py:464
  58.2 3.0 %collective-permute-start.5 = (f32[2,8,128]{2,1,0:T(8,128)S(1)}, f32[2,8,128]{2,1,0:T(8,128)S(1)}, u32[]{:S(2)}, u32[]{:S(2)}) collective-permute-start(f32[2,8,128]{2,1,0:T(8,128)S(1)} %get-tuple-element.53), channel_id=1, source_target_pairs={{0,511},{1,2},{2,1},{3,4},{4,3},{5,6},{6,5},{7,8},{8,7},{9,10},{10... | collective-permute-start | bytes 24584 | tf_op jit(solution)/shard_map/ppermute | solution.py:463
  61.2 10.3 %local_pairs.6 = (f32[33,8,128]{2,1,0:T(8,128)S(1)}, bf16[32,64,256]{2,1,0:T(8,128)(2,1)S(1)}) custom-call(s32[552]{0:T(1024)S(1)} %copy-done.10, f32[32,8,128]{2,1,0:T(8,128)S(1)} %get-tuple-element.51.state_ref.refs_5_, f32[32,128,128]{2,1,0:T(8,128)S(1)} %copy-done.5), custom_call_target="tpu_custom_call" | custom-call | flops 10000000000 | bytes 3500000 | tf_op jit(solution)/shard_map/local_pairs/pallas_call | solution.py:252
  71.5 0.0 collective-permute-done.4.refs_6_
  71.5 0.0 collective-permute-done.5.refs_7_
  71.5 2.3 %ghost_pairs.5 = (f32[32,8,128]{2,1,0:T(8,128)S(1)}, f32[2,8,128]{2,1,0:T(8,128)S(1)}, f32[2,8,128]{2,1,0:T(8,128)S(1)}) custom-call(s32[1]{0:T(128)} %bitcast.par_ref.refs_0_, s32[2,2]{1,0:T(2,128)S(1)} %copy-done.2, s32[552]{0:T(1024)S(1)} %copy-done.10, s32[32]{0:T(128)S(1)} %bitcast.13, s32[32,128]{1,0:T(8,128)S(1)} %bitcast.8, ...), custom_call_target="tpu_custom_call" | custom-call | flops 2000000000 | bytes 2000000 | tf_op jit(solution)/shard_map/ghost_pairs/pallas_call | solution.py:355
  73.9 6.8 %collective-permute-start.6 = (f32[2,8,128]{2,1,0:T(8,128)S(1)}, f32[2,8,128]{2,1,0:T(8,128)S(1)}, u32[]{:S(2)}, u32[]{:S(2)}) collective-permute-start(f32[2,8,128]{2,1,0:T(8,128)S(1)} %get-tuple-element.57), channel_id=1, source_target_pairs={{0,1},{1,0},{2,3},{3,2},{4,5},{5,4},{6,7},{7,6},{8,9},{9,8},{10,11... | collective-permute-start | bytes 24584 | tf_op jit(solution)/shard_map/ppermute | solution.py:464
  80.6 1.9 %collective-permute-start.7 = (f32[2,8,128]{2,1,0:T(8,128)S(1)}, f32[2,8,128]{2,1,0:T(8,128)S(1)}, u32[]{:S(2)}, u32[]{:S(2)}) collective-permute-start(f32[2,8,128]{2,1,0:T(8,128)S(1)} %get-tuple-element.58), channel_id=1, source_target_pairs={{0,511},{1,2},{2,1},{3,4},{4,3},{5,6},{6,5},{7,8},{8,7},{9,10},{10... | collective-permute-start | bytes 24584 | tf_op jit(solution)/shard_map/ppermute | solution.py:463
  82.5 10.3 %local_pairs.7 = (f32[33,8,128]{2,1,0:T(8,128)S(1)}, bf16[32,64,256]{2,1,0:T(8,128)(2,1)S(1)}) custom-call(s32[552]{0:T(1024)S(1)} %copy-done.10, f32[32,8,128]{2,1,0:T(8,128)S(1)} %get-tuple-element.56.state_ref.refs_5_, f32[32,128,128]{2,1,0:T(8,128)S(1)} %copy-done.5), custom_call_target="tpu_custom_call" | custom-call | flops 10000000000 | bytes 3500000 | tf_op jit(solution)/shard_map/local_pairs/pallas_call | solution.py:252
  92.9 0.0 collective-permute-done.6.refs_6_
  92.9 0.0 collective-permute-done.7.refs_7_
  92.9 8.9 %ghost_pairs_last.1 = (f32[3,4096]{1,0:T(4,128)}, f32[3,4096]{1,0:T(4,128)}, f32[64,5,4,128]{3,2,1,0:T(4,128)S(1)}, f32[64,5,4,128]{3,2,1,0:T(4,128)S(1)}) custom-call(s32[1]{0:T(128)} %bitcast.par_ref.refs_0_, s32[2,2]{1,0:T(2,128)S(1)} %copy-done.2, s32[552]{0:T(1024)S(1)} %copy-done.10, s32[32]{0:T(128)S(1)} %bitcast.14, s32[32,128]{1,0:T(8,128)S(1)} %bitcast.9, ...), custom_call_target="tpu_custom_call" | custom-call | flops 2000000000 | bytes 2000000 | tf_op jit(solution)/shard_map/ghost_pairs_last/pallas_call | solution.py:355
  101.8 3.3 %collective-permute-start.8 = (f32[64,5,4,128]{3,2,1,0:T(4,128)S(1)}, f32[64,5,4,128]{3,2,1,0:T(4,128)S(1)}, u32[]{:S(2)}, u32[]{:S(2)}) collective-permute-start(f32[64,5,4,128]{3,2,1,0:T(4,128)S(1)} %get-tuple-element.64), channel_id=1, source_target_pairs={{0,1},{1,0},{2,3},{3,2},{4,5},{5,4},{6,7},{7,6},{8,9},{9,8},{10,11... | collective-permute-start | bytes 1966088 | tf_op jit(solution)/shard_map/ppermute | solution.py:488
  105.1 1.7 collective-permute-done.8
  106.8 1.0 add.3
  107.8 9.7 %all-to-all-start = ((f32[64,5,4,128]{3,2,1,0:T(4,128)}), f32[64,5,4,128]{3,2,1,0:T(4,128)S(1)}, u32[]{:S(2)}, u32[]{:S(2)}) async-start(f32[64,5,4,128]{3,2,1,0:T(4,128)} %add.3), calls=%async_computation | async-start | bytes 1310720 | tf_op jit(solution)/shard_map/all_to_all | solution.py:489
  117.6 19.3 %all-to-all-done.dep_ref = f32[64,5,4,128]{3,2,1,0:T(4,128)S(1)} async-done(((f32[64,5,4,128]{3,2,1,0:T(4,128)}), f32[64,5,4,128]{3,2,1,0:T(4,128)S(1)}, u32[]{:S(2)}, u32[]{:S(2)}) %all-to-all-start) | async-done | bytes 655392 | tf_op jit(solution)/shard_map/all_to_all | solution.py:489
  136.9 0.7 known.1
  137.6 5.3 %collective-permute-start.10 = (f32[8,128]{1,0:T(8,128)S(1)}, f32[8,128]{1,0:T(8,128)S(1)}, u32[]{:S(2)}, u32[]{:S(2)}) collective-permute-start(f32[8,128]{1,0:T(8,128)S(1)} %get-tuple-element.71), channel_id=1, source_target_pairs={{0,511},{1,2},{2,1},{3,4},{4,3},{5,6},{6,5},{7,8},{8,7},{9,10},{10... | collective-permute-start | bytes 12296 | tf_op jit(solution)/shard_map/ppermute | solution.py:463
  142.9 1.9 %collective-permute-start.9 = (f32[8,128]{1,0:T(8,128)S(1)}, f32[8,128]{1,0:T(8,128)S(1)}, u32[]{:S(2)}, u32[]{:S(2)}) collective-permute-start(f32[8,128]{1,0:T(8,128)S(1)} %get-tuple-element.72), channel_id=1, source_target_pairs={{0,1},{1,0},{2,3},{3,2},{4,5},{5,4},{6,7},{7,6},{8,9},{9,8},{10,11... | collective-permute-start | bytes 12296 | tf_op jit(solution)/shard_map/ppermute | solution.py:464
  144.8 0.0 collective-permute-done.10.far_ref
  144.8 1.1 collective-permute-done.9.near_ref
  145.9 0.9 sweeps.1
  146.9 0.1 broadcast_in_dim.2
  146.9 21.6 %all_to_all.10.mine_ref = f32[64,3,4,128]{3,2,1,0:T(4,128)S(1)} all-to-all(f32[64,3,4,128]{3,2,1,0:T(4,128)S(1)} %broadcast_in_dim.2), channel_id=1, replica_groups={{0,2,4,6,8,10,12,14,16,18,20,22,24,26,28,30,32,34,36,38,40,42,44,46,48,..., dimensions={0} | all-to-all | bytes 786432 | tf_op jit(solution)/shard_map/all_to_all | solution.py:522
  168.5 5.4 %collective-permute-start.11 = (f32[64,3,4,128]{3,2,1,0:T(4,128)S(1)}, f32[64,3,4,128]{3,2,1,0:T(4,128)S(1)}, u32[]{:S(2)}, u32[]{:S(2)}) collective-permute-start(f32[64,3,4,128]{3,2,1,0:T(4,128)S(1)} %all_to_all.10.mine_ref), channel_id=1, source_target_pairs={{0,1},{1,0},{2,3},{3,2},{4,5},{5,4},{6,7},{7,6},{8,9},{9,8},{10,11... | collective-permute-start | bytes 1179656 | tf_op jit(solution)/shard_map/ppermute | solution.py:523
  174.0 1.3 collective-permute-done.11.other_ref
  175.3 1.7 pick.1
  (16 shorter events, 0.0 us)
Async XLA Ops:
  5.0 20.0 %collective-permute-start = (f32[2,8,128]{2,1,0:T(8,128)}, f32[2,8,128]{2,1,0:T(8,128)S(1)}, u32[]{:S(2)}, u32[]{:S(2)}) collective-permute-start(f32[2,8,128]{2,1,0:T(8,128)} %get-tuple-element.40), channel_id=1, source_target_pairs={{0,1},{1,0},{2,3},{3,2},{4,5},{5,4},{6,7},{7,6},{8,9},{9,8},{10,11... | collective-permute-start | bytes 24584 | tf_op jit(solution)/shard_map/ppermute | solution.py:464
  7.6 17.4 %collective-permute-start.1 = (f32[2,8,128]{2,1,0:T(8,128)}, f32[2,8,128]{2,1,0:T(8,128)S(1)}, u32[]{:S(2)}, u32[]{:S(2)}) collective-permute-start(f32[2,8,128]{2,1,0:T(8,128)} %get-tuple-element.41), channel_id=1, source_target_pairs={{0,511},{1,2},{2,1},{3,4},{4,3},{5,6},{6,5},{7,8},{8,7},{9,10},{10... | collective-permute-start | bytes 24584 | tf_op jit(solution)/shard_map/ppermute | solution.py:463
  11.5 1.6 copy-start.4
  13.1 0.9 copy-start.7
  14.0 0.7 copy-start.9
  14.7 10.3 %copy-start = (s32[4096]{0:T(1024)S(1)}, s32[4096]{0:T(1024)}, u32[]{:S(2)}) copy-start(s32[4096]{0:T(1024)} %param.20) | copy-start | bytes 49156
  14.7 10.3 %copy-start.2 = (s32[2,2]{1,0:T(2,128)S(1)}, s32[2,2]{1,0:T(2,128)}, u32[]{:S(2)}) copy-start(s32[2,2]{1,0:T(2,128)} %refs_1_.7) | copy-start | bytes 52
  14.7 10.4 %copy-start.3 = (s32[32,1]{0,1:T(1,128)S(1)}, s32[32,1]{0,1:T(1,128)}, u32[]{:S(2)}) copy-start(s32[32,1]{0,1:T(1,128)} %param.19) | copy-start | bytes 388
  14.7 10.4 %copy-start.6 = (f32[32,8,128]{2,1,0:T(8,128)S(1)}, f32[32,8,128]{2,1,0:T(8,128)}, u32[]{:S(2)}) copy-start(f32[32,8,128]{2,1,0:T(8,128)} %get-tuple-element.42.refs_8_) | copy-start | bytes 393220
  14.7 10.4 %copy-start.8 = (f32[32,8,128]{2,1,0:T(8,128)S(1)}, f32[32,8,128]{2,1,0:T(8,128)}, u32[]{:S(2)}) copy-start(f32[32,8,128]{2,1,0:T(8,128)} %get-tuple-element.39.state_ref.refs_5_) | copy-start | bytes 393220
  25.1 17.2 %copy-start.5 = (f32[32,128,128]{2,1,0:T(8,128)S(1)}, f32[32,128,128]{2,1,0:T(8,128)}, u32[]{:S(2)}) copy-start(f32[32,128,128]{2,1,0:T(8,128)} %get-tuple-element.43.rb_ref) | copy-start | bytes 6291460
  25.1 17.2 %copy-start.10 = (s32[552]{0:T(1024)S(1)}, s32[552]{0:T(1024)}, u32[]{:S(2)}) copy-start(s32[552]{0:T(1024)} %get-tuple-element.38.list_ref.refs_2_) | copy-start | bytes 6628
  27.4 25.2 %collective-permute-start.2 = (f32[2,8,128]{2,1,0:T(8,128)S(1)}, f32[2,8,128]{2,1,0:T(8,128)S(1)}, u32[]{:S(2)}, u32[]{:S(2)}) collective-permute-start(f32[2,8,128]{2,1,0:T(8,128)S(1)} %get-tuple-element.47), channel_id=1, source_target_pairs={{0,1},{1,0},{2,3},{3,2},{4,5},{5,4},{6,7},{7,6},{8,9},{9,8},{10,11... | collective-permute-start | bytes 24584 | tf_op jit(solution)/shard_map/ppermute | solution.py:464
  40.3 12.3 %collective-permute-start.3 = (f32[2,8,128]{2,1,0:T(8,128)S(1)}, f32[2,8,128]{2,1,0:T(8,128)S(1)}, u32[]{:S(2)}, u32[]{:S(2)}) collective-permute-start(f32[2,8,128]{2,1,0:T(8,128)S(1)} %get-tuple-element.48), channel_id=1, source_target_pairs={{0,511},{1,2},{2,1},{3,4},{4,3},{5,6},{6,5},{7,8},{8,7},{9,10},{10... | collective-permute-start | bytes 24584 | tf_op jit(solution)/shard_map/ppermute | solution.py:463
  55.0 16.5 %collective-permute-start.4 = (f32[2,8,128]{2,1,0:T(8,128)S(1)}, f32[2,8,128]{2,1,0:T(8,128)S(1)}, u32[]{:S(2)}, u32[]{:S(2)}) collective-permute-start(f32[2,8,128]{2,1,0:T(8,128)S(1)} %get-tuple-element.52), channel_id=1, source_target_pairs={{0,1},{1,0},{2,3},{3,2},{4,5},{5,4},{6,7},{7,6},{8,9},{9,8},{10,11... | collective-permute-start | bytes 24584 | tf_op jit(solution)/shard_map/ppermute | solution.py:464
  58.2 13.3 %collective-permute-start.5 = (f32[2,8,128]{2,1,0:T(8,128)S(1)}, f32[2,8,128]{2,1,0:T(8,128)S(1)}, u32[]{:S(2)}, u32[]{:S(2)}) collective-permute-start(f32[2,8,128]{2,1,0:T(8,128)S(1)} %get-tuple-element.53), channel_id=1, source_target_pairs={{0,511},{1,2},{2,1},{3,4},{4,3},{5,6},{6,5},{7,8},{8,7},{9,10},{10... | collective-permute-start | bytes 24584 | tf_op jit(solution)/shard_map/ppermute | solution.py:463
  73.9 19.0 %collective-permute-start.6 = (f32[2,8,128]{2,1,0:T(8,128)S(1)}, f32[2,8,128]{2,1,0:T(8,128)S(1)}, u32[]{:S(2)}, u32[]{:S(2)}) collective-permute-start(f32[2,8,128]{2,1,0:T(8,128)S(1)} %get-tuple-element.57), channel_id=1, source_target_pairs={{0,1},{1,0},{2,3},{3,2},{4,5},{5,4},{6,7},{7,6},{8,9},{9,8},{10,11... | collective-permute-start | bytes 24584 | tf_op jit(solution)/shard_map/ppermute | solution.py:464
  80.6 12.3 %collective-permute-start.7 = (f32[2,8,128]{2,1,0:T(8,128)S(1)}, f32[2,8,128]{2,1,0:T(8,128)S(1)}, u32[]{:S(2)}, u32[]{:S(2)}) collective-permute-start(f32[2,8,128]{2,1,0:T(8,128)S(1)} %get-tuple-element.58), channel_id=1, source_target_pairs={{0,511},{1,2},{2,1},{3,4},{4,3},{5,6},{6,5},{7,8},{8,7},{9,10},{10... | collective-permute-start | bytes 24584 | tf_op jit(solution)/shard_map/ppermute | solution.py:463
  101.8 35.1 %copy-start.1 = (f32[3,512]{1,0:T(4,128)S(1)}, f32[3,512]{1,0:T(4,128)}, u32[]{:S(2)}) copy-start(f32[3,512]{1,0:T(4,128)} %gas_ref.1) | copy-start | bytes 18436
  101.8 5.0 %collective-permute-start.8 = (f32[64,5,4,128]{3,2,1,0:T(4,128)S(1)}, f32[64,5,4,128]{3,2,1,0:T(4,128)S(1)}, u32[]{:S(2)}, u32[]{:S(2)}) collective-permute-start(f32[64,5,4,128]{3,2,1,0:T(4,128)S(1)} %get-tuple-element.64), channel_id=1, source_target_pairs={{0,1},{1,0},{2,3},{3,2},{4,5},{5,4},{6,7},{7,6},{8,9},{9,8},{10,11... | collective-permute-start | bytes 1966088 | tf_op jit(solution)/shard_map/ppermute | solution.py:488
  107.8 29.1 %all-to-all-start = ((f32[64,5,4,128]{3,2,1,0:T(4,128)}), f32[64,5,4,128]{3,2,1,0:T(4,128)S(1)}, u32[]{:S(2)}, u32[]{:S(2)}) async-start(f32[64,5,4,128]{3,2,1,0:T(4,128)} %add.3), calls=%async_computation | async-start | bytes 1310720 | tf_op jit(solution)/shard_map/all_to_all | solution.py:489
  137.6 7.3 %collective-permute-start.10 = (f32[8,128]{1,0:T(8,128)S(1)}, f32[8,128]{1,0:T(8,128)S(1)}, u32[]{:S(2)}, u32[]{:S(2)}) collective-permute-start(f32[8,128]{1,0:T(8,128)S(1)} %get-tuple-element.71), channel_id=1, source_target_pairs={{0,511},{1,2},{2,1},{3,4},{4,3},{5,6},{6,5},{7,8},{8,7},{9,10},{10... | collective-permute-start | bytes 12296 | tf_op jit(solution)/shard_map/ppermute | solution.py:463
  142.9 3.1 %collective-permute-start.9 = (f32[8,128]{1,0:T(8,128)S(1)}, f32[8,128]{1,0:T(8,128)S(1)}, u32[]{:S(2)}, u32[]{:S(2)}) collective-permute-start(f32[8,128]{1,0:T(8,128)S(1)} %get-tuple-element.72), channel_id=1, source_target_pairs={{0,1},{1,0},{2,3},{3,2},{4,5},{5,4},{6,7},{7,6},{8,9},{9,8},{10,11... | collective-permute-start | bytes 12296 | tf_op jit(solution)/shard_map/ppermute | solution.py:464
  168.5 6.8 %collective-permute-start.11 = (f32[64,3,4,128]{3,2,1,0:T(4,128)S(1)}, f32[64,3,4,128]{3,2,1,0:T(4,128)S(1)}, u32[]{:S(2)}, u32[]{:S(2)}) collective-permute-start(f32[64,3,4,128]{3,2,1,0:T(4,128)S(1)} %all_to_all.10.mine_ref), channel_id=1, source_target_pairs={{0,1},{1,0},{2,3},{3,2},{4,5},{5,4},{6,7},{7,6},{8,9},{9,8},{10,11... | collective-permute-start | bytes 1179656 | tf_op jit(solution)/shard_map/ppermute | solution.py:523

commit v3 on v2

--- a/solution.py
+++ b/solution.py
@@ -18,7 +18,7 @@
 K = 5
 CHUNKS = 4
 DEPROWS = 24
-ROOM = NPAIR + GROUP
+ROOM = NPAIR + 2 * GROUP
 LISTS = 4 * ROOM + 8
 
 SLAB = 4.0
@@ -64,7 +64,7 @@
 
 def prepare_kernel(
     par_ref, ghost_hbm, pos_hbm, vel_hbm, gas_hbm, mass_hbm, beta_hbm, first_hbm, second_hbm,
-    state_ref, aux_ref, rb_ref, near_ref, far_ref, list_ref,
+    state_ref, aux_ref, near_ref, far_ref, list_ref,
     ghost_ref, pos_ref, vel_ref, gas_ref, mass_ref, beta_ref, first_ref, second_ref, sems,
 ):
     sources = (ghost_hbm, pos_hbm, vel_hbm, gas_hbm, mass_hbm, beta_hbm, first_hbm, second_hbm)
@@ -84,24 +84,23 @@
         )
         aux_ref[b] = jnp.concatenate([zero3, gas_ref[:, lanes], beta_ref[rows], mass_ref[rows]], axis=0)
     fill_sends(par_ref, ghost_ref, state_ref, near_ref, far_ref)
-    column = jnp.transpose(radius)
-    for b in range(NB):
-        rb_ref[b] = jnp.broadcast_to(column[:, b : b + 1], (BP, BP))
 
     def sort_pair(p, counts):
         local, ghost = counts
         first = first_ref[p]
         second = second_ref[p]
         is_ghost = (second >= NB).astype(jnp.int32)
-        slot = jnp.where(is_ghost == 1, 2 * ROOM + ghost, local)
+        slot = jnp.where(is_ghost == 1, 2 * ROOM + ghost, GROUP + local)
         list_ref[slot] = first
         list_ref[ROOM + slot] = second
         return local + 1 - is_ghost, ghost + is_ghost
 
     local, ghost = lax.fori_loop(0, NPAIR, sort_pair, (jnp.int32(0), jnp.int32(0)))
     for s in range(GROUP):
-        list_ref[local + s] = NB
-        list_ref[ROOM + local + s] = 0
+        list_ref[s] = NB
+        list_ref[ROOM + s] = 0
+        list_ref[GROUP + local + s] = NB
+        list_ref[ROOM + GROUP + local + s] = 0
         list_ref[2 * ROOM + ghost + s] = NB
         list_ref[3 * ROOM + ghost + s] = NB
     list_ref[4 * ROOM] = (local + GROUP - 1) // GROUP
@@ -111,13 +110,12 @@
 def prepare(par, ghost_list, pos, vel, gas_seen, mass, beta, first, second):
     tile = jax.ShapeDtypeStruct((NB, 8, BP), F32)
     send = jax.ShapeDtypeStruct((NG, 8, BP), F32)
-    wide = jax.ShapeDtypeStruct((NB, BP, BP), F32)
     lists = jax.ShapeDtypeStruct((LISTS,), jnp.int32)
     return pl.pallas_call(
         prepare_kernel,
         in_specs=[SMEM] + [pl.BlockSpec(memory_space=pl.ANY)] * 8,
-        out_shape=(tile, tile, wide, send, send, lists),
-        out_specs=(VMEM,) * 5 + (SMEM,),
+        out_shape=(tile, tile, send, send, lists),
+        out_specs=(VMEM,) * 4 + (SMEM,),
         scratch_shapes=[
             pltpu.SMEM((2, NG), jnp.int32),
             pltpu.VMEM((3, NB * BP), F32),
@@ -130,7 +128,7 @@
             pltpu.SemaphoreType.DMA((8,)),
         ],
         compiler_params=pltpu.CompilerParams(vmem_limit_bytes=58 * 1024 * 1024),
-        cost_estimate=cost(100000, 3000000),
+        cost_estimate=cost(100000, 600000),
         name="prepare",
     )(par, ghost_list, pos, vel, gas_seen, mass, beta, first, second)
 
@@ -199,8 +197,11 @@
         g_ref[base + s] = jnp.concatenate([left, right], axis=1).astype(BF16)
 
 
-def pair_sums(a, b, state_ref, jt_ref, g_ref, a_ref, rb_ref):
-    both = jnp.dot(jt_ref[b], g_ref[a], preferred_element_type=F32)
+def pair_product(a, b, jt_ref, g_ref):
+    return jnp.dot(jt_ref[b], g_ref[a], preferred_element_type=F32)
+
+
+def pair_weights(both, a, b, state_ref, rb_ref):
     dist2 = both[:, :BP]
     slide = both[:, BP:]
     inv = lax.rsqrt(dist2)
@@ -212,7 +213,10 @@
     push_low = (push - push_high.astype(F32)).astype(BF16)
     root_high = root.astype(BF16)
     root_low = (root - root_high.astype(F32)).astype(BF16)
-    weights = jnp.concatenate([push_high, push_low, root_high, root_low], axis=0)
+    return jnp.concatenate([push_high, push_low, root_high, root_low], axis=0)
+
+
+def partner_sums(b, weights, a_ref):
     left_x = a_ref[b, :, :BP]
     left_v = a_ref[b, :, BP:]
     left = jnp.concatenate([left_x, left_x, left_v, left_v], axis=1)
@@ -220,15 +224,16 @@
     return sums[0:8] + sums[8:16] + sums[16:24]
 
 
-def all_pairs(groups, offset, partner_base, list_ref, acc_ref, state_ref, jt_ref, g_ref, a_ref, rb_ref):
+def ghost_loop(groups, list_ref, acc_ref, state_ref, jt_ref, g_ref, a_ref, rb_ref):
     def group(k, carry):
-        start = offset + k * GROUP
+        start = 2 * ROOM + k * GROUP
         firsts = [list_ref[start + s] for s in range(GROUP)]
-        seconds = [list_ref[start + ROOM + s] - partner_base for s in range(GROUP)]
-        sums = [
-            pair_sums(jnp.minimum(a, NB - 1), b, state_ref, jt_ref, g_ref, a_ref, rb_ref)
-            for a, b in zip(firsts, seconds)
-        ]
+        sums = []
+        for s in range(GROUP):
+            a = jnp.minimum(firsts[s], NB - 1)
+            b = list_ref[start + ROOM + s] - NB
+            weights = pair_weights(pair_product(a, b, jt_ref, g_ref), a, b, state_ref, rb_ref)
+            sums.append(partner_sums(b, weights, a_ref))
         for a, value in zip(firsts, sums):
             acc_ref[a] += value
         return carry
@@ -236,7 +241,37 @@
     lax.fori_loop(0, groups, group, 0)
 
 
-def local_kernel(list_ref, state_ref, rb_ref, acc_ref, g_ref, jt_ref, a_ref):
+def local_loop(groups, list_ref, acc_ref, state_ref, jt_ref, g_ref, a_ref, rb_ref, held_ref):
+    def finish(start, s):
+        a = list_ref[start + s]
+        b = list_ref[ROOM + start + s]
+        acc_ref[a] += partner_sums(b, held_ref[s], a_ref)
+
+    def group(k, carry):
+        start = k * GROUP
+        for s in range(GROUP):
+            a = jnp.minimum(list_ref[start + GROUP + s], NB - 1)
+            b = list_ref[ROOM + start + GROUP + s]
+            both = pair_product(a, b, jt_ref, g_ref)
+            finish(start, s)
+            held_ref[s] = pair_weights(both, a, b, state_ref, rb_ref)
+        return carry
+
+    held_ref[...] = jnp.zeros(held_ref.shape, BF16)
+    lax.fori_loop(0, groups, group, 0)
+    for s in range(GROUP):
+        finish(groups * GROUP, s)
+
+
+def local_kernel(opening, *refs):
+    if opening:
+        list_ref, state_ref, acc_ref, g_ref, rb_ref, jt_ref, a_ref, held_ref = refs
+        column = jnp.transpose(state_ref[:, 6, :])
+        for b in range(NB):
+            rb_ref[b] = jnp.broadcast_to(column[:, b : b + 1], (BP, BP))
+    else:
+        list_ref, state_ref, rb_ref, acc_ref, g_ref, jt_ref, a_ref, held_ref = refs
+
     def blocks(k, carry):
         tile = state_ref[pl.ds(k * 4, 4)]
         partner_side(tile, k * 4, jt_ref, a_ref)
@@ -245,30 +280,39 @@
 
     lax.fori_loop(0, NB // 4, blocks, 0)
     acc_ref[...] = jnp.zeros(acc_ref.shape, F32)
-    all_pairs(list_ref[4 * ROOM], 0, 0, list_ref, acc_ref, state_ref, jt_ref, g_ref, a_ref, rb_ref)
-
-
-def local_pairs(lists, state, rb):
-    return pl.pallas_call(
-        local_kernel,
-        in_specs=[SMEM] + [VMEM] * 2,
-        out_shape=(
-            jax.ShapeDtypeStruct((NB + 1, 8, BP), F32),
-            jax.ShapeDtypeStruct((NB, 64, 2 * BP), BF16),
-        ),
-        out_specs=(VMEM,) * 2,
-        scratch_shapes=[pltpu.VMEM((NB, BP, 64), BF16), pltpu.VMEM((NB, 32, 2 * BP), BF16)],
+    local_loop(list_ref[4 * ROOM], list_ref, acc_ref, state_ref, jt_ref, g_ref, a_ref, rb_ref, held_ref)
+
+
+def local_pairs(lists, state, rb=None):
+    opening = rb is None
+    outs = (
+        jax.ShapeDtypeStruct((NB + 1, 8, BP), F32),
+        jax.ShapeDtypeStruct((NB, 64, 2 * BP), BF16),
+    )
+    wide = (jax.ShapeDtypeStruct((NB, BP, BP), F32),)
+    args = (lists, state) if opening else (lists, state, rb)
+    outs = pl.pallas_call(
+        functools.partial(local_kernel, opening),
+        in_specs=[SMEM] + [VMEM] * (len(args) - 1),
+        out_shape=outs + (wide if opening else ()),
+        out_specs=(VMEM,) * (3 if opening else 2),
+        scratch_shapes=[
+            pltpu.VMEM((NB, BP, 64), BF16),
+            pltpu.VMEM((NB, 32, 2 * BP), BF16),
+            pltpu.VMEM((GROUP, 4 * BP, BP), BF16),
+        ],
         compiler_params=PARAMS,
         cost_estimate=cost(10000000000, 3500000, 4000000),
         name="local_pairs",
-    )(lists, state, rb)
+    )(*args)
+    return outs if opening else (*outs, rb)
 
 
 def ghost_kernel(last, *refs):
     (par_ref, ghost_ref, list_ref, owner_ref), refs = refs[:4], refs[4:]
     (cell_ref, state_ref, near_in, far_in, aux_ref, part_ref, g_ref), refs = refs[:7], refs[7:]
     if last:
-        (pos_out, vel_out, keep_ref, give_ref), scratch = refs[:4], refs[4:]
+        (pos_out, vel_out, keep_ref, give_ref), (*scratch, spread_ref) = refs[:4], refs[4:]
     else:
         (new_ref, near_out, far_out), scratch = refs[:3], refs[3:]
     ext_ref, jt_ref, a_ref, rb_ref, acc_ref = scratch
@@ -287,9 +331,7 @@
         rb_ref[b] = jnp.broadcast_to(column[:, b : b + 1], (BP, BP))
     partner_side(ext_ref[0:4], 0, jt_ref, a_ref)
     acc_ref[...] = part_ref[...]
-    all_pairs(
-        list_ref[4 * ROOM + 1], 2 * ROOM, NB, list_ref, acc_ref, state_ref, jt_ref, g_ref, a_ref, rb_ref
-    )
+    ghost_loop(list_ref[4 * ROOM + 1], list_ref, acc_ref, state_ref, jt_ref, g_ref, a_ref, rb_ref)
 
     tile = state_ref[...]
     acc = acc_ref[0:NB]
@@ -330,15 +372,16 @@
         amounts = jnp.where(quarter == chunk, amounts, 0.0)
         stacked = jnp.concatenate(list(parts3(amounts)) + [zeros], axis=0).astype(BF16)
         spread = lax.dot_general(stacked, hot, (((1,), (1,)), ((), ())), preferred_element_type=F32)
-        spread = spread[0:DEPROWS] + spread[DEPROWS : 2 * DEPROWS] + spread[2 * DEPROWS : 3 * DEPROWS]
+        spread_ref[b] = spread[0:DEPROWS] + spread[DEPROWS : 2 * DEPROWS] + spread[2 * DEPROWS : 3 * DEPROWS]
+
+    for b in range(NB):
         owner = owner_ref[b]
-        chip = owner // 2
+
+        def put(target, b=b, chip=owner // 2):
+            for q in range(K):
+                target[chip, q] += spread_ref[b, CHUNKS * q : CHUNKS * (q + 1)]
+
         mine = owner % 2 == par
-
-        def put(target, chip=chip, spread=spread):
-            for q in range(K):
-                target[chip, q] += spread[CHUNKS * q : CHUNKS * (q + 1)]
-
         pl.when(mine)(functools.partial(put, keep_ref))
         pl.when(jnp.logical_not(mine))(functools.partial(put, give_ref))
 
@@ -363,7 +406,8 @@
             pltpu.VMEM((2 * NG, 32, 2 * BP), BF16),
             pltpu.VMEM((2 * NG, BP, BP), F32),
             pltpu.VMEM((NB + 1, 8, BP), F32),
-        ],
+        ]
+        + ([pltpu.VMEM((NB, DEPROWS, BP), F32)] if last else []),
         compiler_params=PARAMS,
         cost_estimate=cost(2000000000, 2000000, 500000),
         name="ghost_pairs_last" if last else "ghost_pairs",
@@ -472,13 +516,14 @@
     cells = cell_map.reshape(NB, BP)
     owner = block_owner.reshape(NB)
 
-    state, aux, rb, near, far, lists = prepare(
+    state, aux, near, far, lists = prepare(
         par, ghost_list, positions, velocities, gas_at_particle, mass, beta, pair_first, pair_second
     )
     scalars = (par, ghost_list, lists, owner)
+    rb = None
     for step in range(SUBSTEPS):
         near, far = exchange(near, far)
-        part, g = local_pairs(lists, state, rb)
+        part, g, rb = local_pairs(lists, state, rb)
         last = step == SUBSTEPS - 1
         outs = ghost_pairs(last, chips, scalars, cells, state, near, far, aux, part, g)
         if not last:

time: 178 us -> 167 us (0.938)
  Pallas kernels: 64.8 us -> 57.4 us
  starting transfers between devices: 61.8 us -> 59.7 us
    pallas_call x4, Pallas kernels: 15.9 us -> 11.6 us  [ghost_pairs(): pl.pallas_call(functools.partial(ghost_kernel, last), in_specs=[SMEM] * 4...]
  transfers between devices with their start and end apart: 13 -> 13, of which waited for: 4 -> 4; matrix products, arithmetic and copies ran while one was open for 0% -> 0% of each run, Pallas kernels for 23% -> 24%
where the time goes in v3:
time: 167 us; the launch traced here: 166 us
  starting transfers between devices  59.7 us (36%)
  Pallas kernels  57.4 us (34%)
  waiting for transfers between devices  23.5 us (14%)
  blocking collectives  21.6 us (13%)
    pallas_call x4, Pallas kernels, local_pairs(): pl.pallas_call(functools.partial(local_kernel, opening), in_specs=[SMEM]...  39.5 us
    ppermute x5, starting transfers between devices, exchange(): near = lax.ppermute(near, axes, near_pairs)  25.9 us
    all_to_all x1, blocking collectives, body(): lax.all_to_all(table, 'dom', 0, 0, axis_index_groups=same_core, tiled=True)  21.6 us
    all_to_all x1, waiting for transfers between devices, body(): lax.all_to_all(dep, 'dom', 0, 0, axis_index_groups=same_core, tiled=True)  19.3 us
    ppermute x5, starting transfers between devices, exchange(): far = lax.ppermute(far, axes, far_pairs)  15.9 us
    pallas_call x4, Pallas kernels, ghost_pairs(): pl.pallas_call(functools.partial(ghost_kernel, last), in_specs=[SMEM] * 4...  11.6 us
    all_to_all x1, starting transfers between devices, body(): lax.all_to_all(dep, 'dom', 0, 0, axis_index_groups=same_core, tiled=True)  9.7 us
    ppermute x1, starting transfers between devices, body(): other = lax.ppermute(table, axes, near_pairs)  5.42 us
  transfers between devices with their start and end apart: 13, of which 4 were waited for; matrix products, arithmetic and copies ran while one was open for 0% of the time, Pallas kernels for 24%

profile of v3, /device:TPU:7, one launch (start us, length us, event | category | flops | bytes accessed | tf_op | source)
XLA Modules:
  0.0 165.9 jit_solution(7429065704269799009)
XLA Ops:
  0.6 2.9 %prepare.1 = (f32[32,8,128]{2,1,0:T(8,128)}, f32[32,8,128]{2,1,0:T(8,128)}, f32[2,8,128]{2,1,0:T(8,128)}, f32[2,8,128]{2,1,0:T(8,128)}, s32[584]{0:T(1024)}) custom-call(s32[1]{0:T(128)} %bitcast.par_ref.refs_0_, s32[2,2]{1,0:T(2,128)} %refs_1_.7, f32[3,4096]{1,0:T(4,128)} %pos_hbm.1, f32[3,4096]{1,0:T(4,128)} %vel_hbm.1, f32[3,4096]{1,0:T(4,128)} %gas_hbm.1, ...), custom_call_target="tpu_custom_call" | custom-call | flops 100000 | bytes 600000 | tf_op jit(solution)/shard_map/prepare/pallas_call | solution.py:114
  3.6 2.6 %collective-permute-start = (f32[2,8,128]{2,1,0:T(8,128)}, f32[2,8,128]{2,1,0:T(8,128)S(1)}, u32[]{:S(2)}, u32[]{:S(2)}) collective-permute-start(f32[2,8,128]{2,1,0:T(8,128)} %get-tuple-element.40), channel_id=1, source_target_pairs={{0,1},{1,0},{2,3},{3,2},{4,5},{5,4},{6,7},{7,6},{8,9},{9,8},{10,11... | collective-permute-start | bytes 24584 | tf_op jit(solution)/shard_map/ppermute | solution.py:508
  6.1 3.9 %collective-permute-start.1 = (f32[2,8,128]{2,1,0:T(8,128)}, f32[2,8,128]{2,1,0:T(8,128)S(1)}, u32[]{:S(2)}, u32[]{:S(2)}) collective-permute-start(f32[2,8,128]{2,1,0:T(8,128)} %get-tuple-element.41), channel_id=1, source_target_pairs={{0,511},{1,2},{2,1},{3,4},{4,3},{5,6},{6,5},{7,8},{8,7},{9,10},{10... | collective-permute-start | bytes 24584 | tf_op jit(solution)/shard_map/ppermute | solution.py:507
  10.1 0.0 copy-start.5
  10.1 0.9 copy-done.5
  11.0 0.7 copy-done.7
  11.7 10.4 %local_pairs.4 = (f32[33,8,128]{2,1,0:T(8,128)S(1)}, bf16[32,64,256]{2,1,0:T(8,128)(2,1)S(1)}, f32[32,128,128]{2,1,0:T(8,128)S(1)}) custom-call(s32[584]{0:T(1024)S(1)} %copy-done.7, f32[32,8,128]{2,1,0:T(8,128)S(1)} %copy-done.5), custom_call_target="tpu_custom_call" | custom-call | flops 10000000000 | bytes 3500000 | tf_op jit(solution)/shard_map/local_pairs/pallas_call | solution.py:294
  22.1 0.0 collective-permute-done.refs_6_
  22.1 0.0 collective-permute-done.1.refs_7_
  22.1 0.0 copy-done
  22.1 0.0 copy-done.2
  22.1 0.0 copy-done.3
  22.1 0.0 copy-start.8
  22.1 2.3 %ghost_pairs.3 = (f32[32,8,128]{2,1,0:T(8,128)S(1)}, f32[2,8,128]{2,1,0:T(8,128)S(1)}, f32[2,8,128]{2,1,0:T(8,128)S(1)}) custom-call(s32[1]{0:T(128)} %bitcast.par_ref.refs_0_, s32[2,2]{1,0:T(2,128)S(1)} %copy-done.2, s32[584]{0:T(1024)S(1)} %copy-done.7, s32[32]{0:T(128)S(1)} %bitcast.11, s32[32,128]{1,0:T(8,128)S(1)} %bitcast.6, ...), custom_call_target="tpu_custom_call" | custom-call | flops 2000000000 | bytes 2000000 | tf_op jit(solution)/shard_map/ghost_pairs/pallas_call | solution.py:398
  24.5 12.4 %collective-permute-start.2 = (f32[2,8,128]{2,1,0:T(8,128)S(1)}, f32[2,8,128]{2,1,0:T(8,128)S(1)}, u32[]{:S(2)}, u32[]{:S(2)}) collective-permute-start(f32[2,8,128]{2,1,0:T(8,128)S(1)} %get-tuple-element.46), channel_id=1, source_target_pairs={{0,1},{1,0},{2,3},{3,2},{4,5},{5,4},{6,7},{7,6},{8,9},{9,8},{10,11... | collective-permute-start | bytes 24584 | tf_op jit(solution)/shard_map/ppermute | solution.py:508
  36.8 1.9 %collective-permute-start.3 = (f32[2,8,128]{2,1,0:T(8,128)S(1)}, f32[2,8,128]{2,1,0:T(8,128)S(1)}, u32[]{:S(2)}, u32[]{:S(2)}) collective-permute-start(f32[2,8,128]{2,1,0:T(8,128)S(1)} %get-tuple-element.47), channel_id=1, source_target_pairs={{0,511},{1,2},{2,1},{3,4},{4,3},{5,6},{6,5},{7,8},{8,7},{9,10},{10... | collective-permute-start | bytes 24584 | tf_op jit(solution)/shard_map/ppermute | solution.py:507
  38.8 9.7 %local_pairs.5 = (f32[33,8,128]{2,1,0:T(8,128)S(1)}, bf16[32,64,256]{2,1,0:T(8,128)(2,1)S(1)}) custom-call(s32[584]{0:T(1024)S(1)} %copy-done.8, f32[32,8,128]{2,1,0:T(8,128)S(1)} %get-tuple-element.45.refs_1_.refs_5_, f32[32,128,128]{2,1,0:T(8,128)S(1)} %get-tuple-element.48.refs_2_), custom_call_target="tpu_custom_call" | custom-call | flops 10000000000 | bytes 3500000 | tf_op jit(solution)/shard_map/local_pairs/pallas_call | solution.py:294
  48.5 0.0 collective-permute-done.2.refs_6_
  48.5 0.0 collective-permute-done.3.refs_7_
  48.5 2.3 %ghost_pairs.4 = (f32[32,8,128]{2,1,0:T(8,128)S(1)}, f32[2,8,128]{2,1,0:T(8,128)S(1)}, f32[2,8,128]{2,1,0:T(8,128)S(1)}) custom-call(s32[1]{0:T(128)} %bitcast.par_ref.refs_0_, s32[2,2]{1,0:T(2,128)S(1)} %copy-done.2, s32[584]{0:T(1024)S(1)} %copy-done.8, s32[32]{0:T(128)S(1)} %bitcast.12, s32[32,128]{1,0:T(8,128)S(1)} %bitcast.7, ...), custom_call_target="tpu_custom_call" | custom-call | flops 2000000000 | bytes 2000000 | tf_op jit(solution)/shard_map/ghost_pairs/pallas_call | solution.py:398
  50.9 2.7 %collective-permute-start.4 = (f32[2,8,128]{2,1,0:T(8,128)S(1)}, f32[2,8,128]{2,1,0:T(8,128)S(1)}, u32[]{:S(2)}, u32[]{:S(2)}) collective-permute-start(f32[2,8,128]{2,1,0:T(8,128)S(1)} %get-tuple-element.52), channel_id=1, source_target_pairs={{0,1},{1,0},{2,3},{3,2},{4,5},{5,4},{6,7},{7,6},{8,9},{9,8},{10,11... | collective-permute-start | bytes 24584 | tf_op jit(solution)/shard_map/ppermute | solution.py:508
  53.5 2.9 %collective-permute-start.5 = (f32[2,8,128]{2,1,0:T(8,128)S(1)}, f32[2,8,128]{2,1,0:T(8,128)S(1)}, u32[]{:S(2)}, u32[]{:S(2)}) collective-permute-start(f32[2,8,128]{2,1,0:T(8,128)S(1)} %get-tuple-element.53), channel_id=1, source_target_pairs={{0,511},{1,2},{2,1},{3,4},{4,3},{5,6},{6,5},{7,8},{8,7},{9,10},{10... | collective-permute-start | bytes 24584 | tf_op jit(solution)/shard_map/ppermute | solution.py:507
  56.4 9.7 %local_pairs.6 = (f32[33,8,128]{2,1,0:T(8,128)S(1)}, bf16[32,64,256]{2,1,0:T(8,128)(2,1)S(1)}) custom-call(s32[584]{0:T(1024)S(1)} %copy-done.8, f32[32,8,128]{2,1,0:T(8,128)S(1)} %get-tuple-element.51.refs_1_.refs_5_, f32[32,128,128]{2,1,0:T(8,128)S(1)} %get-tuple-element.48.refs_2_), custom_call_target="tpu_custom_call" | custom-call | flops 10000000000 | bytes 3500000 | tf_op jit(solution)/shard_map/local_pairs/pallas_call | solution.py:294
  66.2 0.0 collective-permute-done.4.refs_6_
  66.2 0.0 collective-permute-done.5.refs_7_
  66.2 2.3 %ghost_pairs.5 = (f32[32,8,128]{2,1,0:T(8,128)S(1)}, f32[2,8,128]{2,1,0:T(8,128)S(1)}, f32[2,8,128]{2,1,0:T(8,128)S(1)}) custom-call(s32[1]{0:T(128)} %bitcast.par_ref.refs_0_, s32[2,2]{1,0:T(2,128)S(1)} %copy-done.2, s32[584]{0:T(1024)S(1)} %copy-done.8, s32[32]{0:T(128)S(1)} %bitcast.13, s32[32,128]{1,0:T(8,128)S(1)} %bitcast.8, ...), custom_call_target="tpu_custom_call" | custom-call | flops 2000000000 | bytes 2000000 | tf_op jit(solution)/shard_map/ghost_pairs/pallas_call | solution.py:398
  68.5 6.4 %collective-permute-start.6 = (f32[2,8,128]{2,1,0:T(8,128)S(1)}, f32[2,8,128]{2,1,0:T(8,128)S(1)}, u32[]{:S(2)}, u32[]{:S(2)}) collective-permute-start(f32[2,8,128]{2,1,0:T(8,128)S(1)} %get-tuple-element.57), channel_id=1, source_target_pairs={{0,1},{1,0},{2,3},{3,2},{4,5},{5,4},{6,7},{7,6},{8,9},{9,8},{10,11... | collective-permute-start | bytes 24584 | tf_op jit(solution)/shard_map/ppermute | solution.py:508
  74.9 1.9 %collective-permute-start.7 = (f32[2,8,128]{2,1,0:T(8,128)S(1)}, f32[2,8,128]{2,1,0:T(8,128)S(1)}, u32[]{:S(2)}, u32[]{:S(2)}) collective-permute-start(f32[2,8,128]{2,1,0:T(8,128)S(1)} %get-tuple-element.58), channel_id=1, source_target_pairs={{0,511},{1,2},{2,1},{3,4},{4,3},{5,6},{6,5},{7,8},{8,7},{9,10},{10... | collective-permute-start | bytes 24584 | tf_op jit(solution)/shard_map/ppermute | solution.py:507
  76.8 9.7 %local_pairs.7 = (f32[33,8,128]{2,1,0:T(8,128)S(1)}, bf16[32,64,256]{2,1,0:T(8,128)(2,1)S(1)}) custom-call(s32[584]{0:T(1024)S(1)} %copy-done.8, f32[32,8,128]{2,1,0:T(8,128)S(1)} %get-tuple-element.56.refs_1_.refs_5_, f32[32,128,128]{2,1,0:T(8,128)S(1)} %get-tuple-element.48.refs_2_), custom_call_target="tpu_custom_call" | custom-call | flops 10000000000 | bytes 3500000 | tf_op jit(solution)/shard_map/local_pairs/pallas_call | solution.py:294
  86.5 0.0 collective-permute-done.6.refs_6_
  86.6 0.0 collective-permute-done.7.refs_7_
  86.6 4.6 %ghost_pairs_last.1 = (f32[3,4096]{1,0:T(4,128)}, f32[3,4096]{1,0:T(4,128)}, f32[64,5,4,128]{3,2,1,0:T(4,128)S(1)}, f32[64,5,4,128]{3,2,1,0:T(4,128)S(1)}) custom-call(s32[1]{0:T(128)} %bitcast.par_ref.refs_0_, s32[2,2]{1,0:T(2,128)S(1)} %copy-done.2, s32[584]{0:T(1024)S(1)} %copy-done.8, s32[32]{0:T(128)S(1)} %bitcast.14, s32[32,128]{1,0:T(8,128)S(1)} %bitcast.9, ...), custom_call_target="tpu_custom_call" | custom-call | flops 2000000000 | bytes 2000000 | tf_op jit(solution)/shard_map/ghost_pairs_last/pallas_call | solution.py:398
  91.2 2.8 %collective-permute-start.8 = (f32[64,5,4,128]{3,2,1,0:T(4,128)S(1)}, f32[64,5,4,128]{3,2,1,0:T(4,128)S(1)}, u32[]{:S(2)}, u32[]{:S(2)}) collective-permute-start(f32[64,5,4,128]{3,2,1,0:T(4,128)S(1)} %get-tuple-element.64), channel_id=1, source_target_pairs={{0,1},{1,0},{2,3},{3,2},{4,5},{5,4},{6,7},{7,6},{8,9},{9,8},{10,11... | collective-permute-start | bytes 1966088 | tf_op jit(solution)/shard_map/ppermute | solution.py:533
  94.0 1.7 %collective-permute-done.8 = f32[64,5,4,128]{3,2,1,0:T(4,128)S(1)} collective-permute-done((f32[64,5,4,128]{3,2,1,0:T(4,128)S(1)}, f32[64,5,4,128]{3,2,1,0:T(4,128)S(1)}, u32[]{:S(2)}, u32[]{:S(2)}) %collective-permute-start.8) | collective-permute-done | bytes 655392 | tf_op jit(solution)/shard_map/ppermute | solution.py:533
  95.7 1.0 add.3
  96.7 9.7 %all-to-all-start = ((f32[64,5,4,128]{3,2,1,0:T(4,128)}), f32[64,5,4,128]{3,2,1,0:T(4,128)S(1)}, u32[]{:S(2)}, u32[]{:S(2)}) async-start(f32[64,5,4,128]{3,2,1,0:T(4,128)} %add.3), calls=%async_computation | async-start | bytes 1310720 | tf_op jit(solution)/shard_map/all_to_all | solution.py:534
  106.4 19.3 %all-to-all-done.dep_ref = f32[64,5,4,128]{3,2,1,0:T(4,128)S(1)} async-done(((f32[64,5,4,128]{3,2,1,0:T(4,128)}), f32[64,5,4,128]{3,2,1,0:T(4,128)S(1)}, u32[]{:S(2)}, u32[]{:S(2)}) %all-to-all-start) | async-done | bytes 655392 | tf_op jit(solution)/shard_map/all_to_all | solution.py:534
  125.8 0.7 known.1
  126.4 5.3 %collective-permute-start.10 = (f32[8,128]{1,0:T(8,128)S(1)}, f32[8,128]{1,0:T(8,128)S(1)}, u32[]{:S(2)}, u32[]{:S(2)}) collective-permute-start(f32[8,128]{1,0:T(8,128)S(1)} %get-tuple-element.71), channel_id=1, source_target_pairs={{0,511},{1,2},{2,1},{3,4},{4,3},{5,6},{6,5},{7,8},{8,7},{9,10},{10... | collective-permute-start | bytes 12296 | tf_op jit(solution)/shard_map/ppermute | solution.py:507
  131.7 1.9 %collective-permute-start.9 = (f32[8,128]{1,0:T(8,128)S(1)}, f32[8,128]{1,0:T(8,128)S(1)}, u32[]{:S(2)}, u32[]{:S(2)}) collective-permute-start(f32[8,128]{1,0:T(8,128)S(1)} %get-tuple-element.72), channel_id=1, source_target_pairs={{0,1},{1,0},{2,3},{3,2},{4,5},{5,4},{6,7},{7,6},{8,9},{9,8},{10,11... | collective-permute-start | bytes 12296 | tf_op jit(solution)/shard_map/ppermute | solution.py:508
  133.7 0.0 collective-permute-done.10.far_ref
  133.7 1.1 collective-permute-done.9.near_ref
  134.8 0.9 sweeps.1
  135.7 0.1 broadcast_in_dim.2
  135.8 21.6 %all_to_all.10.mine_ref = f32[64,3,4,128]{3,2,1,0:T(4,128)S(1)} all-to-all(f32[64,3,4,128]{3,2,1,0:T(4,128)S(1)} %broadcast_in_dim.2), channel_id=1, replica_groups={{0,2,4,6,8,10,12,14,16,18,20,22,24,26,28,30,32,34,36,38,40,42,44,46,48,..., dimensions={0} | all-to-all | bytes 786432 | tf_op jit(solution)/shard_map/all_to_all | solution.py:567
  157.4 5.4 %collective-permute-start.11 = (f32[64,3,4,128]{3,2,1,0:T(4,128)S(1)}, f32[64,3,4,128]{3,2,1,0:T(4,128)S(1)}, u32[]{:S(2)}, u32[]{:S(2)}) collective-permute-start(f32[64,3,4,128]{3,2,1,0:T(4,128)S(1)} %all_to_all.10.mine_ref), channel_id=1, source_target_pairs={{0,1},{1,0},{2,3},{3,2},{4,5},{5,4},{6,7},{7,6},{8,9},{9,8},{10,11... | collective-permute-start | bytes 1179656 | tf_op jit(solution)/shard_map/ppermute | solution.py:568
  162.8 1.3 collective-permute-done.11.other_ref
  164.2 1.7 %pick.1 = f32[3,4096]{1,0:T(4,128)} custom-call(s32[1]{0:T(128)} %bitcast.par_ref.refs_0_, s32[32]{0:T(128)S(1)} %bitcast.15, s32[32,128]{1,0:T(8,128)S(1)} %bitcast.10, f32[64,3,4,128]{3,2,1,0:T(4,128)S(1)} %all_to_all.10.mine_ref, f32[64,3,4,128]{3,2,1,0:T(4,128)S(1)} %collective-permute-done.11.other_ref), custom_call_target="tpu_custom_call" | custom-call | flops 60000000 | bytes 900000 | tf_op jit(solution)/shard_map/pick/pallas_call | solution.py:569
  (12 shorter events, 0.0 us)
Async XLA Ops:
  3.6 18.5 %collective-permute-start = (f32[2,8,128]{2,1,0:T(8,128)}, f32[2,8,128]{2,1,0:T(8,128)S(1)}, u32[]{:S(2)}, u32[]{:S(2)}) collective-permute-start(f32[2,8,128]{2,1,0:T(8,128)} %get-tuple-element.40), channel_id=1, source_target_pairs={{0,1},{1,0},{2,3},{3,2},{4,5},{5,4},{6,7},{7,6},{8,9},{9,8},{10,11... | collective-permute-start | bytes 24584 | tf_op jit(solution)/shard_map/ppermute | solution.py:508
  6.1 15.9 %collective-permute-start.1 = (f32[2,8,128]{2,1,0:T(8,128)}, f32[2,8,128]{2,1,0:T(8,128)S(1)}, u32[]{:S(2)}, u32[]{:S(2)}) collective-permute-start(f32[2,8,128]{2,1,0:T(8,128)} %get-tuple-element.41), channel_id=1, source_target_pairs={{0,511},{1,2},{2,1},{3,4},{4,3},{5,6},{6,5},{7,8},{8,7},{9,10},{10... | collective-permute-start | bytes 24584 | tf_op jit(solution)/shard_map/ppermute | solution.py:507
  10.1 0.9 copy-start.5
  11.0 0.7 copy-start.7
  11.6 10.4 %copy-start = (s32[4096]{0:T(1024)S(1)}, s32[4096]{0:T(1024)}, u32[]{:S(2)}) copy-start(s32[4096]{0:T(1024)} %param.20) | copy-start | bytes 49156
  11.6 10.4 %copy-start.2 = (s32[2,2]{1,0:T(2,128)S(1)}, s32[2,2]{1,0:T(2,128)}, u32[]{:S(2)}) copy-start(s32[2,2]{1,0:T(2,128)} %refs_1_.7) | copy-start | bytes 52
  11.7 10.5 %copy-start.3 = (s32[32,1]{0,1:T(1,128)S(1)}, s32[32,1]{0,1:T(1,128)}, u32[]{:S(2)}) copy-start(s32[32,1]{0,1:T(1,128)} %param.19) | copy-start | bytes 388
  11.7 10.5 %copy-start.4 = (f32[32,8,128]{2,1,0:T(8,128)S(1)}, f32[32,8,128]{2,1,0:T(8,128)}, u32[]{:S(2)}) copy-start(f32[32,8,128]{2,1,0:T(8,128)} %get-tuple-element.42.refs_8_) | copy-start | bytes 393220
  11.7 10.5 %copy-start.6 = (f32[32,8,128]{2,1,0:T(8,128)S(1)}, f32[32,8,128]{2,1,0:T(8,128)}, u32[]{:S(2)}) copy-start(f32[32,8,128]{2,1,0:T(8,128)} %get-tuple-element.39.refs_1_.refs_5_) | copy-start | bytes 393220
  22.1 16.6 %copy-start.8 = (s32[584]{0:T(1024)S(1)}, s32[584]{0:T(1024)}, u32[]{:S(2)}) copy-start(s32[584]{0:T(1024)} %get-tuple-element.38.refs_0_.refs_2_) | copy-start | bytes 7012
  24.5 24.0 %collective-permute-start.2 = (f32[2,8,128]{2,1,0:T(8,128)S(1)}, f32[2,8,128]{2,1,0:T(8,128)S(1)}, u32[]{:S(2)}, u32[]{:S(2)}) collective-permute-start(f32[2,8,128]{2,1,0:T(8,128)S(1)} %get-tuple-element.46), channel_id=1, source_target_pairs={{0,1},{1,0},{2,3},{3,2},{4,5},{5,4},{6,7},{7,6},{8,9},{9,8},{10,11... | collective-permute-start | bytes 24584 | tf_op jit(solution)/shard_map/ppermute | solution.py:508
  36.8 11.7 %collective-permute-start.3 = (f32[2,8,128]{2,1,0:T(8,128)S(1)}, f32[2,8,128]{2,1,0:T(8,128)S(1)}, u32[]{:S(2)}, u32[]{:S(2)}) collective-permute-start(f32[2,8,128]{2,1,0:T(8,128)S(1)} %get-tuple-element.47), channel_id=1, source_target_pairs={{0,511},{1,2},{2,1},{3,4},{4,3},{5,6},{6,5},{7,8},{8,7},{9,10},{10... | collective-permute-start | bytes 24584 | tf_op jit(solution)/shard_map/ppermute | solution.py:507
  50.9 15.3 %collective-permute-start.4 = (f32[2,8,128]{2,1,0:T(8,128)S(1)}, f32[2,8,128]{2,1,0:T(8,128)S(1)}, u32[]{:S(2)}, u32[]{:S(2)}) collective-permute-start(f32[2,8,128]{2,1,0:T(8,128)S(1)} %get-tuple-element.52), channel_id=1, source_target_pairs={{0,1},{1,0},{2,3},{3,2},{4,5},{5,4},{6,7},{7,6},{8,9},{9,8},{10,11... | collective-permute-start | bytes 24584 | tf_op jit(solution)/shard_map/ppermute | solution.py:508
  53.5 12.6 %collective-permute-start.5 = (f32[2,8,128]{2,1,0:T(8,128)S(1)}, f32[2,8,128]{2,1,0:T(8,128)S(1)}, u32[]{:S(2)}, u32[]{:S(2)}) collective-permute-start(f32[2,8,128]{2,1,0:T(8,128)S(1)} %get-tuple-element.53), channel_id=1, source_target_pairs={{0,511},{1,2},{2,1},{3,4},{4,3},{5,6},{6,5},{7,8},{8,7},{9,10},{10... | collective-permute-start | bytes 24584 | tf_op jit(solution)/shard_map/ppermute | solution.py:507
  68.5 18.0 %collective-permute-start.6 = (f32[2,8,128]{2,1,0:T(8,128)S(1)}, f32[2,8,128]{2,1,0:T(8,128)S(1)}, u32[]{:S(2)}, u32[]{:S(2)}) collective-permute-start(f32[2,8,128]{2,1,0:T(8,128)S(1)} %get-tuple-element.57), channel_id=1, source_target_pairs={{0,1},{1,0},{2,3},{3,2},{4,5},{5,4},{6,7},{7,6},{8,9},{9,8},{10,11... | collective-permute-start | bytes 24584 | tf_op jit(solution)/shard_map/ppermute | solution.py:508
  74.9 11.7 %collective-permute-start.7 = (f32[2,8,128]{2,1,0:T(8,128)S(1)}, f32[2,8,128]{2,1,0:T(8,128)S(1)}, u32[]{:S(2)}, u32[]{:S(2)}) collective-permute-start(f32[2,8,128]{2,1,0:T(8,128)S(1)} %get-tuple-element.58), channel_id=1, source_target_pairs={{0,511},{1,2},{2,1},{3,4},{4,3},{5,6},{6,5},{7,8},{8,7},{9,10},{10... | collective-permute-start | bytes 24584 | tf_op jit(solution)/shard_map/ppermute | solution.py:507
  91.2 34.6 %copy-start.1 = (f32[3,512]{1,0:T(4,128)S(1)}, f32[3,512]{1,0:T(4,128)}, u32[]{:S(2)}) copy-start(f32[3,512]{1,0:T(4,128)} %gas_ref.1) | copy-start | bytes 18436
  91.2 4.5 %collective-permute-start.8 = (f32[64,5,4,128]{3,2,1,0:T(4,128)S(1)}, f32[64,5,4,128]{3,2,1,0:T(4,128)S(1)}, u32[]{:S(2)}, u32[]{:S(2)}) collective-permute-start(f32[64,5,4,128]{3,2,1,0:T(4,128)S(1)} %get-tuple-element.64), channel_id=1, source_target_pairs={{0,1},{1,0},{2,3},{3,2},{4,5},{5,4},{6,7},{7,6},{8,9},{9,8},{10,11... | collective-permute-start | bytes 1966088 | tf_op jit(solution)/shard_map/ppermute | solution.py:533
  96.7 29.0 %all-to-all-start = ((f32[64,5,4,128]{3,2,1,0:T(4,128)}), f32[64,5,4,128]{3,2,1,0:T(4,128)S(1)}, u32[]{:S(2)}, u32[]{:S(2)}) async-start(f32[64,5,4,128]{3,2,1,0:T(4,128)} %add.3), calls=%async_computation | async-start | bytes 1310720 | tf_op jit(solution)/shard_map/all_to_all | solution.py:534
  126.4 7.3 %collective-permute-start.10 = (f32[8,128]{1,0:T(8,128)S(1)}, f32[8,128]{1,0:T(8,128)S(1)}, u32[]{:S(2)}, u32[]{:S(2)}) collective-permute-start(f32[8,128]{1,0:T(8,128)S(1)} %get-tuple-element.71), channel_id=1, source_target_pairs={{0,511},{1,2},{2,1},{3,4},{4,3},{5,6},{6,5},{7,8},{8,7},{9,10},{10... | collective-permute-start | bytes 12296 | tf_op jit(solution)/shard_map/ppermute | solution.py:507
  131.7 3.1 %collective-permute-start.9 = (f32[8,128]{1,0:T(8,128)S(1)}, f32[8,128]{1,0:T(8,128)S(1)}, u32[]{:S(2)}, u32[]{:S(2)}) collective-permute-start(f32[8,128]{1,0:T(8,128)S(1)} %get-tuple-element.72), channel_id=1, source_target_pairs={{0,1},{1,0},{2,3},{3,2},{4,5},{5,4},{6,7},{7,6},{8,9},{9,8},{10,11... | collective-permute-start | bytes 12296 | tf_op jit(solution)/shard_map/ppermute | solution.py:508
  157.4 6.8 %collective-permute-start.11 = (f32[64,3,4,128]{3,2,1,0:T(4,128)S(1)}, f32[64,3,4,128]{3,2,1,0:T(4,128)S(1)}, u32[]{:S(2)}, u32[]{:S(2)}) collective-permute-start(f32[64,3,4,128]{3,2,1,0:T(4,128)S(1)} %all_to_all.10.mine_ref), channel_id=1, source_target_pairs={{0,1},{1,0},{2,3},{3,2},{4,5},{5,4},{6,7},{7,6},{8,9},{9,8},{10,11... | collective-permute-start | bytes 1179656 | tf_op jit(solution)/shard_map/ppermute | solution.py:568

commit v4 on v3

--- a/solution.py
+++ b/solution.py
@@ -20,6 +20,7 @@
 DEPROWS = 24
 ROOM = NPAIR + 2 * GROUP
 LISTS = 4 * ROOM + 8
+PARITY, GHOST, OWNER, FIRST, SECOND = 0, 4, 8, 128, 256
 
 SLAB = 4.0
 SOFT = 0.01
@@ -55,40 +56,30 @@
     return jnp.concatenate([tile[:, 3:6], tile[:, 0:3], tile[:, 6:8]], axis=1)
 
 
-def fill_sends(par_ref, ghost_ref, state_ref, near_ref, far_ref):
-    par = par_ref[0]
+def fill_sends(int_ref, state_ref, near_ref, far_ref):
+    par = int_ref[PARITY]
     for s in range(NG):
-        near_ref[s] = state_ref[ghost_ref[par, s]]
-        far_ref[s] = state_ref[ghost_ref[1 - par, s]]
-
-
-def prepare_kernel(
-    par_ref, ghost_hbm, pos_hbm, vel_hbm, gas_hbm, mass_hbm, beta_hbm, first_hbm, second_hbm,
-    state_ref, aux_ref, near_ref, far_ref, list_ref,
-    ghost_ref, pos_ref, vel_ref, gas_ref, mass_ref, beta_ref, first_ref, second_ref, sems,
-):
-    sources = (ghost_hbm, pos_hbm, vel_hbm, gas_hbm, mass_hbm, beta_hbm, first_hbm, second_hbm)
-    targets = (ghost_ref, pos_ref, vel_ref, gas_ref, mass_ref, beta_ref, first_ref, second_ref)
-    copies = [pltpu.make_async_copy(s, t, sems.at[i]) for i, (s, t) in enumerate(zip(sources, targets))]
-    for copy in copies:
-        copy.start()
-    for copy in copies:
-        copy.wait()
-    radius = RADIUS_FACTOR * jnp.exp(jnp.log(mass_ref[...]) * (1.0 / 3.0))
+        near_ref[s] = state_ref[int_ref[GHOST + NG * par + s]]
+        far_ref[s] = state_ref[int_ref[GHOST + NG * (1 - par) + s]]
+
+
+def prepare_kernel(int_ref, in_ref, state_ref, aux_ref, near_ref, far_ref, list_ref):
+    mass = jnp.concatenate([in_ref[9:10, b * BP : (b + 1) * BP] for b in range(NB)], axis=0)
+    radius = RADIUS_FACTOR * jnp.exp(jnp.log(mass) * (1.0 / 3.0))
     zero3 = jnp.zeros((3, BP), F32)
     for b in range(NB):
         lanes = slice(b * BP, (b + 1) * BP)
         rows = slice(b, b + 1)
         state_ref[b] = jnp.concatenate(
-            [pos_ref[:, lanes], vel_ref[:, lanes], radius[rows], jnp.zeros((1, BP), F32)], axis=0
+            [in_ref[0:6, lanes], radius[rows], jnp.zeros((1, BP), F32)], axis=0
         )
-        aux_ref[b] = jnp.concatenate([zero3, gas_ref[:, lanes], beta_ref[rows], mass_ref[rows]], axis=0)
-    fill_sends(par_ref, ghost_ref, state_ref, near_ref, far_ref)
+        aux_ref[b] = jnp.concatenate([zero3, in_ref[6:9, lanes], in_ref[10:11, lanes], mass[rows]], axis=0)
+    fill_sends(int_ref, state_ref, near_ref, far_ref)
 
     def sort_pair(p, counts):
         local, ghost = counts
-        first = first_ref[p]
-        second = second_ref[p]
+        first = int_ref[FIRST + p]
+        second = int_ref[SECOND + p]
         is_ghost = (second >= NB).astype(jnp.int32)
         slot = jnp.where(is_ghost == 1, 2 * ROOM + ghost, GROUP + local)
         list_ref[slot] = first
@@ -107,30 +98,19 @@
     list_ref[4 * ROOM + 1] = (ghost + GROUP - 1) // GROUP
 
 
-def prepare(par, ghost_list, pos, vel, gas_seen, mass, beta, first, second):
+def prepare(ints, floats):
     tile = jax.ShapeDtypeStruct((NB, 8, BP), F32)
     send = jax.ShapeDtypeStruct((NG, 8, BP), F32)
     lists = jax.ShapeDtypeStruct((LISTS,), jnp.int32)
     return pl.pallas_call(
         prepare_kernel,
-        in_specs=[SMEM] + [pl.BlockSpec(memory_space=pl.ANY)] * 8,
+        in_specs=[SMEM, VMEM],
         out_shape=(tile, tile, send, send, lists),
         out_specs=(VMEM,) * 4 + (SMEM,),
-        scratch_shapes=[
-            pltpu.SMEM((2, NG), jnp.int32),
-            pltpu.VMEM((3, NB * BP), F32),
-            pltpu.VMEM((3, NB * BP), F32),
-            pltpu.VMEM((3, NB * BP), F32),
-            pltpu.VMEM((NB, BP), F32),
-            pltpu.VMEM((NB, BP), F32),
-            pltpu.SMEM((NPAIR,), jnp.int32),
-            pltpu.SMEM((NPAIR,), jnp.int32),
-            pltpu.SemaphoreType.DMA((8,)),
-        ],
-        compiler_params=pltpu.CompilerParams(vmem_limit_bytes=58 * 1024 * 1024),
+        compiler_params=PARAMS,
         cost_estimate=cost(100000, 600000),
         name="prepare",
-    )(par, ghost_list, pos, vel, gas_seen, mass, beta, first, second)
+    )(ints, floats)
 
 
 def row_index():
@@ -216,24 +196,29 @@
     return jnp.concatenate([push_high, push_low, root_high, root_low], axis=0)
 
 
-def partner_sums(b, weights, a_ref):
-    left_x = a_ref[b, :, :BP]
-    left_v = a_ref[b, :, BP:]
-    left = jnp.concatenate([left_x, left_x, left_v, left_v], axis=1)
-    sums = jnp.dot(left, weights, preferred_element_type=F32)
-    return sums[0:8] + sums[8:16] + sums[16:24]
+def partner_sums(partners, weights, a_ref):
+    lefts = []
+    for b in partners:
+        left_x = a_ref[b, :, :BP]
+        left_v = a_ref[b, :, BP:]
+        lefts.append(jnp.concatenate([left_x, left_x, left_v, left_v], axis=1))
+    sums = jnp.dot(jnp.concatenate(lefts, axis=0), jnp.concatenate(weights, axis=1), preferred_element_type=F32)
+    one, two = sums[0:32, :BP], sums[32:64, BP:]
+    return one[0:8] + one[8:16] + one[16:24], two[0:8] + two[8:16] + two[16:24]
 
 
 def ghost_loop(groups, list_ref, acc_ref, state_ref, jt_ref, g_ref, a_ref, rb_ref):
     def group(k, carry):
         start = 2 * ROOM + k * GROUP
         firsts = [list_ref[start + s] for s in range(GROUP)]
+        seconds = [list_ref[start + ROOM + s] - NB for s in range(GROUP)]
+        weights = []
+        for s in range(GROUP):
+            a, b = jnp.minimum(firsts[s], NB - 1), seconds[s]
+            weights.append(pair_weights(pair_product(a, b, jt_ref, g_ref), a, b, state_ref, rb_ref))
         sums = []
-        for s in range(GROUP):
-            a = jnp.minimum(firsts[s], NB - 1)
-            b = list_ref[start + ROOM + s] - NB
-            weights = pair_weights(pair_product(a, b, jt_ref, g_ref), a, b, state_ref, rb_ref)
-            sums.append(partner_sums(b, weights, a_ref))
+        for s in range(0, GROUP, 2):
+            sums.extend(partner_sums(seconds[s : s + 2], weights[s : s + 2], a_ref))
         for a, value in zip(firsts, sums):
             acc_ref[a] += value
         return carry
@@ -243,9 +228,10 @@
 
 def local_loop(groups, list_ref, acc_ref, state_ref, jt_ref, g_ref, a_ref, rb_ref, held_ref):
     def finish(start, s):
-        a = list_ref[start + s]
-        b = list_ref[ROOM + start + s]
-        acc_ref[a] += partner_sums(b, held_ref[s], a_ref)
+        partners = [list_ref[ROOM + start + s + t] for t in range(2)]
+        sums = partner_sums(partners, [held_ref[s], held_ref[s + 1]], a_ref)
+        for t in range(2):
+            acc_ref[list_ref[start + s + t]] += sums[t]
 
     def group(k, carry):
         start = k * GROUP
@@ -253,13 +239,14 @@
             a = jnp.minimum(list_ref[start + GROUP + s], NB - 1)
             b = list_ref[ROOM + start + GROUP + s]
             both = pair_product(a, b, jt_ref, g_ref)
-            finish(start, s)
+            if s % 2 == 0:
+                finish(start, s)
             held_ref[s] = pair_weights(both, a, b, state_ref, rb_ref)
         return carry
 
     held_ref[...] = jnp.zeros(held_ref.shape, BF16)
     lax.fori_loop(0, groups, group, 0)
-    for s in range(GROUP):
+    for s in range(0, GROUP, 2):
         finish(groups * GROUP, s)
 
 
@@ -309,14 +296,14 @@
 
 
 def ghost_kernel(last, *refs):
-    (par_ref, ghost_ref, list_ref, owner_ref), refs = refs[:4], refs[4:]
+    (int_ref, list_ref), refs = refs[:2], refs[2:]
     (cell_ref, state_ref, near_in, far_in, aux_ref, part_ref, g_ref), refs = refs[:7], refs[7:]
     if last:
         (pos_out, vel_out, keep_ref, give_ref), (*scratch, spread_ref) = refs[:4], refs[4:]
     else:
         (new_ref, near_out, far_out), scratch = refs[:3], refs[3:]
     ext_ref, jt_ref, a_ref, rb_ref, acc_ref = scratch
-    par = par_ref[0]
+    par = int_ref[PARITY]
     row = row_index()
 
     sign = 1.0 - 2.0 * par.astype(F32)
@@ -348,7 +335,7 @@
 
     if not last:
         new_ref[...] = moved
-        fill_sends(par_ref, ghost_ref, new_ref, near_out, far_out)
+        fill_sends(int_ref, new_ref, near_out, far_out)
         return
 
     for b in range(NB):
@@ -375,7 +362,7 @@
         spread_ref[b] = spread[0:DEPROWS] + spread[DEPROWS : 2 * DEPROWS] + spread[2 * DEPROWS : 3 * DEPROWS]
 
     for b in range(NB):
-        owner = owner_ref[b]
+        owner = int_ref[OWNER + b]
 
         def put(target, b=b, chip=owner // 2):
             for q in range(K):
@@ -397,7 +384,7 @@
         outs = (tile, send, send)
     return pl.pallas_call(
         functools.partial(ghost_kernel, last),
-        in_specs=[SMEM] * 4 + [VMEM] * 7,
+        in_specs=[SMEM] * 2 + [VMEM] * 7,
         out_shape=outs,
         out_specs=(VMEM,) * len(outs),
         scratch_shapes=[
@@ -434,8 +421,8 @@
     high_ref[...] = known_ref[CHUNKS - 1]
 
 
-def sweeps_kernel(par_ref, near_ref, far_ref, known_ref, gas_out, table_ref):
-    odd = par_ref[0] == 1
+def sweeps_kernel(int_ref, near_ref, far_ref, known_ref, gas_out, table_ref):
+    odd = int_ref[PARITY] == 1
     below = jnp.where(odd, near_ref[...], far_ref[...])
     above = jnp.where(odd, far_ref[...], near_ref[...])
     full = jnp.concatenate([below] + [known_ref[s] for s in range(CHUNKS)] + [above], axis=1)
@@ -453,8 +440,8 @@
             table_ref[c, s : s + 1, :] = gas[c : c + 1, (s + 1) * BP : (s + 2) * BP]
 
 
-def pick_kernel(par_ref, owner_ref, cell_ref, mine_ref, other_ref, out_ref):
-    par = par_ref[0]
+def pick_kernel(int_ref, cell_ref, mine_ref, other_ref, out_ref):
+    par = int_ref[PARITY]
     place_of = lax.broadcasted_iota(jnp.int32, (BP, BP), 0)
     quarter = lax.broadcasted_iota(jnp.int32, (CHUNKS, BP), 0)
     pad = jnp.zeros((4, BP), F32)
@@ -462,7 +449,7 @@
         cell = cell_ref[b : b + 1, :]
         chunk = cell // BP
         hot = jnp.where(place_of == cell % BP, 1.0, 0.0).astype(BF16)
-        owner = owner_ref[b]
+        owner = int_ref[OWNER + b]
         chip = owner // 2
         mine = owner % 2 == par
         rows = [jnp.where(mine, mine_ref[chip, c], other_ref[chip, c]) for c in range(3)]
@@ -511,15 +498,16 @@
     par = (lax.axis_index("dom") & 1).astype(jnp.int32).reshape(1)
     chips = ndom // 2
     same_core = [list(range(core, ndom, 2)) for core in range(2)]
-    mass = particle_volume.reshape(NB, BP)
-    beta = drag_coef.reshape(NB, BP)
     cells = cell_map.reshape(NB, BP)
-    owner = block_owner.reshape(NB)
-
-    state, aux, near, far, lists = prepare(
-        par, ghost_list, positions, velocities, gas_at_particle, mass, beta, pair_first, pair_second
+    pad = jnp.zeros((3,), jnp.int32)
+    ints = [par, pad, ghost_list.reshape(-1), block_owner.reshape(-1), jnp.zeros((FIRST - OWNER - NB,), jnp.int32)]
+    ints = jnp.concatenate(ints + [pair_first, pair_second])
+    floats = jnp.concatenate(
+        [positions, velocities, gas_at_particle, particle_volume[None], drag_coef[None]], axis=0
     )
-    scalars = (par, ghost_list, lists, owner)
+
+    state, aux, near, far, lists = prepare(ints, floats)
+    scalars = (ints, lists)
     rb = None
     for step in range(SUBSTEPS):
         near, far = exchange(near, far)
@@ -561,20 +549,20 @@
         compiler_params=PARAMS,
         cost_estimate=cost(40000, 50000),
         name="sweeps",
-    )(par, near, far, known)
+    )(ints, near, far, known)
 
     table = jnp.broadcast_to(table[None], (chips, 3, CHUNKS, BP))
     table = lax.all_to_all(table, "dom", 0, 0, axis_index_groups=same_core, tiled=True)
     other = lax.ppermute(table, axes, near_pairs)
     particle_gas = pl.pallas_call(
         pick_kernel,
-        in_specs=[SMEM] * 2 + [VMEM] * 3,
+        in_specs=[SMEM] + [VMEM] * 3,
         out_shape=jax.ShapeDtypeStruct((3, NB * BP), F32),
         out_specs=VMEM,
         compiler_params=PARAMS,
         cost_estimate=cost(60000000, 900000),
         name="pick",
-    )(par, owner, cells, table, other)
+    )(ints, cells, table, other)
     return (pos_out, vel_out, gas, void.reshape(-1), particle_gas)
 
 

time: 167 us -> 171 us (1.024)
  local copies, waits for them, and re-layouts: 1.66 us -> 4.32 us
  starting transfers between devices: 59.7 us -> 62.1 us
    concatenate x0 -> x2, local copies, waits for them, and re-layouts: none -> 3.5 us  [the longest x1 2.73 us: body(): jnp.concatenate([positions, velocities, gas_at_particle, particle_volume[...]
    pallas_call x6, Pallas kernels: 16.3 us -> 13.6 us  [the longest x4 9.41 us: ghost_pairs(): pl.pallas_call(functools.partial(ghost_kernel, last), in_specs=[SMEM] * 2...]
where the time goes in v4:
time: 171 us; the launch traced here: 170 us
  starting transfers between devices  62.1 us (36%)
  Pallas kernels  56.3 us (33%)
  waiting for transfers between devices  23.5 us (14%)
  blocking collectives  21.6 us (13%)
  local copies, waits for them, and re-layouts  4.32 us (3%)
    pallas_call x4, Pallas kernels, local_pairs(): pl.pallas_call(functools.partial(local_kernel, opening), in_specs=[SMEM]...  40.6 us
    ppermute x5, starting transfers between devices, exchange(): near = lax.ppermute(near, axes, near_pairs)  26.3 us
    all_to_all x1, blocking collectives, body(): lax.all_to_all(table, 'dom', 0, 0, axis_index_groups=same_core, tiled=True)  21.6 us
    all_to_all x1, waiting for transfers between devices, body(): lax.all_to_all(dep, 'dom', 0, 0, axis_index_groups=same_core, tiled=True)  19.3 us
    ppermute x5, starting transfers between devices, exchange(): far = lax.ppermute(far, axes, far_pairs)  15.9 us
    all_to_all x1, starting transfers between devices, body(): lax.all_to_all(dep, 'dom', 0, 0, axis_index_groups=same_core, tiled=True)  11 us
    pallas_call x4, Pallas kernels, ghost_pairs(): pl.pallas_call(functools.partial(ghost_kernel, last), in_specs=[SMEM] * 2...  9.41 us
    ppermute x1, starting transfers between devices, body(): other = lax.ppermute(table, axes, near_pairs)  5.42 us
  transfers between devices with their start and end apart: 13, of which 4 were waited for; matrix products, arithmetic and copies ran while one was open for 0% of the time, Pallas kernels for 24%

profile of v4, /device:TPU:7, one launch (start us, length us, event | category | flops | bytes accessed | tf_op | source)
XLA Modules:
  0.0 169.8 jit_solution(7346310229688280843)
XLA Ops:
  0.6 0.8 reshape.27
  1.4 2.7 %concatenate.7.in_ref = f32[11,4096]{1,0:T(8,128)S(1)} concatenate(f32[3,4096]{1,0:T(4,128)} %param.11, f32[3,4096]{1,0:T(4,128)} %param.12, f32[3,4096]{1,0:T(4,128)} %param.15, f32[1,4096]{1,0:T(1,128)} %bitcast.11, f32[1,4096]{1,0:T(1,128)} %bitcast.12), dimensions={0} | concatenate | bytes 360448 | tf_op jit(solution)/shard_map/concatenate | solution.py:505
  4.1 0.8 concatenate.6.int_ref.refs_0_
  4.9 2.4 %prepare.1 = (f32[32,8,128]{2,1,0:T(8,128)S(1)}, f32[32,8,128]{2,1,0:T(8,128)S(1)}, f32[2,8,128]{2,1,0:T(8,128)S(1)}, f32[2,8,128]{2,1,0:T(8,128)S(1)}, s32[584]{0:T(1024)S(1)}) custom-call(s32[384]{0:T(512)S(1)} %concatenate.6.int_ref.refs_0_, f32[11,4096]{1,0:T(8,128)S(1)} %concatenate.7.in_ref), custom_call_target="tpu_custom_call" | custom-call | flops 100000 | bytes 600000 | tf_op jit(solution)/shard_map/prepare/pallas_call | solution.py:105
  7.3 2.6 %collective-permute-start = (f32[2,8,128]{2,1,0:T(8,128)S(1)}, f32[2,8,128]{2,1,0:T(8,128)S(1)}, u32[]{:S(2)}, u32[]{:S(2)}) collective-permute-start(f32[2,8,128]{2,1,0:T(8,128)S(1)} %get-tuple-element.40), channel_id=1, source_target_pairs={{0,1},{1,0},{2,3},{3,2},{4,5},{5,4},{6,7},{7,6},{8,9},{9,8},{10,11... | collective-permute-start | bytes 24584 | tf_op jit(solution)/shard_map/ppermute | solution.py:495
  9.9 3.9 %collective-permute-start.1 = (f32[2,8,128]{2,1,0:T(8,128)S(1)}, f32[2,8,128]{2,1,0:T(8,128)S(1)}, u32[]{:S(2)}, u32[]{:S(2)}) collective-permute-start(f32[2,8,128]{2,1,0:T(8,128)S(1)} %get-tuple-element.41), channel_id=1, source_target_pairs={{0,511},{1,2},{2,1},{3,4},{4,3},{5,6},{6,5},{7,8},{8,7},{9,10},{10... | collective-permute-start | bytes 24584 | tf_op jit(solution)/shard_map/ppermute | solution.py:494
  13.8 0.0 copy-start
  13.9 10.7 %local_pairs.4 = (f32[33,8,128]{2,1,0:T(8,128)S(1)}, bf16[32,64,256]{2,1,0:T(8,128)(2,1)S(1)}, f32[32,128,128]{2,1,0:T(8,128)S(1)}) custom-call(s32[584]{0:T(1024)S(1)} %get-tuple-element.38.refs_0_.refs_1_, f32[32,8,128]{2,1,0:T(8,128)S(1)} %get-tuple-element.39.refs_1_.refs_3_), custom_call_target="tpu_custom_call" | custom-call | flops 10000000000 | bytes 3500000 | tf_op jit(solution)/shard_map/local_pairs/pallas_call | solution.py:281
  24.5 0.0 collective-permute-done.refs_4_
  24.5 0.0 collective-permute-done.1.refs_5_
  24.5 0.0 copy-done
  24.6 1.8 %ghost_pairs.3 = (f32[32,8,128]{2,1,0:T(8,128)S(1)}, f32[2,8,128]{2,1,0:T(8,128)S(1)}, f32[2,8,128]{2,1,0:T(8,128)S(1)}) custom-call(s32[384]{0:T(512)S(1)} %concatenate.6.int_ref.refs_0_, s32[584]{0:T(1024)S(1)} %get-tuple-element.38.refs_0_.refs_1_, s32[32,128]{1,0:T(8,128)S(1)} %bitcast.6, f32[32,8,128]{2,1,0:T(8,128)S(1)} %get-tuple-element.39.refs_1_.refs_3_, ...), custom_call_target="tpu_custom_call" | custom-call | flops 2000000000 | bytes 2000000 | tf_op jit(solution)/shard_map/ghost_pairs/pallas_call | solution.py:385
  26.3 12.3 %collective-permute-start.2 = (f32[2,8,128]{2,1,0:T(8,128)S(1)}, f32[2,8,128]{2,1,0:T(8,128)S(1)}, u32[]{:S(2)}, u32[]{:S(2)}) collective-permute-start(f32[2,8,128]{2,1,0:T(8,128)S(1)} %get-tuple-element.46), channel_id=1, source_target_pairs={{0,1},{1,0},{2,3},{3,2},{4,5},{5,4},{6,7},{7,6},{8,9},{9,8},{10,11... | collective-permute-start | bytes 24584 | tf_op jit(solution)/shard_map/ppermute | solution.py:495
  38.6 1.9 %collective-permute-start.3 = (f32[2,8,128]{2,1,0:T(8,128)S(1)}, f32[2,8,128]{2,1,0:T(8,128)S(1)}, u32[]{:S(2)}, u32[]{:S(2)}) collective-permute-start(f32[2,8,128]{2,1,0:T(8,128)S(1)} %get-tuple-element.47), channel_id=1, source_target_pairs={{0,511},{1,2},{2,1},{3,4},{4,3},{5,6},{6,5},{7,8},{8,7},{9,10},{10... | collective-permute-start | bytes 24584 | tf_op jit(solution)/shard_map/ppermute | solution.py:494
  40.5 10.0 %local_pairs.5 = (f32[33,8,128]{2,1,0:T(8,128)S(1)}, bf16[32,64,256]{2,1,0:T(8,128)(2,1)S(1)}) custom-call(s32[584]{0:T(1024)S(1)} %get-tuple-element.38.refs_0_.refs_1_, f32[32,8,128]{2,1,0:T(8,128)S(1)} %get-tuple-element.45.refs_1_.refs_3_, f32[32,128,128]{2,1,0:T(8,128)S(1)} %get-tuple-element.48.refs_2_), custom_call_target="tpu_custom_call" | custom-call | flops 10000000000 | bytes 3500000 | tf_op jit(solution)/shard_map/local_pairs/pallas_call | solution.py:281
  50.5 0.0 collective-permute-done.2.refs_4_
  50.5 0.0 collective-permute-done.3.refs_5_
  50.5 1.8 %ghost_pairs.4 = (f32[32,8,128]{2,1,0:T(8,128)S(1)}, f32[2,8,128]{2,1,0:T(8,128)S(1)}, f32[2,8,128]{2,1,0:T(8,128)S(1)}) custom-call(s32[384]{0:T(512)S(1)} %concatenate.6.int_ref.refs_0_, s32[584]{0:T(1024)S(1)} %get-tuple-element.38.refs_0_.refs_1_, s32[32,128]{1,0:T(8,128)S(1)} %bitcast.7, f32[32,8,128]{2,1,0:T(8,128)S(1)} %get-tuple-element.45.refs_1_.refs_3_, ...), custom_call_target="tpu_custom_call" | custom-call | flops 2000000000 | bytes 2000000 | tf_op jit(solution)/shard_map/ghost_pairs/pallas_call | solution.py:385
  52.3 3.4 %collective-permute-start.4 = (f32[2,8,128]{2,1,0:T(8,128)S(1)}, f32[2,8,128]{2,1,0:T(8,128)S(1)}, u32[]{:S(2)}, u32[]{:S(2)}) collective-permute-start(f32[2,8,128]{2,1,0:T(8,128)S(1)} %get-tuple-element.52), channel_id=1, source_target_pairs={{0,1},{1,0},{2,3},{3,2},{4,5},{5,4},{6,7},{7,6},{8,9},{9,8},{10,11... | collective-permute-start | bytes 24584 | tf_op jit(solution)/shard_map/ppermute | solution.py:495
  55.7 2.9 %collective-permute-start.5 = (f32[2,8,128]{2,1,0:T(8,128)S(1)}, f32[2,8,128]{2,1,0:T(8,128)S(1)}, u32[]{:S(2)}, u32[]{:S(2)}) collective-permute-start(f32[2,8,128]{2,1,0:T(8,128)S(1)} %get-tuple-element.53), channel_id=1, source_target_pairs={{0,511},{1,2},{2,1},{3,4},{4,3},{5,6},{6,5},{7,8},{8,7},{9,10},{10... | collective-permute-start | bytes 24584 | tf_op jit(solution)/shard_map/ppermute | solution.py:494
  58.6 10.0 %local_pairs.6 = (f32[33,8,128]{2,1,0:T(8,128)S(1)}, bf16[32,64,256]{2,1,0:T(8,128)(2,1)S(1)}) custom-call(s32[584]{0:T(1024)S(1)} %get-tuple-element.38.refs_0_.refs_1_, f32[32,8,128]{2,1,0:T(8,128)S(1)} %get-tuple-element.51.refs_1_.refs_3_, f32[32,128,128]{2,1,0:T(8,128)S(1)} %get-tuple-element.48.refs_2_), custom_call_target="tpu_custom_call" | custom-call | flops 10000000000 | bytes 3500000 | tf_op jit(solution)/shard_map/local_pairs/pallas_call | solution.py:281
  68.6 0.0 collective-permute-done.4.refs_4_
  68.6 0.0 collective-permute-done.5.refs_5_
  68.6 1.8 %ghost_pairs.5 = (f32[32,8,128]{2,1,0:T(8,128)S(1)}, f32[2,8,128]{2,1,0:T(8,128)S(1)}, f32[2,8,128]{2,1,0:T(8,128)S(1)}) custom-call(s32[384]{0:T(512)S(1)} %concatenate.6.int_ref.refs_0_, s32[584]{0:T(1024)S(1)} %get-tuple-element.38.refs_0_.refs_1_, s32[32,128]{1,0:T(8,128)S(1)} %bitcast.8, f32[32,8,128]{2,1,0:T(8,128)S(1)} %get-tuple-element.51.refs_1_.refs_3_, ...), custom_call_target="tpu_custom_call" | custom-call | flops 2000000000 | bytes 2000000 | tf_op jit(solution)/shard_map/ghost_pairs/pallas_call | solution.py:385
  70.4 6.1 %collective-permute-start.6 = (f32[2,8,128]{2,1,0:T(8,128)S(1)}, f32[2,8,128]{2,1,0:T(8,128)S(1)}, u32[]{:S(2)}, u32[]{:S(2)}) collective-permute-start(f32[2,8,128]{2,1,0:T(8,128)S(1)} %get-tuple-element.57), channel_id=1, source_target_pairs={{0,1},{1,0},{2,3},{3,2},{4,5},{5,4},{6,7},{7,6},{8,9},{9,8},{10,11... | collective-permute-start | bytes 24584 | tf_op jit(solution)/shard_map/ppermute | solution.py:495
  76.5 1.9 %collective-permute-start.7 = (f32[2,8,128]{2,1,0:T(8,128)S(1)}, f32[2,8,128]{2,1,0:T(8,128)S(1)}, u32[]{:S(2)}, u32[]{:S(2)}) collective-permute-start(f32[2,8,128]{2,1,0:T(8,128)S(1)} %get-tuple-element.58), channel_id=1, source_target_pairs={{0,511},{1,2},{2,1},{3,4},{4,3},{5,6},{6,5},{7,8},{8,7},{9,10},{10... | collective-permute-start | bytes 24584 | tf_op jit(solution)/shard_map/ppermute | solution.py:494
  78.4 10.0 %local_pairs.7 = (f32[33,8,128]{2,1,0:T(8,128)S(1)}, bf16[32,64,256]{2,1,0:T(8,128)(2,1)S(1)}) custom-call(s32[584]{0:T(1024)S(1)} %get-tuple-element.38.refs_0_.refs_1_, f32[32,8,128]{2,1,0:T(8,128)S(1)} %get-tuple-element.56.refs_1_.refs_3_, f32[32,128,128]{2,1,0:T(8,128)S(1)} %get-tuple-element.48.refs_2_), custom_call_target="tpu_custom_call" | custom-call | flops 10000000000 | bytes 3500000 | tf_op jit(solution)/shard_map/local_pairs/pallas_call | solution.py:281
  88.4 0.0 collective-permute-done.6.refs_4_
  88.4 0.0 collective-permute-done.7.refs_5_
  88.4 4.1 %ghost_pairs_last.1 = (f32[3,4096]{1,0:T(4,128)}, f32[3,4096]{1,0:T(4,128)}, f32[64,5,4,128]{3,2,1,0:T(4,128)S(1)}, f32[64,5,4,128]{3,2,1,0:T(4,128)S(1)}) custom-call(s32[384]{0:T(512)S(1)} %concatenate.6.int_ref.refs_0_, s32[584]{0:T(1024)S(1)} %get-tuple-element.38.refs_0_.refs_1_, s32[32,128]{1,0:T(8,128)S(1)} %bitcast.9, ...), custom_call_target="tpu_custom_call" | custom-call | flops 2000000000 | bytes 2000000 | tf_op jit(solution)/shard_map/ghost_pairs_last/pallas_call | solution.py:385
  92.5 0.0 copy-start.1
  92.5 3.5 %collective-permute-start.8 = (f32[64,5,4,128]{3,2,1,0:T(4,128)S(1)}, f32[64,5,4,128]{3,2,1,0:T(4,128)S(1)}, u32[]{:S(2)}, u32[]{:S(2)}) collective-permute-start(f32[64,5,4,128]{3,2,1,0:T(4,128)S(1)} %get-tuple-element.64), channel_id=1, source_target_pairs={{0,1},{1,0},{2,3},{3,2},{4,5},{5,4},{6,7},{7,6},{8,9},{9,8},{10,11... | collective-permute-start | bytes 1966088 | tf_op jit(solution)/shard_map/ppermute | solution.py:521
  96.0 1.7 %collective-permute-done.8 = f32[64,5,4,128]{3,2,1,0:T(4,128)S(1)} collective-permute-done((f32[64,5,4,128]{3,2,1,0:T(4,128)S(1)}, f32[64,5,4,128]{3,2,1,0:T(4,128)S(1)}, u32[]{:S(2)}, u32[]{:S(2)}) %collective-permute-start.8) | collective-permute-done | bytes 655392 | tf_op jit(solution)/shard_map/ppermute | solution.py:521
  97.7 1.0 add.3
  98.7 11.0 %all-to-all-start = ((f32[64,5,4,128]{3,2,1,0:T(4,128)}), f32[64,5,4,128]{3,2,1,0:T(4,128)S(1)}, u32[]{:S(2)}, u32[]{:S(2)}) async-start(f32[64,5,4,128]{3,2,1,0:T(4,128)} %add.3), calls=%async_computation | async-start | bytes 1310720 | tf_op jit(solution)/shard_map/all_to_all | solution.py:522
  109.7 19.3 %all-to-all-done.dep_ref = f32[64,5,4,128]{3,2,1,0:T(4,128)S(1)} async-done(((f32[64,5,4,128]{3,2,1,0:T(4,128)}), f32[64,5,4,128]{3,2,1,0:T(4,128)S(1)}, u32[]{:S(2)}, u32[]{:S(2)}) %all-to-all-start) | async-done | bytes 655392 | tf_op jit(solution)/shard_map/all_to_all | solution.py:522
  129.1 0.0 copy-done.1
  129.1 0.7 known.1
  129.7 5.3 %collective-permute-start.10 = (f32[8,128]{1,0:T(8,128)S(1)}, f32[8,128]{1,0:T(8,128)S(1)}, u32[]{:S(2)}, u32[]{:S(2)}) collective-permute-start(f32[8,128]{1,0:T(8,128)S(1)} %get-tuple-element.71), channel_id=1, source_target_pairs={{0,511},{1,2},{2,1},{3,4},{4,3},{5,6},{6,5},{7,8},{8,7},{9,10},{10... | collective-permute-start | bytes 12296 | tf_op jit(solution)/shard_map/ppermute | solution.py:494
  135.0 1.9 %collective-permute-start.9 = (f32[8,128]{1,0:T(8,128)S(1)}, f32[8,128]{1,0:T(8,128)S(1)}, u32[]{:S(2)}, u32[]{:S(2)}) collective-permute-start(f32[8,128]{1,0:T(8,128)S(1)} %get-tuple-element.72), channel_id=1, source_target_pairs={{0,1},{1,0},{2,3},{3,2},{4,5},{5,4},{6,7},{7,6},{8,9},{9,8},{10,11... | collective-permute-start | bytes 12296 | tf_op jit(solution)/shard_map/ppermute | solution.py:495
  137.0 0.0 collective-permute-done.10.far_ref
  137.0 1.1 collective-permute-done.9.near_ref
  138.1 1.5 sweeps.1
  139.6 0.1 broadcast_in_dim.18
  139.6 21.6 %all_to_all.10.mine_ref = f32[64,3,4,128]{3,2,1,0:T(4,128)S(1)} all-to-all(f32[64,3,4,128]{3,2,1,0:T(4,128)S(1)} %broadcast_in_dim.18), channel_id=1, replica_groups={{0,2,4,6,8,10,12,14,16,18,20,22,24,26,28,30,32,34,36,38,40,42,44,46,48,..., dimensions={0} | all-to-all | bytes 786432 | tf_op jit(solution)/shard_map/all_to_all | solution.py:555
  161.3 5.4 %collective-permute-start.11 = (f32[64,3,4,128]{3,2,1,0:T(4,128)S(1)}, f32[64,3,4,128]{3,2,1,0:T(4,128)S(1)}, u32[]{:S(2)}, u32[]{:S(2)}) collective-permute-start(f32[64,3,4,128]{3,2,1,0:T(4,128)S(1)} %all_to_all.10.mine_ref), channel_id=1, source_target_pairs={{0,1},{1,0},{2,3},{3,2},{4,5},{5,4},{6,7},{7,6},{8,9},{9,8},{10,11... | collective-permute-start | bytes 1179656 | tf_op jit(solution)/shard_map/ppermute | solution.py:556
  166.7 1.3 collective-permute-done.11.other_ref
  168.0 1.7 %pick.1 = f32[3,4096]{1,0:T(4,128)} custom-call(s32[384]{0:T(512)S(1)} %concatenate.6.int_ref.refs_0_, s32[32,128]{1,0:T(8,128)S(1)} %bitcast.10, f32[64,3,4,128]{3,2,1,0:T(4,128)S(1)} %all_to_all.10.mine_ref, f32[64,3,4,128]{3,2,1,0:T(4,128)S(1)} %collective-permute-done.11.other_ref), custom_call_target="tpu_custom_call" | custom-call | flops 60000000 | bytes 900000 | tf_op jit(solution)/shard_map/pick/pallas_call | solution.py:557
  (3 shorter events, 0.0 us)
Async XLA Ops:
  7.3 17.2 %collective-permute-start = (f32[2,8,128]{2,1,0:T(8,128)S(1)}, f32[2,8,128]{2,1,0:T(8,128)S(1)}, u32[]{:S(2)}, u32[]{:S(2)}) collective-permute-start(f32[2,8,128]{2,1,0:T(8,128)S(1)} %get-tuple-element.40), channel_id=1, source_target_pairs={{0,1},{1,0},{2,3},{3,2},{4,5},{5,4},{6,7},{7,6},{8,9},{9,8},{10,11... | collective-permute-start | bytes 24584 | tf_op jit(solution)/shard_map/ppermute | solution.py:495
  9.9 14.6 %collective-permute-start.1 = (f32[2,8,128]{2,1,0:T(8,128)S(1)}, f32[2,8,128]{2,1,0:T(8,128)S(1)}, u32[]{:S(2)}, u32[]{:S(2)}) collective-permute-start(f32[2,8,128]{2,1,0:T(8,128)S(1)} %get-tuple-element.41), channel_id=1, source_target_pairs={{0,511},{1,2},{2,1},{3,4},{4,3},{5,6},{6,5},{7,8},{8,7},{9,10},{10... | collective-permute-start | bytes 24584 | tf_op jit(solution)/shard_map/ppermute | solution.py:494
  13.8 10.7 %copy-start = (s32[4096]{0:T(1024)S(1)}, s32[4096]{0:T(1024)}, u32[]{:S(2)}) copy-start(s32[4096]{0:T(1024)} %param.20) | copy-start | bytes 49156
  26.3 24.2 %collective-permute-start.2 = (f32[2,8,128]{2,1,0:T(8,128)S(1)}, f32[2,8,128]{2,1,0:T(8,128)S(1)}, u32[]{:S(2)}, u32[]{:S(2)}) collective-permute-start(f32[2,8,128]{2,1,0:T(8,128)S(1)} %get-tuple-element.46), channel_id=1, source_target_pairs={{0,1},{1,0},{2,3},{3,2},{4,5},{5,4},{6,7},{7,6},{8,9},{9,8},{10,11... | collective-permute-start | bytes 24584 | tf_op jit(solution)/shard_map/ppermute | solution.py:495
  38.6 11.9 %collective-permute-start.3 = (f32[2,8,128]{2,1,0:T(8,128)S(1)}, f32[2,8,128]{2,1,0:T(8,128)S(1)}, u32[]{:S(2)}, u32[]{:S(2)}) collective-permute-start(f32[2,8,128]{2,1,0:T(8,128)S(1)} %get-tuple-element.47), channel_id=1, source_target_pairs={{0,511},{1,2},{2,1},{3,4},{4,3},{5,6},{6,5},{7,8},{8,7},{9,10},{10... | collective-permute-start | bytes 24584 | tf_op jit(solution)/shard_map/ppermute | solution.py:494
  52.3 16.2 %collective-permute-start.4 = (f32[2,8,128]{2,1,0:T(8,128)S(1)}, f32[2,8,128]{2,1,0:T(8,128)S(1)}, u32[]{:S(2)}, u32[]{:S(2)}) collective-permute-start(f32[2,8,128]{2,1,0:T(8,128)S(1)} %get-tuple-element.52), channel_id=1, source_target_pairs={{0,1},{1,0},{2,3},{3,2},{4,5},{5,4},{6,7},{7,6},{8,9},{9,8},{10,11... | collective-permute-start | bytes 24584 | tf_op jit(solution)/shard_map/ppermute | solution.py:495
  55.7 12.9 %collective-permute-start.5 = (f32[2,8,128]{2,1,0:T(8,128)S(1)}, f32[2,8,128]{2,1,0:T(8,128)S(1)}, u32[]{:S(2)}, u32[]{:S(2)}) collective-permute-start(f32[2,8,128]{2,1,0:T(8,128)S(1)} %get-tuple-element.53), channel_id=1, source_target_pairs={{0,511},{1,2},{2,1},{3,4},{4,3},{5,6},{6,5},{7,8},{8,7},{9,10},{10... | collective-permute-start | bytes 24584 | tf_op jit(solution)/shard_map/ppermute | solution.py:494
  70.4 18.1 %collective-permute-start.6 = (f32[2,8,128]{2,1,0:T(8,128)S(1)}, f32[2,8,128]{2,1,0:T(8,128)S(1)}, u32[]{:S(2)}, u32[]{:S(2)}) collective-permute-start(f32[2,8,128]{2,1,0:T(8,128)S(1)} %get-tuple-element.57), channel_id=1, source_target_pairs={{0,1},{1,0},{2,3},{3,2},{4,5},{5,4},{6,7},{7,6},{8,9},{9,8},{10,11... | collective-permute-start | bytes 24584 | tf_op jit(solution)/shard_map/ppermute | solution.py:495
  76.5 11.9 %collective-permute-start.7 = (f32[2,8,128]{2,1,0:T(8,128)S(1)}, f32[2,8,128]{2,1,0:T(8,128)S(1)}, u32[]{:S(2)}, u32[]{:S(2)}) collective-permute-start(f32[2,8,128]{2,1,0:T(8,128)S(1)} %get-tuple-element.58), channel_id=1, source_target_pairs={{0,511},{1,2},{2,1},{3,4},{4,3},{5,6},{6,5},{7,8},{8,7},{9,10},{10... | collective-permute-start | bytes 24584 | tf_op jit(solution)/shard_map/ppermute | solution.py:494
  92.5 36.5 %copy-start.1 = (f32[3,512]{1,0:T(4,128)S(1)}, f32[3,512]{1,0:T(4,128)}, u32[]{:S(2)}) copy-start(f32[3,512]{1,0:T(4,128)} %gas_ref.1) | copy-start | bytes 18436
  92.5 5.2 %collective-permute-start.8 = (f32[64,5,4,128]{3,2,1,0:T(4,128)S(1)}, f32[64,5,4,128]{3,2,1,0:T(4,128)S(1)}, u32[]{:S(2)}, u32[]{:S(2)}) collective-permute-start(f32[64,5,4,128]{3,2,1,0:T(4,128)S(1)} %get-tuple-element.64), channel_id=1, source_target_pairs={{0,1},{1,0},{2,3},{3,2},{4,5},{5,4},{6,7},{7,6},{8,9},{9,8},{10,11... | collective-permute-start | bytes 1966088 | tf_op jit(solution)/shard_map/ppermute | solution.py:521
  98.7 30.3 %all-to-all-start = ((f32[64,5,4,128]{3,2,1,0:T(4,128)}), f32[64,5,4,128]{3,2,1,0:T(4,128)S(1)}, u32[]{:S(2)}, u32[]{:S(2)}) async-start(f32[64,5,4,128]{3,2,1,0:T(4,128)} %add.3), calls=%async_computation | async-start | bytes 1310720 | tf_op jit(solution)/shard_map/all_to_all | solution.py:522
  129.7 7.3 %collective-permute-start.10 = (f32[8,128]{1,0:T(8,128)S(1)}, f32[8,128]{1,0:T(8,128)S(1)}, u32[]{:S(2)}, u32[]{:S(2)}) collective-permute-start(f32[8,128]{1,0:T(8,128)S(1)} %get-tuple-element.71), channel_id=1, source_target_pairs={{0,511},{1,2},{2,1},{3,4},{4,3},{5,6},{6,5},{7,8},{8,7},{9,10},{10... | collective-permute-start | bytes 12296 | tf_op jit(solution)/shard_map/ppermute | solution.py:494
  135.0 3.1 %collective-permute-start.9 = (f32[8,128]{1,0:T(8,128)S(1)}, f32[8,128]{1,0:T(8,128)S(1)}, u32[]{:S(2)}, u32[]{:S(2)}) collective-permute-start(f32[8,128]{1,0:T(8,128)S(1)} %get-tuple-element.72), channel_id=1, source_target_pairs={{0,1},{1,0},{2,3},{3,2},{4,5},{5,4},{6,7},{7,6},{8,9},{9,8},{10,11... | collective-permute-start | bytes 12296 | tf_op jit(solution)/shard_map/ppermute | solution.py:495
  161.3 6.8 %collective-permute-start.11 = (f32[64,3,4,128]{3,2,1,0:T(4,128)S(1)}, f32[64,3,4,128]{3,2,1,0:T(4,128)S(1)}, u32[]{:S(2)}, u32[]{:S(2)}) collective-permute-start(f32[64,3,4,128]{3,2,1,0:T(4,128)S(1)} %all_to_all.10.mine_ref), channel_id=1, source_target_pairs={{0,1},{1,0},{2,3},{3,2},{4,5},{5,4},{6,7},{7,6},{8,9},{9,8},{10,11... | collective-permute-start | bytes 1179656 | tf_op jit(solution)/shard_map/ppermute | solution.py:556

commit v5 on v3

--- a/solution.py
+++ b/solution.py
@@ -18,7 +18,8 @@
 K = 5
 CHUNKS = 4
 DEPROWS = 24
-ROOM = NPAIR + 2 * GROUP
+ROOM = NPAIR + 3 * GROUP
+STRIP = 32
 LISTS = 4 * ROOM + 8
 
 SLAB = 4.0
@@ -101,6 +102,8 @@
         list_ref[ROOM + s] = 0
         list_ref[GROUP + local + s] = NB
         list_ref[ROOM + GROUP + local + s] = 0
+        list_ref[2 * GROUP + local + s] = NB
+        list_ref[ROOM + 2 * GROUP + local + s] = 0
         list_ref[2 * ROOM + ghost + s] = NB
         list_ref[3 * ROOM + ghost + s] = NB
     list_ref[4 * ROOM] = (local + GROUP - 1) // GROUP
@@ -201,76 +204,92 @@
     return jnp.dot(jt_ref[b], g_ref[a], preferred_element_type=F32)
 
 
-def pair_weights(both, a, b, state_ref, rb_ref):
-    dist2 = both[:, :BP]
-    slide = both[:, BP:]
-    inv = lax.rsqrt(dist2)
-    overlap = (rb_ref[b] + state_ref[a, 6:7, :]) - dist2 * inv
-    delta = jnp.maximum(overlap, 0.0)
-    root = delta * lax.rsqrt(jnp.maximum(overlap, TINY))
-    push = (root * inv) * (delta - slide * inv)
-    push_high = push.astype(BF16)
-    push_low = (push - push_high.astype(F32)).astype(BF16)
-    root_high = root.astype(BF16)
-    root_low = (root - root_high.astype(F32)).astype(BF16)
-    return jnp.concatenate([push_high, push_low, root_high, root_low], axis=0)
-
-
-def partner_sums(b, weights, a_ref):
+def pair_weights(s, a, b, state_ref, rb_ref, product_ref, held_ref):
+    radius = state_ref[a, 6:7, :]
+    for c in range(0, BP, STRIP):
+        rows = slice(c, c + STRIP)
+        dist2 = product_ref[s, rows, :BP]
+        slide = product_ref[s, rows, BP:]
+        inv = lax.rsqrt(dist2)
+        overlap = (rb_ref[b, rows, :] + radius) - dist2 * inv
+        delta = jnp.maximum(overlap, 0.0)
+        root = delta * lax.rsqrt(jnp.maximum(overlap, TINY))
+        push = (root * inv) * (delta - slide * inv)
+        push_high = push.astype(BF16)
+        root_high = root.astype(BF16)
+        held_ref[s, c : c + STRIP] = push_high
+        held_ref[s, BP + c : BP + c + STRIP] = (push - push_high.astype(F32)).astype(BF16)
+        held_ref[s, 2 * BP + c : 2 * BP + c + STRIP] = root_high
+        held_ref[s, 3 * BP + c : 3 * BP + c + STRIP] = (root - root_high.astype(F32)).astype(BF16)
+
+
+def partner_sums(s, a, b, a_ref, held_ref, acc_ref):
     left_x = a_ref[b, :, :BP]
     left_v = a_ref[b, :, BP:]
     left = jnp.concatenate([left_x, left_x, left_v, left_v], axis=1)
-    sums = jnp.dot(left, weights, preferred_element_type=F32)
-    return sums[0:8] + sums[8:16] + sums[16:24]
-
-
-def ghost_loop(groups, list_ref, acc_ref, state_ref, jt_ref, g_ref, a_ref, rb_ref):
+    sums = jnp.dot(left, held_ref[s], preferred_element_type=F32)
+    acc_ref[a] += sums[0:8] + sums[8:16] + sums[16:24]
+
+
+def ghost_loop(groups, list_ref, acc_ref, state_ref, jt_ref, g_ref, a_ref, rb_ref, product_ref, held_ref):
     def group(k, carry):
         start = 2 * ROOM + k * GROUP
         firsts = [list_ref[start + s] for s in range(GROUP)]
-        sums = []
+        owns = [jnp.minimum(a, NB - 1) for a in firsts]
+        seconds = [list_ref[start + ROOM + s] - NB for s in range(GROUP)]
         for s in range(GROUP):
-            a = jnp.minimum(firsts[s], NB - 1)
-            b = list_ref[start + ROOM + s] - NB
-            weights = pair_weights(pair_product(a, b, jt_ref, g_ref), a, b, state_ref, rb_ref)
-            sums.append(partner_sums(b, weights, a_ref))
-        for a, value in zip(firsts, sums):
-            acc_ref[a] += value
+            product_ref[s] = pair_product(owns[s], seconds[s], jt_ref, g_ref)
+        for s in range(GROUP):
+            pair_weights(s, owns[s], seconds[s], state_ref, rb_ref, product_ref, held_ref)
+        for s in range(GROUP):
+            partner_sums(s, firsts[s], seconds[s], a_ref, held_ref, acc_ref)
         return carry
 
     lax.fori_loop(0, groups, group, 0)
 
 
-def local_loop(groups, list_ref, acc_ref, state_ref, jt_ref, g_ref, a_ref, rb_ref, held_ref):
-    def finish(start, s):
-        a = list_ref[start + s]
-        b = list_ref[ROOM + start + s]
-        acc_ref[a] += partner_sums(b, held_ref[s], a_ref)
+def local_loop(groups, list_ref, acc_ref, state_ref, jt_ref, g_ref, a_ref, rb_ref, product_ref, held_ref):
+    def pair(entry):
+        return list_ref[entry], list_ref[ROOM + entry]
+
+    def product(entry, s):
+        a, b = pair(entry + s)
+        product_ref[s] = pair_product(jnp.minimum(a, NB - 1), b, jt_ref, g_ref)
+
+    def weights(entry, s):
+        a, b = pair(entry + s)
+        pair_weights(s, jnp.minimum(a, NB - 1), b, state_ref, rb_ref, product_ref, held_ref)
+
+    def sums(entry, s):
+        a, b = pair(entry + s)
+        partner_sums(s, a, b, a_ref, held_ref, acc_ref)
 
     def group(k, carry):
         start = k * GROUP
         for s in range(GROUP):
-            a = jnp.minimum(list_ref[start + GROUP + s], NB - 1)
-            b = list_ref[ROOM + start + GROUP + s]
-            both = pair_product(a, b, jt_ref, g_ref)
-            finish(start, s)
-            held_ref[s] = pair_weights(both, a, b, state_ref, rb_ref)
+            sums(start, s)
+            weights(start + GROUP, s)
+            product(start + 2 * GROUP, s)
         return carry
 
     held_ref[...] = jnp.zeros(held_ref.shape, BF16)
+    for s in range(GROUP):
+        product(GROUP, s)
     lax.fori_loop(0, groups, group, 0)
     for s in range(GROUP):
-        finish(groups * GROUP, s)
+        sums(groups * GROUP, s)
 
 
 def local_kernel(opening, *refs):
     if opening:
-        list_ref, state_ref, acc_ref, g_ref, rb_ref, jt_ref, a_ref, held_ref = refs
+        list_ref, state_ref, acc_ref, g_ref, rb_ref, *scratch = refs
         column = jnp.transpose(state_ref[:, 6, :])
         for b in range(NB):
             rb_ref[b] = jnp.broadcast_to(column[:, b : b + 1], (BP, BP))
     else:
-        list_ref, state_ref, rb_ref, acc_ref, g_ref, jt_ref, a_ref, held_ref = refs
+        list_ref, state_ref, rb_ref, acc_ref, g_ref, *scratch = refs
+
+    jt_ref, a_ref, product_ref, held_ref = scratch
 
     def blocks(k, carry):
         tile = state_ref[pl.ds(k * 4, 4)]
@@ -280,7 +299,9 @@
 
     lax.fori_loop(0, NB // 4, blocks, 0)
     acc_ref[...] = jnp.zeros(acc_ref.shape, F32)
-    local_loop(list_ref[4 * ROOM], list_ref, acc_ref, state_ref, jt_ref, g_ref, a_ref, rb_ref, held_ref)
+    local_loop(
+        list_ref[4 * ROOM], list_ref, acc_ref, state_ref, jt_ref, g_ref, a_ref, rb_ref, product_ref, held_ref
+    )
 
 
 def local_pairs(lists, state, rb=None):
@@ -299,6 +320,7 @@
         scratch_shapes=[
             pltpu.VMEM((NB, BP, 64), BF16),
             pltpu.VMEM((NB, 32, 2 * BP), BF16),
+            pltpu.VMEM((GROUP, BP, 2 * BP), F32),
             pltpu.VMEM((GROUP, 4 * BP, BP), BF16),
         ],
         compiler_params=PARAMS,
@@ -315,7 +337,7 @@
         (pos_out, vel_out, keep_ref, give_ref), (*scratch, spread_ref) = refs[:4], refs[4:]
     else:
         (new_ref, near_out, far_out), scratch = refs[:3], refs[3:]
-    ext_ref, jt_ref, a_ref, rb_ref, acc_ref = scratch
+    ext_ref, jt_ref, a_ref, rb_ref, acc_ref, product_ref, held_ref = scratch
     par = par_ref[0]
     row = row_index()
 
@@ -331,7 +353,9 @@
         rb_ref[b] = jnp.broadcast_to(column[:, b : b + 1], (BP, BP))
     partner_side(ext_ref[0:4], 0, jt_ref, a_ref)
     acc_ref[...] = part_ref[...]
-    ghost_loop(list_ref[4 * ROOM + 1], list_ref, acc_ref, state_ref, jt_ref, g_ref, a_ref, rb_ref)
+    ghost_loop(
+        list_ref[4 * ROOM + 1], list_ref, acc_ref, state_ref, jt_ref, g_ref, a_ref, rb_ref, product_ref, held_ref
+    )
 
     tile = state_ref[...]
     acc = acc_ref[0:NB]
@@ -406,6 +430,8 @@
             pltpu.VMEM((2 * NG, 32, 2 * BP), BF16),
             pltpu.VMEM((2 * NG, BP, BP), F32),
             pltpu.VMEM((NB + 1, 8, BP), F32),
+            pltpu.VMEM((GROUP, BP, 2 * BP), F32),
+            pltpu.VMEM((GROUP, 4 * BP, BP), BF16),
         ]
         + ([pltpu.VMEM((NB, DEPROWS, BP), F32)] if last else []),
         compiler_params=PARAMS,

time: 167 us -> 168 us (level)
  no operation moved by 1% of the time
where the time goes in v5:
time: 168 us; the launch traced here: 167 us
  starting transfers between devices  59.8 us (36%)
  Pallas kernels  58.9 us (35%)
  waiting for transfers between devices  23.5 us (14%)
  blocking collectives  21.6 us (13%)
    pallas_call x4, Pallas kernels, local_pairs(): pl.pallas_call(functools.partial(local_kernel, opening), in_specs=[SMEM]...  40 us
    ppermute x5, starting transfers between devices, exchange(): near = lax.ppermute(near, axes, near_pairs)  25.7 us
    all_to_all x1, blocking collectives, body(): lax.all_to_all(table, 'dom', 0, 0, axis_index_groups=same_core, tiled=True)  21.6 us
    all_to_all x1, waiting for transfers between devices, body(): lax.all_to_all(dep, 'dom', 0, 0, axis_index_groups=same_core, tiled=True)  19.3 us
    ppermute x5, starting transfers between devices, exchange(): far = lax.ppermute(far, axes, far_pairs)  15.8 us
    pallas_call x4, Pallas kernels, ghost_pairs(): pl.pallas_call(functools.partial(ghost_kernel, last), in_specs=[SMEM] * 4...  12.6 us
    all_to_all x1, starting transfers between devices, body(): lax.all_to_all(dep, 'dom', 0, 0, axis_index_groups=same_core, tiled=True)  9.96 us
    ppermute x1, starting transfers between devices, body(): other = lax.ppermute(table, axes, near_pairs)  5.42 us
  transfers between devices with their start and end apart: 13, of which 4 were waited for; matrix products, arithmetic and copies ran while one was open for 0% of the time, Pallas kernels for 24%

profile of v5, /device:TPU:7, one launch (start us, length us, event | category | flops | bytes accessed | tf_op | source)
XLA Modules:
  0.0 167.4 jit_solution(8618068592031235742)
XLA Ops:
  0.6 2.9 %prepare.1 = (f32[32,8,128]{2,1,0:T(8,128)}, f32[32,8,128]{2,1,0:T(8,128)}, f32[2,8,128]{2,1,0:T(8,128)}, f32[2,8,128]{2,1,0:T(8,128)}, s32[616]{0:T(1024)}) custom-call(s32[1]{0:T(128)} %bitcast.par_ref.refs_0_, s32[2,2]{1,0:T(2,128)} %refs_1_.7, f32[3,4096]{1,0:T(4,128)} %pos_hbm.1, f32[3,4096]{1,0:T(4,128)} %vel_hbm.1, f32[3,4096]{1,0:T(4,128)} %gas_hbm.1, ...), custom_call_target="tpu_custom_call" | custom-call | flops 100000 | bytes 600000 | tf_op jit(solution)/shard_map/prepare/pallas_call | solution.py:117
  3.6 2.6 %collective-permute-start = (f32[2,8,128]{2,1,0:T(8,128)}, f32[2,8,128]{2,1,0:T(8,128)S(1)}, u32[]{:S(2)}, u32[]{:S(2)}) collective-permute-start(f32[2,8,128]{2,1,0:T(8,128)} %get-tuple-element.40), channel_id=1, source_target_pairs={{0,1},{1,0},{2,3},{3,2},{4,5},{5,4},{6,7},{7,6},{8,9},{9,8},{10,11... | collective-permute-start | bytes 24584 | tf_op jit(solution)/shard_map/ppermute | solution.py:534
  6.1 3.9 %collective-permute-start.1 = (f32[2,8,128]{2,1,0:T(8,128)}, f32[2,8,128]{2,1,0:T(8,128)S(1)}, u32[]{:S(2)}, u32[]{:S(2)}) collective-permute-start(f32[2,8,128]{2,1,0:T(8,128)} %get-tuple-element.41), channel_id=1, source_target_pairs={{0,511},{1,2},{2,1},{3,4},{4,3},{5,6},{6,5},{7,8},{8,7},{9,10},{10... | collective-permute-start | bytes 24584 | tf_op jit(solution)/shard_map/ppermute | solution.py:533
  10.1 0.0 copy-start.5
  10.1 0.9 copy-done.5
  11.0 0.7 copy-done.7
  11.7 0.0 copy-start.6
  11.7 10.6 %local_pairs.4 = (f32[33,8,128]{2,1,0:T(8,128)S(1)}, bf16[32,64,256]{2,1,0:T(8,128)(2,1)S(1)}, f32[32,128,128]{2,1,0:T(8,128)S(1)}) custom-call(s32[616]{0:T(1024)S(1)} %copy-done.7, f32[32,8,128]{2,1,0:T(8,128)S(1)} %copy-done.5), custom_call_target="tpu_custom_call" | custom-call | flops 10000000000 | bytes 3500000 | tf_op jit(solution)/shard_map/local_pairs/pallas_call | solution.py:315
  22.3 0.0 collective-permute-done.refs_6_
  22.3 0.0 collective-permute-done.1.refs_7_
  22.3 0.0 copy-done
  22.3 0.0 copy-start.8
  22.3 2.6 %ghost_pairs.3 = (f32[32,8,128]{2,1,0:T(8,128)S(1)}, f32[2,8,128]{2,1,0:T(8,128)S(1)}, f32[2,8,128]{2,1,0:T(8,128)S(1)}) custom-call(s32[1]{0:T(128)} %bitcast.par_ref.refs_0_, s32[2,2]{1,0:T(2,128)S(1)} %copy-done.2, s32[616]{0:T(1024)S(1)} %copy-done.7, s32[32]{0:T(128)S(1)} %bitcast.11, s32[32,128]{1,0:T(8,128)S(1)} %bitcast.6, ...), custom_call_target="tpu_custom_call" | custom-call | flops 2000000000 | bytes 2000000 | tf_op jit(solution)/shard_map/ghost_pairs/pallas_call | solution.py:422
  24.9 12.3 %collective-permute-start.2 = (f32[2,8,128]{2,1,0:T(8,128)S(1)}, f32[2,8,128]{2,1,0:T(8,128)S(1)}, u32[]{:S(2)}, u32[]{:S(2)}) collective-permute-start(f32[2,8,128]{2,1,0:T(8,128)S(1)} %get-tuple-element.46), channel_id=1, source_target_pairs={{0,1},{1,0},{2,3},{3,2},{4,5},{5,4},{6,7},{7,6},{8,9},{9,8},{10,11... | collective-permute-start | bytes 24584 | tf_op jit(solution)/shard_map/ppermute | solution.py:534
  37.2 1.9 %collective-permute-start.3 = (f32[2,8,128]{2,1,0:T(8,128)S(1)}, f32[2,8,128]{2,1,0:T(8,128)S(1)}, u32[]{:S(2)}, u32[]{:S(2)}) collective-permute-start(f32[2,8,128]{2,1,0:T(8,128)S(1)} %get-tuple-element.47), channel_id=1, source_target_pairs={{0,511},{1,2},{2,1},{3,4},{4,3},{5,6},{6,5},{7,8},{8,7},{9,10},{10... | collective-permute-start | bytes 24584 | tf_op jit(solution)/shard_map/ppermute | solution.py:533
  39.1 9.8 %local_pairs.5 = (f32[33,8,128]{2,1,0:T(8,128)S(1)}, bf16[32,64,256]{2,1,0:T(8,128)(2,1)S(1)}) custom-call(s32[616]{0:T(1024)S(1)} %copy-done.8, f32[32,8,128]{2,1,0:T(8,128)S(1)} %get-tuple-element.45.refs_1_.refs_5_, f32[32,128,128]{2,1,0:T(8,128)S(1)} %get-tuple-element.48.refs_2_), custom_call_target="tpu_custom_call" | custom-call | flops 10000000000 | bytes 3500000 | tf_op jit(solution)/shard_map/local_pairs/pallas_call | solution.py:315
  48.9 0.0 collective-permute-done.2.refs_6_
  49.0 0.0 collective-permute-done.3.refs_7_
  49.0 2.6 %ghost_pairs.4 = (f32[32,8,128]{2,1,0:T(8,128)S(1)}, f32[2,8,128]{2,1,0:T(8,128)S(1)}, f32[2,8,128]{2,1,0:T(8,128)S(1)}) custom-call(s32[1]{0:T(128)} %bitcast.par_ref.refs_0_, s32[2,2]{1,0:T(2,128)S(1)} %copy-done.2, s32[616]{0:T(1024)S(1)} %copy-done.8, s32[32]{0:T(128)S(1)} %bitcast.12, s32[32,128]{1,0:T(8,128)S(1)} %bitcast.7, ...), custom_call_target="tpu_custom_call" | custom-call | flops 2000000000 | bytes 2000000 | tf_op jit(solution)/shard_map/ghost_pairs/pallas_call | solution.py:422
  51.5 2.8 %collective-permute-start.4 = (f32[2,8,128]{2,1,0:T(8,128)S(1)}, f32[2,8,128]{2,1,0:T(8,128)S(1)}, u32[]{:S(2)}, u32[]{:S(2)}) collective-permute-start(f32[2,8,128]{2,1,0:T(8,128)S(1)} %get-tuple-element.52), channel_id=1, source_target_pairs={{0,1},{1,0},{2,3},{3,2},{4,5},{5,4},{6,7},{7,6},{8,9},{9,8},{10,11... | collective-permute-start | bytes 24584 | tf_op jit(solution)/shard_map/ppermute | solution.py:534
  54.3 2.8 %collective-permute-start.5 = (f32[2,8,128]{2,1,0:T(8,128)S(1)}, f32[2,8,128]{2,1,0:T(8,128)S(1)}, u32[]{:S(2)}, u32[]{:S(2)}) collective-permute-start(f32[2,8,128]{2,1,0:T(8,128)S(1)} %get-tuple-element.53), channel_id=1, source_target_pairs={{0,511},{1,2},{2,1},{3,4},{4,3},{5,6},{6,5},{7,8},{8,7},{9,10},{10... | collective-permute-start | bytes 24584 | tf_op jit(solution)/shard_map/ppermute | solution.py:533
  57.1 9.8 %local_pairs.6 = (f32[33,8,128]{2,1,0:T(8,128)S(1)}, bf16[32,64,256]{2,1,0:T(8,128)(2,1)S(1)}) custom-call(s32[616]{0:T(1024)S(1)} %copy-done.8, f32[32,8,128]{2,1,0:T(8,128)S(1)} %get-tuple-element.51.refs_1_.refs_5_, f32[32,128,128]{2,1,0:T(8,128)S(1)} %get-tuple-element.48.refs_2_), custom_call_target="tpu_custom_call" | custom-call | flops 10000000000 | bytes 3500000 | tf_op jit(solution)/shard_map/local_pairs/pallas_call | solution.py:315
  66.9 0.0 collective-permute-done.4.refs_6_
  67.0 0.0 collective-permute-done.5.refs_7_
  67.0 2.6 %ghost_pairs.5 = (f32[32,8,128]{2,1,0:T(8,128)S(1)}, f32[2,8,128]{2,1,0:T(8,128)S(1)}, f32[2,8,128]{2,1,0:T(8,128)S(1)}) custom-call(s32[1]{0:T(128)} %bitcast.par_ref.refs_0_, s32[2,2]{1,0:T(2,128)S(1)} %copy-done.2, s32[616]{0:T(1024)S(1)} %copy-done.8, s32[32]{0:T(128)S(1)} %bitcast.13, s32[32,128]{1,0:T(8,128)S(1)} %bitcast.8, ...), custom_call_target="tpu_custom_call" | custom-call | flops 2000000000 | bytes 2000000 | tf_op jit(solution)/shard_map/ghost_pairs/pallas_call | solution.py:422
  69.6 6.1 %collective-permute-start.6 = (f32[2,8,128]{2,1,0:T(8,128)S(1)}, f32[2,8,128]{2,1,0:T(8,128)S(1)}, u32[]{:S(2)}, u32[]{:S(2)}) collective-permute-start(f32[2,8,128]{2,1,0:T(8,128)S(1)} %get-tuple-element.57), channel_id=1, source_target_pairs={{0,1},{1,0},{2,3},{3,2},{4,5},{5,4},{6,7},{7,6},{8,9},{9,8},{10,11... | collective-permute-start | bytes 24584 | tf_op jit(solution)/shard_map/ppermute | solution.py:534
  75.7 1.9 %collective-permute-start.7 = (f32[2,8,128]{2,1,0:T(8,128)S(1)}, f32[2,8,128]{2,1,0:T(8,128)S(1)}, u32[]{:S(2)}, u32[]{:S(2)}) collective-permute-start(f32[2,8,128]{2,1,0:T(8,128)S(1)} %get-tuple-element.58), channel_id=1, source_target_pairs={{0,511},{1,2},{2,1},{3,4},{4,3},{5,6},{6,5},{7,8},{8,7},{9,10},{10... | collective-permute-start | bytes 24584 | tf_op jit(solution)/shard_map/ppermute | solution.py:533
  77.6 9.8 %local_pairs.7 = (f32[33,8,128]{2,1,0:T(8,128)S(1)}, bf16[32,64,256]{2,1,0:T(8,128)(2,1)S(1)}) custom-call(s32[616]{0:T(1024)S(1)} %copy-done.8, f32[32,8,128]{2,1,0:T(8,128)S(1)} %get-tuple-element.56.refs_1_.refs_5_, f32[32,128,128]{2,1,0:T(8,128)S(1)} %get-tuple-element.48.refs_2_), custom_call_target="tpu_custom_call" | custom-call | flops 10000000000 | bytes 3500000 | tf_op jit(solution)/shard_map/local_pairs/pallas_call | solution.py:315
  87.5 0.0 collective-permute-done.6.refs_6_
  87.5 0.0 collective-permute-done.7.refs_7_
  87.5 4.9 %ghost_pairs_last.1 = (f32[3,4096]{1,0:T(4,128)}, f32[3,4096]{1,0:T(4,128)}, f32[64,5,4,128]{3,2,1,0:T(4,128)S(1)}, f32[64,5,4,128]{3,2,1,0:T(4,128)S(1)}) custom-call(s32[1]{0:T(128)} %bitcast.par_ref.refs_0_, s32[2,2]{1,0:T(2,128)S(1)} %copy-done.2, s32[616]{0:T(1024)S(1)} %copy-done.8, s32[32]{0:T(128)S(1)} %bitcast.14, s32[32,128]{1,0:T(8,128)S(1)} %bitcast.9, ...), custom_call_target="tpu_custom_call" | custom-call | flops 2000000000 | bytes 2000000 | tf_op jit(solution)/shard_map/ghost_pairs_last/pallas_call | solution.py:422
  92.4 2.9 %collective-permute-start.8 = (f32[64,5,4,128]{3,2,1,0:T(4,128)S(1)}, f32[64,5,4,128]{3,2,1,0:T(4,128)S(1)}, u32[]{:S(2)}, u32[]{:S(2)}) collective-permute-start(f32[64,5,4,128]{3,2,1,0:T(4,128)S(1)} %get-tuple-element.64), channel_id=1, source_target_pairs={{0,1},{1,0},{2,3},{3,2},{4,5},{5,4},{6,7},{7,6},{8,9},{9,8},{10,11... | collective-permute-start | bytes 1966088 | tf_op jit(solution)/shard_map/ppermute | solution.py:559
  95.3 1.7 %collective-permute-done.8 = f32[64,5,4,128]{3,2,1,0:T(4,128)S(1)} collective-permute-done((f32[64,5,4,128]{3,2,1,0:T(4,128)S(1)}, f32[64,5,4,128]{3,2,1,0:T(4,128)S(1)}, u32[]{:S(2)}, u32[]{:S(2)}) %collective-permute-start.8) | collective-permute-done | bytes 655392 | tf_op jit(solution)/shard_map/ppermute | solution.py:559
  97.0 1.0 add.3
  98.0 10.0 %all-to-all-start = ((f32[64,5,4,128]{3,2,1,0:T(4,128)}), f32[64,5,4,128]{3,2,1,0:T(4,128)S(1)}, u32[]{:S(2)}, u32[]{:S(2)}) async-start(f32[64,5,4,128]{3,2,1,0:T(4,128)} %add.3), calls=%async_computation | async-start | bytes 1310720 | tf_op jit(solution)/shard_map/all_to_all | solution.py:560
  108.0 19.3 %all-to-all-done.dep_ref = f32[64,5,4,128]{3,2,1,0:T(4,128)S(1)} async-done(((f32[64,5,4,128]{3,2,1,0:T(4,128)}), f32[64,5,4,128]{3,2,1,0:T(4,128)S(1)}, u32[]{:S(2)}, u32[]{:S(2)}) %all-to-all-start) | async-done | bytes 655392 | tf_op jit(solution)/shard_map/all_to_all | solution.py:560
  127.3 0.0 copy-done.1
  127.3 0.7 known.1
  128.0 5.3 %collective-permute-start.10 = (f32[8,128]{1,0:T(8,128)S(1)}, f32[8,128]{1,0:T(8,128)S(1)}, u32[]{:S(2)}, u32[]{:S(2)}) collective-permute-start(f32[8,128]{1,0:T(8,128)S(1)} %get-tuple-element.71), channel_id=1, source_target_pairs={{0,511},{1,2},{2,1},{3,4},{4,3},{5,6},{6,5},{7,8},{8,7},{9,10},{10... | collective-permute-start | bytes 12296 | tf_op jit(solution)/shard_map/ppermute | solution.py:533
  133.3 1.9 %collective-permute-start.9 = (f32[8,128]{1,0:T(8,128)S(1)}, f32[8,128]{1,0:T(8,128)S(1)}, u32[]{:S(2)}, u32[]{:S(2)}) collective-permute-start(f32[8,128]{1,0:T(8,128)S(1)} %get-tuple-element.72), channel_id=1, source_target_pairs={{0,1},{1,0},{2,3},{3,2},{4,5},{5,4},{6,7},{7,6},{8,9},{9,8},{10,11... | collective-permute-start | bytes 12296 | tf_op jit(solution)/shard_map/ppermute | solution.py:534
  135.2 0.0 collective-permute-done.10.far_ref
  135.2 1.1 collective-permute-done.9.near_ref
  136.3 0.9 sweeps.1
  137.3 0.1 broadcast_in_dim.2
  137.3 21.6 %all_to_all.10.mine_ref = f32[64,3,4,128]{3,2,1,0:T(4,128)S(1)} all-to-all(f32[64,3,4,128]{3,2,1,0:T(4,128)S(1)} %broadcast_in_dim.2), channel_id=1, replica_groups={{0,2,4,6,8,10,12,14,16,18,20,22,24,26,28,30,32,34,36,38,40,42,44,46,48,..., dimensions={0} | all-to-all | bytes 786432 | tf_op jit(solution)/shard_map/all_to_all | solution.py:593
  159.0 5.4 %collective-permute-start.11 = (f32[64,3,4,128]{3,2,1,0:T(4,128)S(1)}, f32[64,3,4,128]{3,2,1,0:T(4,128)S(1)}, u32[]{:S(2)}, u32[]{:S(2)}) collective-permute-start(f32[64,3,4,128]{3,2,1,0:T(4,128)S(1)} %all_to_all.10.mine_ref), channel_id=1, source_target_pairs={{0,1},{1,0},{2,3},{3,2},{4,5},{5,4},{6,7},{7,6},{8,9},{9,8},{10,11... | collective-permute-start | bytes 1179656 | tf_op jit(solution)/shard_map/ppermute | solution.py:594
  164.4 1.3 collective-permute-done.11.other_ref
  165.7 1.7 %pick.1 = f32[3,4096]{1,0:T(4,128)} custom-call(s32[1]{0:T(128)} %bitcast.par_ref.refs_0_, s32[32]{0:T(128)S(1)} %bitcast.15, s32[32,128]{1,0:T(8,128)S(1)} %bitcast.10, f32[64,3,4,128]{3,2,1,0:T(4,128)S(1)} %all_to_all.10.mine_ref, f32[64,3,4,128]{3,2,1,0:T(4,128)S(1)} %collective-permute-done.11.other_ref), custom_call_target="tpu_custom_call" | custom-call | flops 60000000 | bytes 900000 | tf_op jit(solution)/shard_map/pick/pallas_call | solution.py:595
  (12 shorter events, 0.0 us)
Async XLA Ops:
  3.6 18.7 %collective-permute-start = (f32[2,8,128]{2,1,0:T(8,128)}, f32[2,8,128]{2,1,0:T(8,128)S(1)}, u32[]{:S(2)}, u32[]{:S(2)}) collective-permute-start(f32[2,8,128]{2,1,0:T(8,128)} %get-tuple-element.40), channel_id=1, source_target_pairs={{0,1},{1,0},{2,3},{3,2},{4,5},{5,4},{6,7},{7,6},{8,9},{9,8},{10,11... | collective-permute-start | bytes 24584 | tf_op jit(solution)/shard_map/ppermute | solution.py:534
  6.1 16.1 %collective-permute-start.1 = (f32[2,8,128]{2,1,0:T(8,128)}, f32[2,8,128]{2,1,0:T(8,128)S(1)}, u32[]{:S(2)}, u32[]{:S(2)}) collective-permute-start(f32[2,8,128]{2,1,0:T(8,128)} %get-tuple-element.41), channel_id=1, source_target_pairs={{0,511},{1,2},{2,1},{3,4},{4,3},{5,6},{6,5},{7,8},{8,7},{9,10},{10... | collective-permute-start | bytes 24584 | tf_op jit(solution)/shard_map/ppermute | solution.py:533
  10.1 0.9 copy-start.5
  11.0 0.7 copy-start.7
  11.6 10.6 %copy-start = (s32[4096]{0:T(1024)S(1)}, s32[4096]{0:T(1024)}, u32[]{:S(2)}) copy-start(s32[4096]{0:T(1024)} %param.20) | copy-start | bytes 49156
  11.6 10.6 %copy-start.2 = (s32[2,2]{1,0:T(2,128)S(1)}, s32[2,2]{1,0:T(2,128)}, u32[]{:S(2)}) copy-start(s32[2,2]{1,0:T(2,128)} %refs_1_.7) | copy-start | bytes 52
  11.7 10.6 %copy-start.3 = (s32[32,1]{0,1:T(1,128)S(1)}, s32[32,1]{0,1:T(1,128)}, u32[]{:S(2)}) copy-start(s32[32,1]{0,1:T(1,128)} %param.19) | copy-start | bytes 388
  11.7 10.7 %copy-start.4 = (f32[32,8,128]{2,1,0:T(8,128)S(1)}, f32[32,8,128]{2,1,0:T(8,128)}, u32[]{:S(2)}) copy-start(f32[32,8,128]{2,1,0:T(8,128)} %get-tuple-element.42.refs_8_) | copy-start | bytes 393220
  11.7 10.7 %copy-start.6 = (f32[32,8,128]{2,1,0:T(8,128)S(1)}, f32[32,8,128]{2,1,0:T(8,128)}, u32[]{:S(2)}) copy-start(f32[32,8,128]{2,1,0:T(8,128)} %get-tuple-element.39.refs_1_.refs_5_) | copy-start | bytes 393220
  22.3 16.8 %copy-start.8 = (s32[616]{0:T(1024)S(1)}, s32[616]{0:T(1024)}, u32[]{:S(2)}) copy-start(s32[616]{0:T(1024)} %get-tuple-element.38.refs_0_.refs_2_) | copy-start | bytes 7396
  24.9 24.0 %collective-permute-start.2 = (f32[2,8,128]{2,1,0:T(8,128)S(1)}, f32[2,8,128]{2,1,0:T(8,128)S(1)}, u32[]{:S(2)}, u32[]{:S(2)}) collective-permute-start(f32[2,8,128]{2,1,0:T(8,128)S(1)} %get-tuple-element.46), channel_id=1, source_target_pairs={{0,1},{1,0},{2,3},{3,2},{4,5},{5,4},{6,7},{7,6},{8,9},{9,8},{10,11... | collective-permute-start | bytes 24584 | tf_op jit(solution)/shard_map/ppermute | solution.py:534
  37.2 11.8 %collective-permute-start.3 = (f32[2,8,128]{2,1,0:T(8,128)S(1)}, f32[2,8,128]{2,1,0:T(8,128)S(1)}, u32[]{:S(2)}, u32[]{:S(2)}) collective-permute-start(f32[2,8,128]{2,1,0:T(8,128)S(1)} %get-tuple-element.47), channel_id=1, source_target_pairs={{0,511},{1,2},{2,1},{3,4},{4,3},{5,6},{6,5},{7,8},{8,7},{9,10},{10... | collective-permute-start | bytes 24584 | tf_op jit(solution)/shard_map/ppermute | solution.py:533
  51.5 15.4 %collective-permute-start.4 = (f32[2,8,128]{2,1,0:T(8,128)S(1)}, f32[2,8,128]{2,1,0:T(8,128)S(1)}, u32[]{:S(2)}, u32[]{:S(2)}) collective-permute-start(f32[2,8,128]{2,1,0:T(8,128)S(1)} %get-tuple-element.52), channel_id=1, source_target_pairs={{0,1},{1,0},{2,3},{3,2},{4,5},{5,4},{6,7},{7,6},{8,9},{9,8},{10,11... | collective-permute-start | bytes 24584 | tf_op jit(solution)/shard_map/ppermute | solution.py:534
  54.3 12.6 %collective-permute-start.5 = (f32[2,8,128]{2,1,0:T(8,128)S(1)}, f32[2,8,128]{2,1,0:T(8,128)S(1)}, u32[]{:S(2)}, u32[]{:S(2)}) collective-permute-start(f32[2,8,128]{2,1,0:T(8,128)S(1)} %get-tuple-element.53), channel_id=1, source_target_pairs={{0,511},{1,2},{2,1},{3,4},{4,3},{5,6},{6,5},{7,8},{8,7},{9,10},{10... | collective-permute-start | bytes 24584 | tf_op jit(solution)/shard_map/ppermute | solution.py:533
  69.6 17.9 %collective-permute-start.6 = (f32[2,8,128]{2,1,0:T(8,128)S(1)}, f32[2,8,128]{2,1,0:T(8,128)S(1)}, u32[]{:S(2)}, u32[]{:S(2)}) collective-permute-start(f32[2,8,128]{2,1,0:T(8,128)S(1)} %get-tuple-element.57), channel_id=1, source_target_pairs={{0,1},{1,0},{2,3},{3,2},{4,5},{5,4},{6,7},{7,6},{8,9},{9,8},{10,11... | collective-permute-start | bytes 24584 | tf_op jit(solution)/shard_map/ppermute | solution.py:534
  75.7 11.8 %collective-permute-start.7 = (f32[2,8,128]{2,1,0:T(8,128)S(1)}, f32[2,8,128]{2,1,0:T(8,128)S(1)}, u32[]{:S(2)}, u32[]{:S(2)}) collective-permute-start(f32[2,8,128]{2,1,0:T(8,128)S(1)} %get-tuple-element.58), channel_id=1, source_target_pairs={{0,511},{1,2},{2,1},{3,4},{4,3},{5,6},{6,5},{7,8},{8,7},{9,10},{10... | collective-permute-start | bytes 24584 | tf_op jit(solution)/shard_map/ppermute | solution.py:533
  92.4 34.9 %copy-start.1 = (f32[3,512]{1,0:T(4,128)S(1)}, f32[3,512]{1,0:T(4,128)}, u32[]{:S(2)}) copy-start(f32[3,512]{1,0:T(4,128)} %gas_ref.1) | copy-start | bytes 18436
  92.4 4.6 %collective-permute-start.8 = (f32[64,5,4,128]{3,2,1,0:T(4,128)S(1)}, f32[64,5,4,128]{3,2,1,0:T(4,128)S(1)}, u32[]{:S(2)}, u32[]{:S(2)}) collective-permute-start(f32[64,5,4,128]{3,2,1,0:T(4,128)S(1)} %get-tuple-element.64), channel_id=1, source_target_pairs={{0,1},{1,0},{2,3},{3,2},{4,5},{5,4},{6,7},{7,6},{8,9},{9,8},{10,11... | collective-permute-start | bytes 1966088 | tf_op jit(solution)/shard_map/ppermute | solution.py:559
  98.0 29.3 %all-to-all-start = ((f32[64,5,4,128]{3,2,1,0:T(4,128)}), f32[64,5,4,128]{3,2,1,0:T(4,128)S(1)}, u32[]{:S(2)}, u32[]{:S(2)}) async-start(f32[64,5,4,128]{3,2,1,0:T(4,128)} %add.3), calls=%async_computation | async-start | bytes 1310720 | tf_op jit(solution)/shard_map/all_to_all | solution.py:560
  128.0 7.3 %collective-permute-start.10 = (f32[8,128]{1,0:T(8,128)S(1)}, f32[8,128]{1,0:T(8,128)S(1)}, u32[]{:S(2)}, u32[]{:S(2)}) collective-permute-start(f32[8,128]{1,0:T(8,128)S(1)} %get-tuple-element.71), channel_id=1, source_target_pairs={{0,511},{1,2},{2,1},{3,4},{4,3},{5,6},{6,5},{7,8},{8,7},{9,10},{10... | collective-permute-start | bytes 12296 | tf_op jit(solution)/shard_map/ppermute | solution.py:533
  133.3 3.1 %collective-permute-start.9 = (f32[8,128]{1,0:T(8,128)S(1)}, f32[8,128]{1,0:T(8,128)S(1)}, u32[]{:S(2)}, u32[]{:S(2)}) collective-permute-start(f32[8,128]{1,0:T(8,128)S(1)} %get-tuple-element.72), channel_id=1, source_target_pairs={{0,1},{1,0},{2,3},{3,2},{4,5},{5,4},{6,7},{7,6},{8,9},{9,8},{10,11... | collective-permute-start | bytes 12296 | tf_op jit(solution)/shard_map/ppermute | solution.py:534
  159.0 6.8 %collective-permute-start.11 = (f32[64,3,4,128]{3,2,1,0:T(4,128)S(1)}, f32[64,3,4,128]{3,2,1,0:T(4,128)S(1)}, u32[]{:S(2)}, u32[]{:S(2)}) collective-permute-start(f32[64,3,4,128]{3,2,1,0:T(4,128)S(1)} %all_to_all.10.mine_ref), channel_id=1, source_target_pairs={{0,1},{1,0},{2,3},{3,2},{4,5},{5,4},{6,7},{7,6},{8,9},{9,8},{10,11... | collective-permute-start | bytes 1179656 | tf_op jit(solution)/shard_map/ppermute | solution.py:594

commit v6 on v3

--- a/solution.py
+++ b/solution.py
@@ -147,35 +147,18 @@
 
 def partner_side(tile, base, jt_ref, a_ref):
     row = row_index()
-    r = row[0]
     ones = jnp.ones((8, BP), F32)
     zeros = jnp.zeros((8, BP), F32)
     swapped, norm, cross = features(tile)
     full = jnp.where(row < 6, tile, jnp.where(row == 6, norm, cross))
     high, mid, low = parts3(full)
-    is_v = (r >= 3) & (r < 6)
-    for s in range(4):
+    for s in range(tile.shape[0]):
         h, m, l = high[s], mid[s], low[s]
         stack = jnp.concatenate([h, h, h, m, m, l, ones, zeros], axis=0)
         jt_ref[base + s] = jnp.transpose(stack).astype(BF16)
-        by_x = jnp.concatenate(
-            [
-                jnp.where(r < 3, h, jnp.where(r == 6, 1.0, 0.0)),
-                jnp.where(r < 3, m, 0.0),
-                jnp.where(r < 3, l, 0.0),
-                zeros,
-            ],
-            axis=0,
-        )
-        by_v = jnp.concatenate(
-            [
-                jnp.where(is_v, h, jnp.where(r == 7, 1.0, 0.0)),
-                jnp.where(is_v, m, 0.0),
-                jnp.where(is_v, l, 0.0),
-                zeros,
-            ],
-            axis=0,
-        )
+        tail = [ones[0:1], zeros[0:6]]
+        by_x = jnp.concatenate([h[0:3], m[0:3], l[0:3]] + tail, axis=0)
+        by_v = jnp.concatenate([h[3:6], m[3:6], l[3:6]] + tail, axis=0)
         a_ref[base + s] = jnp.concatenate([by_x, by_v], axis=1).astype(BF16)
 
 
@@ -191,7 +174,7 @@
     ch, cm, cl = parts3(cross)
     own_n = jnp.where(row == 0, nh, jnp.where(row == 1, nm, jnp.where(row == 2, nl, 0.0)))
     own_c = jnp.where(row == 0, ch, jnp.where(row == 1, cm, jnp.where(row == 2, cl, 0.0)))
-    for s in range(4):
+    for s in range(tile.shape[0]):
         left = jnp.concatenate([xh[s], xm[s], xl[s], xh[s], xm[s], xh[s], own_n[s], zeros], axis=0)
         right = jnp.concatenate([vh[s], vm[s], vl[s], vh[s], vm[s], vh[s], own_c[s], zeros], axis=0)
         g_ref[base + s] = jnp.concatenate([left, right], axis=1).astype(BF16)
@@ -219,9 +202,11 @@
 def partner_sums(b, weights, a_ref):
     left_x = a_ref[b, :, :BP]
     left_v = a_ref[b, :, BP:]
-    left = jnp.concatenate([left_x, left_x, left_v, left_v], axis=1)
-    sums = jnp.dot(left, weights, preferred_element_type=F32)
-    return sums[0:8] + sums[8:16] + sums[16:24]
+    left_x = jnp.concatenate([left_x, left_x], axis=1)
+    left_v = jnp.concatenate([left_v, left_v], axis=1)
+    by_x = jnp.dot(left_x, weights[: 2 * BP], preferred_element_type=F32)
+    by_v = jnp.dot(left_v, weights[2 * BP :], preferred_element_type=F32)
+    return jnp.concatenate([by_x, by_v], axis=0)
 
 
 def ghost_loop(groups, list_ref, acc_ref, state_ref, jt_ref, g_ref, a_ref, rb_ref):
@@ -273,12 +258,12 @@
         list_ref, state_ref, rb_ref, acc_ref, g_ref, jt_ref, a_ref, held_ref = refs
 
     def blocks(k, carry):
-        tile = state_ref[pl.ds(k * 4, 4)]
-        partner_side(tile, k * 4, jt_ref, a_ref)
-        own_side(tile, k * 4, g_ref)
+        tile = state_ref[pl.ds(k * 8, 8)]
+        partner_side(tile, k * 8, jt_ref, a_ref)
+        own_side(tile, k * 8, g_ref)
         return carry
 
-    lax.fori_loop(0, NB // 4, blocks, 0)
+    lax.fori_loop(0, NB // 8, blocks, 0)
     acc_ref[...] = jnp.zeros(acc_ref.shape, F32)
     local_loop(list_ref[4 * ROOM], list_ref, acc_ref, state_ref, jt_ref, g_ref, a_ref, rb_ref, held_ref)
 
@@ -286,7 +271,7 @@
 def local_pairs(lists, state, rb=None):
     opening = rb is None
     outs = (
-        jax.ShapeDtypeStruct((NB + 1, 8, BP), F32),
+        jax.ShapeDtypeStruct((NB + 1, 32, BP), F32),
         jax.ShapeDtypeStruct((NB, 64, 2 * BP), BF16),
     )
     wide = (jax.ShapeDtypeStruct((NB, BP, BP), F32),)
@@ -298,7 +283,7 @@
         out_specs=(VMEM,) * (3 if opening else 2),
         scratch_shapes=[
             pltpu.VMEM((NB, BP, 64), BF16),
-            pltpu.VMEM((NB, 32, 2 * BP), BF16),
+            pltpu.VMEM((NB, 16, 2 * BP), BF16),
             pltpu.VMEM((GROUP, 4 * BP, BP), BF16),
         ],
         compiler_params=PARAMS,
@@ -334,7 +319,16 @@
     ghost_loop(list_ref[4 * ROOM + 1], list_ref, acc_ref, state_ref, jt_ref, g_ref, a_ref, rb_ref)
 
     tile = state_ref[...]
-    acc = acc_ref[0:NB]
+    raw = acc_ref[0:NB]
+    acc = jnp.concatenate(
+        [
+            raw[:, 0:3] + raw[:, 3:6] + raw[:, 6:9],
+            raw[:, 16:19] + raw[:, 19:22] + raw[:, 22:25],
+            raw[:, 9:10],
+            raw[:, 25:26],
+        ],
+        axis=1,
+    )
     aux = aux_ref[...]
     by_x = STIFF * (tile * acc[:, 6:7] - acc)
     by_v = acc - tile * acc[:, 7:8]
@@ -403,9 +397,9 @@
         scratch_shapes=[
             pltpu.VMEM((8, 8, BP), F32),
             pltpu.VMEM((2 * NG, BP, 64), BF16),
-            pltpu.VMEM((2 * NG, 32, 2 * BP), BF16),
+            pltpu.VMEM((2 * NG, 16, 2 * BP), BF16),
             pltpu.VMEM((2 * NG, BP, BP), F32),
-            pltpu.VMEM((NB + 1, 8, BP), F32),
+            pltpu.VMEM((NB + 1, 32, BP), F32),
         ]
         + ([pltpu.VMEM((NB, DEPROWS, BP), F32)] if last else []),
         compiler_params=PARAMS,

time: 167 us -> 164 us (0.982)
    pallas_call x4, Pallas kernels: 39.5 us -> 35.2 us  [local_pairs(): pl.pallas_call(functools.partial(local_kernel, opening), in_specs=[SMEM]...]
    pallas_call x4, Pallas kernels: 11.6 us -> 14.4 us  [ghost_pairs(): pl.pallas_call(functools.partial(ghost_kernel, last), in_specs=[SMEM] * 4...]
    ppermute x5, starting transfers between devices: 25.9 us -> 23.5 us  [exchange(): near = lax.ppermute(near, axes, near_pairs)]
  transfers between devices with their start and end apart: 13 -> 13, of which waited for: 4 -> 4; matrix products, arithmetic and copies ran while one was open for 0% -> 0% of each run, Pallas kernels for 24% -> 21%
where the time goes in v6:
time: 164 us
  starting transfers between devices  59.1 us (36%)
  Pallas kernels  55.8 us (34%)
  waiting for transfers between devices  23.5 us (14%)
  blocking collectives  21.6 us (13%)
  local copies, waits for them, and re-layouts  1.66 us (1%)
    pallas_call x4, Pallas kernels, local_pairs(): pl.pallas_call(functools.partial(local_kernel, opening), in_specs=[SMEM]...  35.2 us
    ppermute x5, starting transfers between devices, exchange(): near = lax.ppermute(near, axes, near_pairs)  23.5 us
    all_to_all x1, blocking collectives, body(): lax.all_to_all(table, 'dom', 0, 0, axis_index_groups=same_core, tiled=True)  21.6 us
    all_to_all x1, waiting for transfers between devices, body(): lax.all_to_all(dep, 'dom', 0, 0, axis_index_groups=same_core, tiled=True)  19.3 us
    ppermute x5, starting transfers between devices, exchange(): far = lax.ppermute(far, axes, far_pairs)  16.7 us
    pallas_call x4, Pallas kernels, ghost_pairs(): pl.pallas_call(functools.partial(ghost_kernel, last), in_specs=[SMEM] * 4...  14.4 us
    all_to_all x1, starting transfers between devices, body(): lax.all_to_all(dep, 'dom', 0, 0, axis_index_groups=same_core, tiled=True)  11 us
    ppermute x1, starting transfers between devices, body(): other = lax.ppermute(table, axes, near_pairs)  5.42 us
  transfers between devices with their start and end apart: 13, of which 4 were waited for; matrix products, arithmetic and copies ran while one was open for 0% of the time, Pallas kernels for 21%

profile of v6, /device:TPU:7, one launch (start us, length us, event | category | flops | bytes accessed | tf_op | source)
XLA Modules:
  0.0 163.7 jit_solution(14440804367625609383)
XLA Ops:
  0.6 2.9 %prepare.1 = (f32[32,8,128]{2,1,0:T(8,128)}, f32[32,8,128]{2,1,0:T(8,128)}, f32[2,8,128]{2,1,0:T(8,128)}, f32[2,8,128]{2,1,0:T(8,128)}, s32[584]{0:T(1024)}) custom-call(s32[1]{0:T(128)} %bitcast.par_ref.refs_0_, s32[2,2]{1,0:T(2,128)} %refs_1_.7, f32[3,4096]{1,0:T(4,128)} %pos_hbm.1, f32[3,4096]{1,0:T(4,128)} %vel_hbm.1, f32[3,4096]{1,0:T(4,128)} %gas_hbm.1, ...), custom_call_target="tpu_custom_call" | custom-call | flops 100000 | bytes 600000 | tf_op jit(solution)/shard_map/prepare/pallas_call | solution.py:114
  3.6 2.6 %collective-permute-start = (f32[2,8,128]{2,1,0:T(8,128)}, f32[2,8,128]{2,1,0:T(8,128)S(1)}, u32[]{:S(2)}, u32[]{:S(2)}) collective-permute-start(f32[2,8,128]{2,1,0:T(8,128)} %get-tuple-element.40), channel_id=1, source_target_pairs={{0,1},{1,0},{2,3},{3,2},{4,5},{5,4},{6,7},{7,6},{8,9},{9,8},{10,11... | collective-permute-start | bytes 24584 | tf_op jit(solution)/shard_map/ppermute | solution.py:502
  6.1 3.9 %collective-permute-start.1 = (f32[2,8,128]{2,1,0:T(8,128)}, f32[2,8,128]{2,1,0:T(8,128)S(1)}, u32[]{:S(2)}, u32[]{:S(2)}) collective-permute-start(f32[2,8,128]{2,1,0:T(8,128)} %get-tuple-element.41), channel_id=1, source_target_pairs={{0,511},{1,2},{2,1},{3,4},{4,3},{5,6},{6,5},{7,8},{8,7},{9,10},{10... | collective-permute-start | bytes 24584 | tf_op jit(solution)/shard_map/ppermute | solution.py:501
  10.1 0.9 copy-done.5
  11.0 0.7 copy-done.7
  11.7 9.3 %local_pairs.4 = (f32[33,32,128]{2,1,0:T(8,128)S(1)}, bf16[32,64,256]{2,1,0:T(8,128)(2,1)S(1)}, f32[32,128,128]{2,1,0:T(8,128)S(1)}) custom-call(s32[584]{0:T(1024)S(1)} %copy-done.7, f32[32,8,128]{2,1,0:T(8,128)S(1)} %copy-done.5), custom_call_target="tpu_custom_call" | custom-call | flops 10000000000 | bytes 3500000 | tf_op jit(solution)/shard_map/local_pairs/pallas_call | solution.py:279
  21.0 0.0 collective-permute-done.refs_6_
  21.0 0.0 collective-permute-done.1.refs_7_
  21.0 0.0 copy-done
  21.0 0.0 copy-done.2
  21.0 0.0 copy-done.3
  21.0 0.0 copy-done.4
  21.1 0.0 copy-start.8
  21.1 3.0 %ghost_pairs.3 = (f32[32,8,128]{2,1,0:T(8,128)S(1)}, f32[2,8,128]{2,1,0:T(8,128)S(1)}, f32[2,8,128]{2,1,0:T(8,128)S(1)}) custom-call(s32[1]{0:T(128)} %bitcast.par_ref.refs_0_, s32[2,2]{1,0:T(2,128)S(1)} %copy-done.2, s32[584]{0:T(1024)S(1)} %copy-done.7, s32[32]{0:T(128)S(1)} %bitcast.11, s32[32,128]{1,0:T(8,128)S(1)} %bitcast.6, ...), custom_call_target="tpu_custom_call" | custom-call | flops 2000000000 | bytes 2000000 | tf_op jit(solution)/shard_map/ghost_pairs/pallas_call | solution.py:392
  24.1 11.6 %collective-permute-start.2 = (f32[2,8,128]{2,1,0:T(8,128)S(1)}, f32[2,8,128]{2,1,0:T(8,128)S(1)}, u32[]{:S(2)}, u32[]{:S(2)}) collective-permute-start(f32[2,8,128]{2,1,0:T(8,128)S(1)} %get-tuple-element.46), channel_id=1, source_target_pairs={{0,1},{1,0},{2,3},{3,2},{4,5},{5,4},{6,7},{7,6},{8,9},{9,8},{10,11... | collective-permute-start | bytes 24584 | tf_op jit(solution)/shard_map/ppermute | solution.py:502
  35.8 1.9 %collective-permute-start.3 = (f32[2,8,128]{2,1,0:T(8,128)S(1)}, f32[2,8,128]{2,1,0:T(8,128)S(1)}, u32[]{:S(2)}, u32[]{:S(2)}) collective-permute-start(f32[2,8,128]{2,1,0:T(8,128)S(1)} %get-tuple-element.47), channel_id=1, source_target_pairs={{0,511},{1,2},{2,1},{3,4},{4,3},{5,6},{6,5},{7,8},{8,7},{9,10},{10... | collective-permute-start | bytes 24584 | tf_op jit(solution)/shard_map/ppermute | solution.py:501
  37.7 8.6 %local_pairs.5 = (f32[33,32,128]{2,1,0:T(8,128)S(1)}, bf16[32,64,256]{2,1,0:T(8,128)(2,1)S(1)}) custom-call(s32[584]{0:T(1024)S(1)} %copy-done.8, f32[32,8,128]{2,1,0:T(8,128)S(1)} %get-tuple-element.45.refs_1_.refs_5_, f32[32,128,128]{2,1,0:T(8,128)S(1)} %get-tuple-element.48.refs_2_), custom_call_target="tpu_custom_call" | custom-call | flops 10000000000 | bytes 3500000 | tf_op jit(solution)/shard_map/local_pairs/pallas_call | solution.py:279
  46.3 0.0 collective-permute-done.2.refs_6_
  46.3 0.0 collective-permute-done.3.refs_7_
  46.3 3.0 %ghost_pairs.4 = (f32[32,8,128]{2,1,0:T(8,128)S(1)}, f32[2,8,128]{2,1,0:T(8,128)S(1)}, f32[2,8,128]{2,1,0:T(8,128)S(1)}) custom-call(s32[1]{0:T(128)} %bitcast.par_ref.refs_0_, s32[2,2]{1,0:T(2,128)S(1)} %copy-done.2, s32[584]{0:T(1024)S(1)} %copy-done.8, s32[32]{0:T(128)S(1)} %bitcast.12, s32[32,128]{1,0:T(8,128)S(1)} %bitcast.7, ...), custom_call_target="tpu_custom_call" | custom-call | flops 2000000000 | bytes 2000000 | tf_op jit(solution)/shard_map/ghost_pairs/pallas_call | solution.py:392
  49.4 2.0 %collective-permute-start.4 = (f32[2,8,128]{2,1,0:T(8,128)S(1)}, f32[2,8,128]{2,1,0:T(8,128)S(1)}, u32[]{:S(2)}, u32[]{:S(2)}) collective-permute-start(f32[2,8,128]{2,1,0:T(8,128)S(1)} %get-tuple-element.52), channel_id=1, source_target_pairs={{0,1},{1,0},{2,3},{3,2},{4,5},{5,4},{6,7},{7,6},{8,9},{9,8},{10,11... | collective-permute-start | bytes 24584 | tf_op jit(solution)/shard_map/ppermute | solution.py:502
  51.4 3.6 %collective-permute-start.5 = (f32[2,8,128]{2,1,0:T(8,128)S(1)}, f32[2,8,128]{2,1,0:T(8,128)S(1)}, u32[]{:S(2)}, u32[]{:S(2)}) collective-permute-start(f32[2,8,128]{2,1,0:T(8,128)S(1)} %get-tuple-element.53), channel_id=1, source_target_pairs={{0,511},{1,2},{2,1},{3,4},{4,3},{5,6},{6,5},{7,8},{8,7},{9,10},{10... | collective-permute-start | bytes 24584 | tf_op jit(solution)/shard_map/ppermute | solution.py:501
  55.0 8.6 %local_pairs.6 = (f32[33,32,128]{2,1,0:T(8,128)S(1)}, bf16[32,64,256]{2,1,0:T(8,128)(2,1)S(1)}) custom-call(s32[584]{0:T(1024)S(1)} %copy-done.8, f32[32,8,128]{2,1,0:T(8,128)S(1)} %get-tuple-element.51.refs_1_.refs_5_, f32[32,128,128]{2,1,0:T(8,128)S(1)} %get-tuple-element.48.refs_2_), custom_call_target="tpu_custom_call" | custom-call | flops 10000000000 | bytes 3500000 | tf_op jit(solution)/shard_map/local_pairs/pallas_call | solution.py:279
  63.6 0.0 collective-permute-done.4.refs_6_
  63.6 0.0 collective-permute-done.5.refs_7_
  63.6 3.0 %ghost_pairs.5 = (f32[32,8,128]{2,1,0:T(8,128)S(1)}, f32[2,8,128]{2,1,0:T(8,128)S(1)}, f32[2,8,128]{2,1,0:T(8,128)S(1)}) custom-call(s32[1]{0:T(128)} %bitcast.par_ref.refs_0_, s32[2,2]{1,0:T(2,128)S(1)} %copy-done.2, s32[584]{0:T(1024)S(1)} %copy-done.8, s32[32]{0:T(128)S(1)} %bitcast.13, s32[32,128]{1,0:T(8,128)S(1)} %bitcast.8, ...), custom_call_target="tpu_custom_call" | custom-call | flops 2000000000 | bytes 2000000 | tf_op jit(solution)/shard_map/ghost_pairs/pallas_call | solution.py:392
  66.7 5.4 %collective-permute-start.6 = (f32[2,8,128]{2,1,0:T(8,128)S(1)}, f32[2,8,128]{2,1,0:T(8,128)S(1)}, u32[]{:S(2)}, u32[]{:S(2)}) collective-permute-start(f32[2,8,128]{2,1,0:T(8,128)S(1)} %get-tuple-element.57), channel_id=1, source_target_pairs={{0,1},{1,0},{2,3},{3,2},{4,5},{5,4},{6,7},{7,6},{8,9},{9,8},{10,11... | collective-permute-start | bytes 24584 | tf_op jit(solution)/shard_map/ppermute | solution.py:502
  72.1 1.9 %collective-permute-start.7 = (f32[2,8,128]{2,1,0:T(8,128)S(1)}, f32[2,8,128]{2,1,0:T(8,128)S(1)}, u32[]{:S(2)}, u32[]{:S(2)}) collective-permute-start(f32[2,8,128]{2,1,0:T(8,128)S(1)} %get-tuple-element.58), channel_id=1, source_target_pairs={{0,511},{1,2},{2,1},{3,4},{4,3},{5,6},{6,5},{7,8},{8,7},{9,10},{10... | collective-permute-start | bytes 24584 | tf_op jit(solution)/shard_map/ppermute | solution.py:501
  74.0 8.6 %local_pairs.7 = (f32[33,32,128]{2,1,0:T(8,128)S(1)}, bf16[32,64,256]{2,1,0:T(8,128)(2,1)S(1)}) custom-call(s32[584]{0:T(1024)S(1)} %copy-done.8, f32[32,8,128]{2,1,0:T(8,128)S(1)} %get-tuple-element.56.refs_1_.refs_5_, f32[32,128,128]{2,1,0:T(8,128)S(1)} %get-tuple-element.48.refs_2_), custom_call_target="tpu_custom_call" | custom-call | flops 10000000000 | bytes 3500000 | tf_op jit(solution)/shard_map/local_pairs/pallas_call | solution.py:279
  82.7 0.0 collective-permute-done.6.refs_6_
  82.7 0.0 collective-permute-done.7.refs_7_
  82.7 5.3 %ghost_pairs_last.1 = (f32[3,4096]{1,0:T(4,128)}, f32[3,4096]{1,0:T(4,128)}, f32[64,5,4,128]{3,2,1,0:T(4,128)S(1)}, f32[64,5,4,128]{3,2,1,0:T(4,128)S(1)}) custom-call(s32[1]{0:T(128)} %bitcast.par_ref.refs_0_, s32[2,2]{1,0:T(2,128)S(1)} %copy-done.2, s32[584]{0:T(1024)S(1)} %copy-done.8, s32[32]{0:T(128)S(1)} %bitcast.14, s32[32,128]{1,0:T(8,128)S(1)} %bitcast.9, ...), custom_call_target="tpu_custom_call" | custom-call | flops 2000000000 | bytes 2000000 | tf_op jit(solution)/shard_map/ghost_pairs_last/pallas_call | solution.py:392
  88.0 2.5 %collective-permute-start.8 = (f32[64,5,4,128]{3,2,1,0:T(4,128)S(1)}, f32[64,5,4,128]{3,2,1,0:T(4,128)S(1)}, u32[]{:S(2)}, u32[]{:S(2)}) collective-permute-start(f32[64,5,4,128]{3,2,1,0:T(4,128)S(1)} %get-tuple-element.64), channel_id=1, source_target_pairs={{0,1},{1,0},{2,3},{3,2},{4,5},{5,4},{6,7},{7,6},{8,9},{9,8},{10,11... | collective-permute-start | bytes 1966088 | tf_op jit(solution)/shard_map/ppermute | solution.py:527
  90.5 1.7 %collective-permute-done.8 = f32[64,5,4,128]{3,2,1,0:T(4,128)S(1)} collective-permute-done((f32[64,5,4,128]{3,2,1,0:T(4,128)S(1)}, f32[64,5,4,128]{3,2,1,0:T(4,128)S(1)}, u32[]{:S(2)}, u32[]{:S(2)}) %collective-permute-start.8) | collective-permute-done | bytes 655392 | tf_op jit(solution)/shard_map/ppermute | solution.py:527
  92.2 1.0 add.3
  93.2 11.0 %all-to-all-start = ((f32[64,5,4,128]{3,2,1,0:T(4,128)}), f32[64,5,4,128]{3,2,1,0:T(4,128)S(1)}, u32[]{:S(2)}, u32[]{:S(2)}) async-start(f32[64,5,4,128]{3,2,1,0:T(4,128)} %add.3), calls=%async_computation | async-start | bytes 1310720 | tf_op jit(solution)/shard_map/all_to_all | solution.py:528
  104.2 19.3 %all-to-all-done.dep_ref = f32[64,5,4,128]{3,2,1,0:T(4,128)S(1)} async-done(((f32[64,5,4,128]{3,2,1,0:T(4,128)}), f32[64,5,4,128]{3,2,1,0:T(4,128)S(1)}, u32[]{:S(2)}, u32[]{:S(2)}) %all-to-all-start) | async-done | bytes 655392 | tf_op jit(solution)/shard_map/all_to_all | solution.py:528
  123.5 0.7 known.1
  124.2 5.3 %collective-permute-start.10 = (f32[8,128]{1,0:T(8,128)S(1)}, f32[8,128]{1,0:T(8,128)S(1)}, u32[]{:S(2)}, u32[]{:S(2)}) collective-permute-start(f32[8,128]{1,0:T(8,128)S(1)} %get-tuple-element.71), channel_id=1, source_target_pairs={{0,511},{1,2},{2,1},{3,4},{4,3},{5,6},{6,5},{7,8},{8,7},{9,10},{10... | collective-permute-start | bytes 12296 | tf_op jit(solution)/shard_map/ppermute | solution.py:501
  129.5 1.9 %collective-permute-start.9 = (f32[8,128]{1,0:T(8,128)S(1)}, f32[8,128]{1,0:T(8,128)S(1)}, u32[]{:S(2)}, u32[]{:S(2)}) collective-permute-start(f32[8,128]{1,0:T(8,128)S(1)} %get-tuple-element.72), channel_id=1, source_target_pairs={{0,1},{1,0},{2,3},{3,2},{4,5},{5,4},{6,7},{7,6},{8,9},{9,8},{10,11... | collective-permute-start | bytes 12296 | tf_op jit(solution)/shard_map/ppermute | solution.py:502
  131.4 0.0 collective-permute-done.10.far_ref
  131.4 1.1 collective-permute-done.9.near_ref
  132.5 0.9 sweeps.1
  133.5 0.1 broadcast_in_dim.2
  133.5 21.6 %all_to_all.10.mine_ref = f32[64,3,4,128]{3,2,1,0:T(4,128)S(1)} all-to-all(f32[64,3,4,128]{3,2,1,0:T(4,128)S(1)} %broadcast_in_dim.2), channel_id=1, replica_groups={{0,2,4,6,8,10,12,14,16,18,20,22,24,26,28,30,32,34,36,38,40,42,44,46,48,..., dimensions={0} | all-to-all | bytes 786432 | tf_op jit(solution)/shard_map/all_to_all | solution.py:561
  155.2 5.4 %collective-permute-start.11 = (f32[64,3,4,128]{3,2,1,0:T(4,128)S(1)}, f32[64,3,4,128]{3,2,1,0:T(4,128)S(1)}, u32[]{:S(2)}, u32[]{:S(2)}) collective-permute-start(f32[64,3,4,128]{3,2,1,0:T(4,128)S(1)} %all_to_all.10.mine_ref), channel_id=1, source_target_pairs={{0,1},{1,0},{2,3},{3,2},{4,5},{5,4},{6,7},{7,6},{8,9},{9,8},{10,11... | collective-permute-start | bytes 1179656 | tf_op jit(solution)/shard_map/ppermute | solution.py:562
  160.6 1.3 collective-permute-done.11.other_ref
  161.9 1.7 %pick.1 = f32[3,4096]{1,0:T(4,128)} custom-call(s32[1]{0:T(128)} %bitcast.par_ref.refs_0_, s32[32]{0:T(128)S(1)} %bitcast.15, s32[32,128]{1,0:T(8,128)S(1)} %bitcast.10, f32[64,3,4,128]{3,2,1,0:T(4,128)S(1)} %all_to_all.10.mine_ref, f32[64,3,4,128]{3,2,1,0:T(4,128)S(1)} %collective-permute-done.11.other_ref), custom_call_target="tpu_custom_call" | custom-call | flops 60000000 | bytes 900000 | tf_op jit(solution)/shard_map/pick/pallas_call | solution.py:563
  (12 shorter events, 0.0 us)
Async XLA Ops:
  3.6 17.4 %collective-permute-start = (f32[2,8,128]{2,1,0:T(8,128)}, f32[2,8,128]{2,1,0:T(8,128)S(1)}, u32[]{:S(2)}, u32[]{:S(2)}) collective-permute-start(f32[2,8,128]{2,1,0:T(8,128)} %get-tuple-element.40), channel_id=1, source_target_pairs={{0,1},{1,0},{2,3},{3,2},{4,5},{5,4},{6,7},{7,6},{8,9},{9,8},{10,11... | collective-permute-start | bytes 24584 | tf_op jit(solution)/shard_map/ppermute | solution.py:502
  6.1 14.8 %collective-permute-start.1 = (f32[2,8,128]{2,1,0:T(8,128)}, f32[2,8,128]{2,1,0:T(8,128)S(1)}, u32[]{:S(2)}, u32[]{:S(2)}) collective-permute-start(f32[2,8,128]{2,1,0:T(8,128)} %get-tuple-element.41), channel_id=1, source_target_pairs={{0,511},{1,2},{2,1},{3,4},{4,3},{5,6},{6,5},{7,8},{8,7},{9,10},{10... | collective-permute-start | bytes 24584 | tf_op jit(solution)/shard_map/ppermute | solution.py:501
  10.1 0.9 copy-start.5
  11.0 0.7 copy-start.7
  11.6 9.4 %copy-start = (s32[4096]{0:T(1024)S(1)}, s32[4096]{0:T(1024)}, u32[]{:S(2)}) copy-start(s32[4096]{0:T(1024)} %param.20) | copy-start | bytes 49156
  11.6 9.4 %copy-start.2 = (s32[2,2]{1,0:T(2,128)S(1)}, s32[2,2]{1,0:T(2,128)}, u32[]{:S(2)}) copy-start(s32[2,2]{1,0:T(2,128)} %refs_1_.7) | copy-start | bytes 52
  11.7 9.4 %copy-start.3 = (s32[32,1]{0,1:T(1,128)S(1)}, s32[32,1]{0,1:T(1,128)}, u32[]{:S(2)}) copy-start(s32[32,1]{0,1:T(1,128)} %param.19) | copy-start | bytes 388
  11.7 9.4 %copy-start.4 = (f32[32,8,128]{2,1,0:T(8,128)S(1)}, f32[32,8,128]{2,1,0:T(8,128)}, u32[]{:S(2)}) copy-start(f32[32,8,128]{2,1,0:T(8,128)} %get-tuple-element.42.refs_8_) | copy-start | bytes 393220
  11.7 9.4 %copy-start.6 = (f32[32,8,128]{2,1,0:T(8,128)S(1)}, f32[32,8,128]{2,1,0:T(8,128)}, u32[]{:S(2)}) copy-start(f32[32,8,128]{2,1,0:T(8,128)} %get-tuple-element.39.refs_1_.refs_5_) | copy-start | bytes 393220
  21.1 16.6 %copy-start.8 = (s32[584]{0:T(1024)S(1)}, s32[584]{0:T(1024)}, u32[]{:S(2)}) copy-start(s32[584]{0:T(1024)} %get-tuple-element.38.refs_0_.refs_2_) | copy-start | bytes 7012
  24.1 22.2 %collective-permute-start.2 = (f32[2,8,128]{2,1,0:T(8,128)S(1)}, f32[2,8,128]{2,1,0:T(8,128)S(1)}, u32[]{:S(2)}, u32[]{:S(2)}) collective-permute-start(f32[2,8,128]{2,1,0:T(8,128)S(1)} %get-tuple-element.46), channel_id=1, source_target_pairs={{0,1},{1,0},{2,3},{3,2},{4,5},{5,4},{6,7},{7,6},{8,9},{9,8},{10,11... | collective-permute-start | bytes 24584 | tf_op jit(solution)/shard_map/ppermute | solution.py:502
  35.8 10.6 %collective-permute-start.3 = (f32[2,8,128]{2,1,0:T(8,128)S(1)}, f32[2,8,128]{2,1,0:T(8,128)S(1)}, u32[]{:S(2)}, u32[]{:S(2)}) collective-permute-start(f32[2,8,128]{2,1,0:T(8,128)S(1)} %get-tuple-element.47), channel_id=1, source_target_pairs={{0,511},{1,2},{2,1},{3,4},{4,3},{5,6},{6,5},{7,8},{8,7},{9,10},{10... | collective-permute-start | bytes 24584 | tf_op jit(solution)/shard_map/ppermute | solution.py:501
  49.4 14.2 %collective-permute-start.4 = (f32[2,8,128]{2,1,0:T(8,128)S(1)}, f32[2,8,128]{2,1,0:T(8,128)S(1)}, u32[]{:S(2)}, u32[]{:S(2)}) collective-permute-start(f32[2,8,128]{2,1,0:T(8,128)S(1)} %get-tuple-element.52), channel_id=1, source_target_pairs={{0,1},{1,0},{2,3},{3,2},{4,5},{5,4},{6,7},{7,6},{8,9},{9,8},{10,11... | collective-permute-start | bytes 24584 | tf_op jit(solution)/shard_map/ppermute | solution.py:502
  51.4 12.3 %collective-permute-start.5 = (f32[2,8,128]{2,1,0:T(8,128)S(1)}, f32[2,8,128]{2,1,0:T(8,128)S(1)}, u32[]{:S(2)}, u32[]{:S(2)}) collective-permute-start(f32[2,8,128]{2,1,0:T(8,128)S(1)} %get-tuple-element.53), channel_id=1, source_target_pairs={{0,511},{1,2},{2,1},{3,4},{4,3},{5,6},{6,5},{7,8},{8,7},{9,10},{10... | collective-permute-start | bytes 24584 | tf_op jit(solution)/shard_map/ppermute | solution.py:501
  66.7 16.0 %collective-permute-start.6 = (f32[2,8,128]{2,1,0:T(8,128)S(1)}, f32[2,8,128]{2,1,0:T(8,128)S(1)}, u32[]{:S(2)}, u32[]{:S(2)}) collective-permute-start(f32[2,8,128]{2,1,0:T(8,128)S(1)} %get-tuple-element.57), channel_id=1, source_target_pairs={{0,1},{1,0},{2,3},{3,2},{4,5},{5,4},{6,7},{7,6},{8,9},{9,8},{10,11... | collective-permute-start | bytes 24584 | tf_op jit(solution)/shard_map/ppermute | solution.py:502
  72.1 10.6 %collective-permute-start.7 = (f32[2,8,128]{2,1,0:T(8,128)S(1)}, f32[2,8,128]{2,1,0:T(8,128)S(1)}, u32[]{:S(2)}, u32[]{:S(2)}) collective-permute-start(f32[2,8,128]{2,1,0:T(8,128)S(1)} %get-tuple-element.58), channel_id=1, source_target_pairs={{0,511},{1,2},{2,1},{3,4},{4,3},{5,6},{6,5},{7,8},{8,7},{9,10},{10... | collective-permute-start | bytes 24584 | tf_op jit(solution)/shard_map/ppermute | solution.py:501
  87.9 35.6 %copy-start.1 = (f32[3,512]{1,0:T(4,128)S(1)}, f32[3,512]{1,0:T(4,128)}, u32[]{:S(2)}) copy-start(f32[3,512]{1,0:T(4,128)} %gas_ref.1) | copy-start | bytes 18436
  88.0 4.2 %collective-permute-start.8 = (f32[64,5,4,128]{3,2,1,0:T(4,128)S(1)}, f32[64,5,4,128]{3,2,1,0:T(4,128)S(1)}, u32[]{:S(2)}, u32[]{:S(2)}) collective-permute-start(f32[64,5,4,128]{3,2,1,0:T(4,128)S(1)} %get-tuple-element.64), channel_id=1, source_target_pairs={{0,1},{1,0},{2,3},{3,2},{4,5},{5,4},{6,7},{7,6},{8,9},{9,8},{10,11... | collective-permute-start | bytes 1966088 | tf_op jit(solution)/shard_map/ppermute | solution.py:527
  93.2 30.3 %all-to-all-start = ((f32[64,5,4,128]{3,2,1,0:T(4,128)}), f32[64,5,4,128]{3,2,1,0:T(4,128)S(1)}, u32[]{:S(2)}, u32[]{:S(2)}) async-start(f32[64,5,4,128]{3,2,1,0:T(4,128)} %add.3), calls=%async_computation | async-start | bytes 1310720 | tf_op jit(solution)/shard_map/all_to_all | solution.py:528
  124.2 7.3 %collective-permute-start.10 = (f32[8,128]{1,0:T(8,128)S(1)}, f32[8,128]{1,0:T(8,128)S(1)}, u32[]{:S(2)}, u32[]{:S(2)}) collective-permute-start(f32[8,128]{1,0:T(8,128)S(1)} %get-tuple-element.71), channel_id=1, source_target_pairs={{0,511},{1,2},{2,1},{3,4},{4,3},{5,6},{6,5},{7,8},{8,7},{9,10},{10... | collective-permute-start | bytes 12296 | tf_op jit(solution)/shard_map/ppermute | solution.py:501
  129.5 3.1 %collective-permute-start.9 = (f32[8,128]{1,0:T(8,128)S(1)}, f32[8,128]{1,0:T(8,128)S(1)}, u32[]{:S(2)}, u32[]{:S(2)}) collective-permute-start(f32[8,128]{1,0:T(8,128)S(1)} %get-tuple-element.72), channel_id=1, source_target_pairs={{0,1},{1,0},{2,3},{3,2},{4,5},{5,4},{6,7},{7,6},{8,9},{9,8},{10,11... | collective-permute-start | bytes 12296 | tf_op jit(solution)/shard_map/ppermute | solution.py:502
  155.2 6.8 %collective-permute-start.11 = (f32[64,3,4,128]{3,2,1,0:T(4,128)S(1)}, f32[64,3,4,128]{3,2,1,0:T(4,128)S(1)}, u32[]{:S(2)}, u32[]{:S(2)}) collective-permute-start(f32[64,3,4,128]{3,2,1,0:T(4,128)S(1)} %all_to_all.10.mine_ref), channel_id=1, source_target_pairs={{0,1},{1,0},{2,3},{3,2},{4,5},{5,4},{6,7},{7,6},{8,9},{9,8},{10,11... | collective-permute-start | bytes 1179656 | tf_op jit(solution)/shard_map/ppermute | solution.py:562

commit v7 on v6

--- a/solution.py
+++ b/solution.py
@@ -18,6 +18,7 @@
 K = 5
 CHUNKS = 4
 DEPROWS = 24
+DEPTH = 48
 ROOM = NPAIR + 2 * GROUP
 LISTS = 4 * ROOM + 8
 
@@ -95,7 +96,7 @@
         list_ref[ROOM + slot] = second
         return local + 1 - is_ghost, ghost + is_ghost
 
-    local, ghost = lax.fori_loop(0, NPAIR, sort_pair, (jnp.int32(0), jnp.int32(0)))
+    local, ghost = lax.fori_loop(0, NPAIR, sort_pair, (jnp.int32(0), jnp.int32(0)), unroll=4)
     for s in range(GROUP):
         list_ref[s] = NB
         list_ref[ROOM + s] = 0
@@ -154,7 +155,9 @@
     high, mid, low = parts3(full)
     for s in range(tile.shape[0]):
         h, m, l = high[s], mid[s], low[s]
-        stack = jnp.concatenate([h, h, h, m, m, l, ones, zeros], axis=0)
+        h_one = jnp.where(row[0] < 6, h, 1.0)
+        m_one = jnp.where(row[0] < 6, m, 1.0)
+        stack = jnp.concatenate([h, h_one, h_one, m, m_one, l], axis=0)
         jt_ref[base + s] = jnp.transpose(stack).astype(BF16)
         tail = [ones[0:1], zeros[0:6]]
         by_x = jnp.concatenate([h[0:3], m[0:3], l[0:3]] + tail, axis=0)
@@ -164,7 +167,6 @@
 
 def own_side(tile, base, g_ref):
     row = row_index()
-    zeros = jnp.zeros((8, BP), F32)
     swapped, norm, cross = features(tile)
     xh, xm, xl = parts3(jnp.where(row < 3, -2.0 * tile, 0.0))
     xh = jnp.where(row == 6, 1.0, xh)
@@ -172,11 +174,11 @@
     vh = jnp.where(row == 7, 1.0, vh)
     nh, nm, nl = parts3(norm + SOFT)
     ch, cm, cl = parts3(cross)
-    own_n = jnp.where(row == 0, nh, jnp.where(row == 1, nm, jnp.where(row == 2, nl, 0.0)))
-    own_c = jnp.where(row == 0, ch, jnp.where(row == 1, cm, jnp.where(row == 2, cl, 0.0)))
+    lefts = (xh, jnp.where(row == 6, nh, xm), jnp.where(row == 6, nm, xl), xh, jnp.where(row == 6, nl, xm), xh)
+    rights = (vh, jnp.where(row == 7, ch, vm), jnp.where(row == 7, cm, vl), vh, jnp.where(row == 7, cl, vm), vh)
     for s in range(tile.shape[0]):
-        left = jnp.concatenate([xh[s], xm[s], xl[s], xh[s], xm[s], xh[s], own_n[s], zeros], axis=0)
-        right = jnp.concatenate([vh[s], vm[s], vl[s], vh[s], vm[s], vh[s], own_c[s], zeros], axis=0)
+        left = jnp.concatenate([part[s] for part in lefts], axis=0)
+        right = jnp.concatenate([part[s] for part in rights], axis=0)
         g_ref[base + s] = jnp.concatenate([left, right], axis=1).astype(BF16)
 
 
@@ -272,7 +274,7 @@
     opening = rb is None
     outs = (
         jax.ShapeDtypeStruct((NB + 1, 32, BP), F32),
-        jax.ShapeDtypeStruct((NB, 64, 2 * BP), BF16),
+        jax.ShapeDtypeStruct((NB, DEPTH, 2 * BP), BF16),
     )
     wide = (jax.ShapeDtypeStruct((NB, BP, BP), F32),)
     args = (lists, state) if opening else (lists, state, rb)
@@ -282,7 +284,7 @@
         out_shape=outs + (wide if opening else ()),
         out_specs=(VMEM,) * (3 if opening else 2),
         scratch_shapes=[
-            pltpu.VMEM((NB, BP, 64), BF16),
+            pltpu.VMEM((NB, BP, DEPTH), BF16),
             pltpu.VMEM((NB, 16, 2 * BP), BF16),
             pltpu.VMEM((GROUP, 4 * BP, BP), BF16),
         ],
@@ -396,7 +398,7 @@
         out_specs=(VMEM,) * len(outs),
         scratch_shapes=[
             pltpu.VMEM((8, 8, BP), F32),
-            pltpu.VMEM((2 * NG, BP, 64), BF16),
+            pltpu.VMEM((2 * NG, BP, DEPTH), BF16),
             pltpu.VMEM((2 * NG, 16, 2 * BP), BF16),
             pltpu.VMEM((2 * NG, BP, BP), F32),
             pltpu.VMEM((NB + 1, 32, BP), F32),

time: 164 us -> 164 us (level)
    pallas_call x4, Pallas kernels: 14.4 us -> 11.9 us  [ghost_pairs(): pl.pallas_call(functools.partial(ghost_kernel, last), in_specs=[SMEM] * 4...]
    pallas_call x4, Pallas kernels: 35.2 us -> 37.3 us  [local_pairs(): pl.pallas_call(functools.partial(local_kernel, opening), in_specs=[SMEM]...]
  transfers between devices with their start and end apart: 13 -> 13, of which waited for: 4 -> 4; matrix products, arithmetic and copies ran while one was open for 0% -> 0% of each run, Pallas kernels for 21% -> 23%
where the time goes in v7:
time: 164 us; the launch traced here: 163 us
  starting transfers between devices  59.5 us (36%)
  Pallas kernels  55 us (34%)
  waiting for transfers between devices  23.5 us (14%)
  blocking collectives  21.6 us (13%)
  local copies, waits for them, and re-layouts  1.66 us (1%)
    pallas_call x4, Pallas kernels, local_pairs(): pl.pallas_call(functools.partial(local_kernel, opening), in_specs=[SMEM]...  37.3 us
    ppermute x5, starting transfers between devices, exchange(): near = lax.ppermute(near, axes, near_pairs)  25.2 us
    all_to_all x1, blocking collectives, body(): lax.all_to_all(table, 'dom', 0, 0, axis_index_groups=same_core, tiled=True)  21.6 us
    all_to_all x1, waiting for transfers between devices, body(): lax.all_to_all(dep, 'dom', 0, 0, axis_index_groups=same_core, tiled=True)  19.3 us
    ppermute x5, starting transfers between devices, exchange(): far = lax.ppermute(far, axes, far_pairs)  15.5 us
    pallas_call x4, Pallas kernels, ghost_pairs(): pl.pallas_call(functools.partial(ghost_kernel, last), in_specs=[SMEM] * 4...  11.9 us
    all_to_all x1, starting transfers between devices, body(): lax.all_to_all(dep, 'dom', 0, 0, axis_index_groups=same_core, tiled=True)  10.8 us
    ppermute x1, starting transfers between devices, body(): other = lax.ppermute(table, axes, near_pairs)  5.42 us
  transfers between devices with their start and end apart: 13, of which 4 were waited for; matrix products, arithmetic and copies ran while one was open for 0% of the time, Pallas kernels for 23%

profile of v7, /device:TPU:7, one launch (start us, length us, event | category | flops | bytes accessed | tf_op | source)
XLA Modules:
  0.0 163.3 jit_solution(5758117765610183094)
XLA Ops:
  0.6 2.5 %prepare.1 = (f32[32,8,128]{2,1,0:T(8,128)}, f32[32,8,128]{2,1,0:T(8,128)}, f32[2,8,128]{2,1,0:T(8,128)}, f32[2,8,128]{2,1,0:T(8,128)}, s32[584]{0:T(1024)}) custom-call(s32[1]{0:T(128)} %bitcast.par_ref.refs_0_, s32[2,2]{1,0:T(2,128)} %refs_1_.7, f32[3,4096]{1,0:T(4,128)} %pos_hbm.1, f32[3,4096]{1,0:T(4,128)} %vel_hbm.1, f32[3,4096]{1,0:T(4,128)} %gas_hbm.1, ...), custom_call_target="tpu_custom_call" | custom-call | flops 100000 | bytes 600000 | tf_op jit(solution)/shard_map/prepare/pallas_call | solution.py:115
  3.1 2.6 %collective-permute-start = (f32[2,8,128]{2,1,0:T(8,128)}, f32[2,8,128]{2,1,0:T(8,128)S(1)}, u32[]{:S(2)}, u32[]{:S(2)}) collective-permute-start(f32[2,8,128]{2,1,0:T(8,128)} %get-tuple-element.40), channel_id=1, source_target_pairs={{0,1},{1,0},{2,3},{3,2},{4,5},{5,4},{6,7},{7,6},{8,9},{9,8},{10,11... | collective-permute-start | bytes 24584 | tf_op jit(solution)/shard_map/ppermute | solution.py:504
  5.7 3.9 %collective-permute-start.1 = (f32[2,8,128]{2,1,0:T(8,128)}, f32[2,8,128]{2,1,0:T(8,128)S(1)}, u32[]{:S(2)}, u32[]{:S(2)}) collective-permute-start(f32[2,8,128]{2,1,0:T(8,128)} %get-tuple-element.41), channel_id=1, source_target_pairs={{0,511},{1,2},{2,1},{3,4},{4,3},{5,6},{6,5},{7,8},{8,7},{9,10},{10... | collective-permute-start | bytes 24584 | tf_op jit(solution)/shard_map/ppermute | solution.py:503
  9.6 0.0 copy-start.5
  9.6 0.9 copy-done.5
  10.5 0.7 copy-done.7
  11.2 0.0 copy-start.6
  11.2 9.8 %local_pairs.4 = (f32[33,32,128]{2,1,0:T(8,128)S(1)}, bf16[32,48,256]{2,1,0:T(8,128)(2,1)S(1)}, f32[32,128,128]{2,1,0:T(8,128)S(1)}) custom-call(s32[584]{0:T(1024)S(1)} %copy-done.7, f32[32,8,128]{2,1,0:T(8,128)S(1)} %copy-done.5), custom_call_target="tpu_custom_call" | custom-call | flops 10000000000 | bytes 3500000 | tf_op jit(solution)/shard_map/local_pairs/pallas_call | solution.py:281
  21.0 0.0 collective-permute-done.refs_6_
  21.0 0.0 collective-permute-done.1.refs_7_
  21.1 0.0 copy-done
  21.1 0.0 copy-start.8
  21.1 2.4 %ghost_pairs.3 = (f32[32,8,128]{2,1,0:T(8,128)S(1)}, f32[2,8,128]{2,1,0:T(8,128)S(1)}, f32[2,8,128]{2,1,0:T(8,128)S(1)}) custom-call(s32[1]{0:T(128)} %bitcast.par_ref.refs_0_, s32[2,2]{1,0:T(2,128)S(1)} %copy-done.2, s32[584]{0:T(1024)S(1)} %copy-done.7, s32[32]{0:T(128)S(1)} %bitcast.11, s32[32,128]{1,0:T(8,128)S(1)} %bitcast.6, ...), custom_call_target="tpu_custom_call" | custom-call | flops 2000000000 | bytes 2000000 | tf_op jit(solution)/shard_map/ghost_pairs/pallas_call | solution.py:394
  23.6 11.8 %collective-permute-start.2 = (f32[2,8,128]{2,1,0:T(8,128)S(1)}, f32[2,8,128]{2,1,0:T(8,128)S(1)}, u32[]{:S(2)}, u32[]{:S(2)}) collective-permute-start(f32[2,8,128]{2,1,0:T(8,128)S(1)} %get-tuple-element.46), channel_id=1, source_target_pairs={{0,1},{1,0},{2,3},{3,2},{4,5},{5,4},{6,7},{7,6},{8,9},{9,8},{10,11... | collective-permute-start | bytes 24584 | tf_op jit(solution)/shard_map/ppermute | solution.py:504
  35.3 1.9 %collective-permute-start.3 = (f32[2,8,128]{2,1,0:T(8,128)S(1)}, f32[2,8,128]{2,1,0:T(8,128)S(1)}, u32[]{:S(2)}, u32[]{:S(2)}) collective-permute-start(f32[2,8,128]{2,1,0:T(8,128)S(1)} %get-tuple-element.47), channel_id=1, source_target_pairs={{0,511},{1,2},{2,1},{3,4},{4,3},{5,6},{6,5},{7,8},{8,7},{9,10},{10... | collective-permute-start | bytes 24584 | tf_op jit(solution)/shard_map/ppermute | solution.py:503
  37.2 0.0 copy-done.8
  37.3 9.2 %local_pairs.5 = (f32[33,32,128]{2,1,0:T(8,128)S(1)}, bf16[32,48,256]{2,1,0:T(8,128)(2,1)S(1)}) custom-call(s32[584]{0:T(1024)S(1)} %copy-done.8, f32[32,8,128]{2,1,0:T(8,128)S(1)} %get-tuple-element.45.refs_1_.refs_5_, f32[32,128,128]{2,1,0:T(8,128)S(1)} %get-tuple-element.48.refs_2_), custom_call_target="tpu_custom_call" | custom-call | flops 10000000000 | bytes 3500000 | tf_op jit(solution)/shard_map/local_pairs/pallas_call | solution.py:281
  46.4 0.0 collective-permute-done.2.refs_6_
  46.4 0.0 collective-permute-done.3.refs_7_
  46.4 2.4 %ghost_pairs.4 = (f32[32,8,128]{2,1,0:T(8,128)S(1)}, f32[2,8,128]{2,1,0:T(8,128)S(1)}, f32[2,8,128]{2,1,0:T(8,128)S(1)}) custom-call(s32[1]{0:T(128)} %bitcast.par_ref.refs_0_, s32[2,2]{1,0:T(2,128)S(1)} %copy-done.2, s32[584]{0:T(1024)S(1)} %copy-done.8, s32[32]{0:T(128)S(1)} %bitcast.12, s32[32,128]{1,0:T(8,128)S(1)} %bitcast.7, ...), custom_call_target="tpu_custom_call" | custom-call | flops 2000000000 | bytes 2000000 | tf_op jit(solution)/shard_map/ghost_pairs/pallas_call | solution.py:394
  48.9 2.6 %collective-permute-start.4 = (f32[2,8,128]{2,1,0:T(8,128)S(1)}, f32[2,8,128]{2,1,0:T(8,128)S(1)}, u32[]{:S(2)}, u32[]{:S(2)}) collective-permute-start(f32[2,8,128]{2,1,0:T(8,128)S(1)} %get-tuple-element.52), channel_id=1, source_target_pairs={{0,1},{1,0},{2,3},{3,2},{4,5},{5,4},{6,7},{7,6},{8,9},{9,8},{10,11... | collective-permute-start | bytes 24584 | tf_op jit(solution)/shard_map/ppermute | solution.py:504
  51.4 2.4 %collective-permute-start.5 = (f32[2,8,128]{2,1,0:T(8,128)S(1)}, f32[2,8,128]{2,1,0:T(8,128)S(1)}, u32[]{:S(2)}, u32[]{:S(2)}) collective-permute-start(f32[2,8,128]{2,1,0:T(8,128)S(1)} %get-tuple-element.53), channel_id=1, source_target_pairs={{0,511},{1,2},{2,1},{3,4},{4,3},{5,6},{6,5},{7,8},{8,7},{9,10},{10... | collective-permute-start | bytes 24584 | tf_op jit(solution)/shard_map/ppermute | solution.py:503
  53.8 9.2 %local_pairs.6 = (f32[33,32,128]{2,1,0:T(8,128)S(1)}, bf16[32,48,256]{2,1,0:T(8,128)(2,1)S(1)}) custom-call(s32[584]{0:T(1024)S(1)} %copy-done.8, f32[32,8,128]{2,1,0:T(8,128)S(1)} %get-tuple-element.51.refs_1_.refs_5_, f32[32,128,128]{2,1,0:T(8,128)S(1)} %get-tuple-element.48.refs_2_), custom_call_target="tpu_custom_call" | custom-call | flops 10000000000 | bytes 3500000 | tf_op jit(solution)/shard_map/local_pairs/pallas_call | solution.py:281
  63.0 0.0 collective-permute-done.4.refs_6_
  63.0 0.0 collective-permute-done.5.refs_7_
  63.0 2.4 %ghost_pairs.5 = (f32[32,8,128]{2,1,0:T(8,128)S(1)}, f32[2,8,128]{2,1,0:T(8,128)S(1)}, f32[2,8,128]{2,1,0:T(8,128)S(1)}) custom-call(s32[1]{0:T(128)} %bitcast.par_ref.refs_0_, s32[2,2]{1,0:T(2,128)S(1)} %copy-done.2, s32[584]{0:T(1024)S(1)} %copy-done.8, s32[32]{0:T(128)S(1)} %bitcast.13, s32[32,128]{1,0:T(8,128)S(1)} %bitcast.8, ...), custom_call_target="tpu_custom_call" | custom-call | flops 2000000000 | bytes 2000000 | tf_op jit(solution)/shard_map/ghost_pairs/pallas_call | solution.py:394
  65.5 6.4 %collective-permute-start.6 = (f32[2,8,128]{2,1,0:T(8,128)S(1)}, f32[2,8,128]{2,1,0:T(8,128)S(1)}, u32[]{:S(2)}, u32[]{:S(2)}) collective-permute-start(f32[2,8,128]{2,1,0:T(8,128)S(1)} %get-tuple-element.57), channel_id=1, source_target_pairs={{0,1},{1,0},{2,3},{3,2},{4,5},{5,4},{6,7},{7,6},{8,9},{9,8},{10,11... | collective-permute-start | bytes 24584 | tf_op jit(solution)/shard_map/ppermute | solution.py:504
  71.8 1.9 %collective-permute-start.7 = (f32[2,8,128]{2,1,0:T(8,128)S(1)}, f32[2,8,128]{2,1,0:T(8,128)S(1)}, u32[]{:S(2)}, u32[]{:S(2)}) collective-permute-start(f32[2,8,128]{2,1,0:T(8,128)S(1)} %get-tuple-element.58), channel_id=1, source_target_pairs={{0,511},{1,2},{2,1},{3,4},{4,3},{5,6},{6,5},{7,8},{8,7},{9,10},{10... | collective-permute-start | bytes 24584 | tf_op jit(solution)/shard_map/ppermute | solution.py:503
  73.7 9.1 %local_pairs.7 = (f32[33,32,128]{2,1,0:T(8,128)S(1)}, bf16[32,48,256]{2,1,0:T(8,128)(2,1)S(1)}) custom-call(s32[584]{0:T(1024)S(1)} %copy-done.8, f32[32,8,128]{2,1,0:T(8,128)S(1)} %get-tuple-element.56.refs_1_.refs_5_, f32[32,128,128]{2,1,0:T(8,128)S(1)} %get-tuple-element.48.refs_2_), custom_call_target="tpu_custom_call" | custom-call | flops 10000000000 | bytes 3500000 | tf_op jit(solution)/shard_map/local_pairs/pallas_call | solution.py:281
  82.9 0.0 collective-permute-done.6.refs_6_
  82.9 0.0 collective-permute-done.7.refs_7_
  82.9 4.7 %ghost_pairs_last.1 = (f32[3,4096]{1,0:T(4,128)}, f32[3,4096]{1,0:T(4,128)}, f32[64,5,4,128]{3,2,1,0:T(4,128)S(1)}, f32[64,5,4,128]{3,2,1,0:T(4,128)S(1)}) custom-call(s32[1]{0:T(128)} %bitcast.par_ref.refs_0_, s32[2,2]{1,0:T(2,128)S(1)} %copy-done.2, s32[584]{0:T(1024)S(1)} %copy-done.8, s32[32]{0:T(128)S(1)} %bitcast.14, s32[32,128]{1,0:T(8,128)S(1)} %bitcast.9, ...), custom_call_target="tpu_custom_call" | custom-call | flops 2000000000 | bytes 2000000 | tf_op jit(solution)/shard_map/ghost_pairs_last/pallas_call | solution.py:394
  87.6 2.7 %collective-permute-start.8 = (f32[64,5,4,128]{3,2,1,0:T(4,128)S(1)}, f32[64,5,4,128]{3,2,1,0:T(4,128)S(1)}, u32[]{:S(2)}, u32[]{:S(2)}) collective-permute-start(f32[64,5,4,128]{3,2,1,0:T(4,128)S(1)} %get-tuple-element.64), channel_id=1, source_target_pairs={{0,1},{1,0},{2,3},{3,2},{4,5},{5,4},{6,7},{7,6},{8,9},{9,8},{10,11... | collective-permute-start | bytes 1966088 | tf_op jit(solution)/shard_map/ppermute | solution.py:529
  90.3 1.7 %collective-permute-done.8 = f32[64,5,4,128]{3,2,1,0:T(4,128)S(1)} collective-permute-done((f32[64,5,4,128]{3,2,1,0:T(4,128)S(1)}, f32[64,5,4,128]{3,2,1,0:T(4,128)S(1)}, u32[]{:S(2)}, u32[]{:S(2)}) %collective-permute-start.8) | collective-permute-done | bytes 655392 | tf_op jit(solution)/shard_map/ppermute | solution.py:529
  92.0 1.0 add.3
  93.0 10.8 %all-to-all-start = ((f32[64,5,4,128]{3,2,1,0:T(4,128)}), f32[64,5,4,128]{3,2,1,0:T(4,128)S(1)}, u32[]{:S(2)}, u32[]{:S(2)}) async-start(f32[64,5,4,128]{3,2,1,0:T(4,128)} %add.3), calls=%async_computation | async-start | bytes 1310720 | tf_op jit(solution)/shard_map/all_to_all | solution.py:530
  103.8 19.3 %all-to-all-done.dep_ref = f32[64,5,4,128]{3,2,1,0:T(4,128)S(1)} async-done(((f32[64,5,4,128]{3,2,1,0:T(4,128)}), f32[64,5,4,128]{3,2,1,0:T(4,128)S(1)}, u32[]{:S(2)}, u32[]{:S(2)}) %all-to-all-start) | async-done | bytes 655392 | tf_op jit(solution)/shard_map/all_to_all | solution.py:530
  123.1 0.7 known.1
  123.8 5.3 %collective-permute-start.10 = (f32[8,128]{1,0:T(8,128)S(1)}, f32[8,128]{1,0:T(8,128)S(1)}, u32[]{:S(2)}, u32[]{:S(2)}) collective-permute-start(f32[8,128]{1,0:T(8,128)S(1)} %get-tuple-element.71), channel_id=1, source_target_pairs={{0,511},{1,2},{2,1},{3,4},{4,3},{5,6},{6,5},{7,8},{8,7},{9,10},{10... | collective-permute-start | bytes 12296 | tf_op jit(solution)/shard_map/ppermute | solution.py:503
  129.1 1.9 %collective-permute-start.9 = (f32[8,128]{1,0:T(8,128)S(1)}, f32[8,128]{1,0:T(8,128)S(1)}, u32[]{:S(2)}, u32[]{:S(2)}) collective-permute-start(f32[8,128]{1,0:T(8,128)S(1)} %get-tuple-element.72), channel_id=1, source_target_pairs={{0,1},{1,0},{2,3},{3,2},{4,5},{5,4},{6,7},{7,6},{8,9},{9,8},{10,11... | collective-permute-start | bytes 12296 | tf_op jit(solution)/shard_map/ppermute | solution.py:504
  131.0 0.0 collective-permute-done.10.far_ref
  131.1 1.1 collective-permute-done.9.near_ref
  132.2 0.9 sweeps.1
  133.1 0.1 broadcast_in_dim.2
  133.1 21.6 %all_to_all.10.mine_ref = f32[64,3,4,128]{3,2,1,0:T(4,128)S(1)} all-to-all(f32[64,3,4,128]{3,2,1,0:T(4,128)S(1)} %broadcast_in_dim.2), channel_id=1, replica_groups={{0,2,4,6,8,10,12,14,16,18,20,22,24,26,28,30,32,34,36,38,40,42,44,46,48,..., dimensions={0} | all-to-all | bytes 786432 | tf_op jit(solution)/shard_map/all_to_all | solution.py:563
  154.8 5.4 %collective-permute-start.11 = (f32[64,3,4,128]{3,2,1,0:T(4,128)S(1)}, f32[64,3,4,128]{3,2,1,0:T(4,128)S(1)}, u32[]{:S(2)}, u32[]{:S(2)}) collective-permute-start(f32[64,3,4,128]{3,2,1,0:T(4,128)S(1)} %all_to_all.10.mine_ref), channel_id=1, source_target_pairs={{0,1},{1,0},{2,3},{3,2},{4,5},{5,4},{6,7},{7,6},{8,9},{9,8},{10,11... | collective-permute-start | bytes 1179656 | tf_op jit(solution)/shard_map/ppermute | solution.py:564
  160.2 1.3 collective-permute-done.11.other_ref
  161.5 1.7 %pick.1 = f32[3,4096]{1,0:T(4,128)} custom-call(s32[1]{0:T(128)} %bitcast.par_ref.refs_0_, s32[32]{0:T(128)S(1)} %bitcast.15, s32[32,128]{1,0:T(8,128)S(1)} %bitcast.10, f32[64,3,4,128]{3,2,1,0:T(4,128)S(1)} %all_to_all.10.mine_ref, f32[64,3,4,128]{3,2,1,0:T(4,128)S(1)} %collective-permute-done.11.other_ref), custom_call_target="tpu_custom_call" | custom-call | flops 60000000 | bytes 900000 | tf_op jit(solution)/shard_map/pick/pallas_call | solution.py:565
  (12 shorter events, 0.0 us)
Async XLA Ops:
  3.1 17.9 %collective-permute-start = (f32[2,8,128]{2,1,0:T(8,128)}, f32[2,8,128]{2,1,0:T(8,128)S(1)}, u32[]{:S(2)}, u32[]{:S(2)}) collective-permute-start(f32[2,8,128]{2,1,0:T(8,128)} %get-tuple-element.40), channel_id=1, source_target_pairs={{0,1},{1,0},{2,3},{3,2},{4,5},{5,4},{6,7},{7,6},{8,9},{9,8},{10,11... | collective-permute-start | bytes 24584 | tf_op jit(solution)/shard_map/ppermute | solution.py:504
  5.7 15.4 %collective-permute-start.1 = (f32[2,8,128]{2,1,0:T(8,128)}, f32[2,8,128]{2,1,0:T(8,128)S(1)}, u32[]{:S(2)}, u32[]{:S(2)}) collective-permute-start(f32[2,8,128]{2,1,0:T(8,128)} %get-tuple-element.41), channel_id=1, source_target_pairs={{0,511},{1,2},{2,1},{3,4},{4,3},{5,6},{6,5},{7,8},{8,7},{9,10},{10... | collective-permute-start | bytes 24584 | tf_op jit(solution)/shard_map/ppermute | solution.py:503
  9.6 0.9 copy-start.5
  10.5 0.7 copy-start.7
  11.2 9.9 %copy-start = (s32[4096]{0:T(1024)S(1)}, s32[4096]{0:T(1024)}, u32[]{:S(2)}) copy-start(s32[4096]{0:T(1024)} %param.20) | copy-start | bytes 49156
  11.2 9.9 %copy-start.2 = (s32[2,2]{1,0:T(2,128)S(1)}, s32[2,2]{1,0:T(2,128)}, u32[]{:S(2)}) copy-start(s32[2,2]{1,0:T(2,128)} %refs_1_.7) | copy-start | bytes 52
  11.2 9.9 %copy-start.3 = (s32[32,1]{0,1:T(1,128)S(1)}, s32[32,1]{0,1:T(1,128)}, u32[]{:S(2)}) copy-start(s32[32,1]{0,1:T(1,128)} %param.19) | copy-start | bytes 388
  11.2 9.9 %copy-start.4 = (f32[32,8,128]{2,1,0:T(8,128)S(1)}, f32[32,8,128]{2,1,0:T(8,128)}, u32[]{:S(2)}) copy-start(f32[32,8,128]{2,1,0:T(8,128)} %get-tuple-element.42.refs_8_) | copy-start | bytes 393220
  11.2 9.9 %copy-start.6 = (f32[32,8,128]{2,1,0:T(8,128)S(1)}, f32[32,8,128]{2,1,0:T(8,128)}, u32[]{:S(2)}) copy-start(f32[32,8,128]{2,1,0:T(8,128)} %get-tuple-element.39.refs_1_.refs_5_) | copy-start | bytes 393220
  21.1 16.1 %copy-start.8 = (s32[584]{0:T(1024)S(1)}, s32[584]{0:T(1024)}, u32[]{:S(2)}) copy-start(s32[584]{0:T(1024)} %get-tuple-element.38.refs_0_.refs_2_) | copy-start | bytes 7012
  23.6 22.9 %collective-permute-start.2 = (f32[2,8,128]{2,1,0:T(8,128)S(1)}, f32[2,8,128]{2,1,0:T(8,128)S(1)}, u32[]{:S(2)}, u32[]{:S(2)}) collective-permute-start(f32[2,8,128]{2,1,0:T(8,128)S(1)} %get-tuple-element.46), channel_id=1, source_target_pairs={{0,1},{1,0},{2,3},{3,2},{4,5},{5,4},{6,7},{7,6},{8,9},{9,8},{10,11... | collective-permute-start | bytes 24584 | tf_op jit(solution)/shard_map/ppermute | solution.py:504
  35.3 11.1 %collective-permute-start.3 = (f32[2,8,128]{2,1,0:T(8,128)S(1)}, f32[2,8,128]{2,1,0:T(8,128)S(1)}, u32[]{:S(2)}, u32[]{:S(2)}) collective-permute-start(f32[2,8,128]{2,1,0:T(8,128)S(1)} %get-tuple-element.47), channel_id=1, source_target_pairs={{0,511},{1,2},{2,1},{3,4},{4,3},{5,6},{6,5},{7,8},{8,7},{9,10},{10... | collective-permute-start | bytes 24584 | tf_op jit(solution)/shard_map/ppermute | solution.py:503
  48.9 14.1 %collective-permute-start.4 = (f32[2,8,128]{2,1,0:T(8,128)S(1)}, f32[2,8,128]{2,1,0:T(8,128)S(1)}, u32[]{:S(2)}, u32[]{:S(2)}) collective-permute-start(f32[2,8,128]{2,1,0:T(8,128)S(1)} %get-tuple-element.52), channel_id=1, source_target_pairs={{0,1},{1,0},{2,3},{3,2},{4,5},{5,4},{6,7},{7,6},{8,9},{9,8},{10,11... | collective-permute-start | bytes 24584 | tf_op jit(solution)/shard_map/ppermute | solution.py:504
  51.4 11.6 %collective-permute-start.5 = (f32[2,8,128]{2,1,0:T(8,128)S(1)}, f32[2,8,128]{2,1,0:T(8,128)S(1)}, u32[]{:S(2)}, u32[]{:S(2)}) collective-permute-start(f32[2,8,128]{2,1,0:T(8,128)S(1)} %get-tuple-element.53), channel_id=1, source_target_pairs={{0,511},{1,2},{2,1},{3,4},{4,3},{5,6},{6,5},{7,8},{8,7},{9,10},{10... | collective-permute-start | bytes 24584 | tf_op jit(solution)/shard_map/ppermute | solution.py:503
  65.5 17.4 %collective-permute-start.6 = (f32[2,8,128]{2,1,0:T(8,128)S(1)}, f32[2,8,128]{2,1,0:T(8,128)S(1)}, u32[]{:S(2)}, u32[]{:S(2)}) collective-permute-start(f32[2,8,128]{2,1,0:T(8,128)S(1)} %get-tuple-element.57), channel_id=1, source_target_pairs={{0,1},{1,0},{2,3},{3,2},{4,5},{5,4},{6,7},{7,6},{8,9},{9,8},{10,11... | collective-permute-start | bytes 24584 | tf_op jit(solution)/shard_map/ppermute | solution.py:504
  71.8 11.1 %collective-permute-start.7 = (f32[2,8,128]{2,1,0:T(8,128)S(1)}, f32[2,8,128]{2,1,0:T(8,128)S(1)}, u32[]{:S(2)}, u32[]{:S(2)}) collective-permute-start(f32[2,8,128]{2,1,0:T(8,128)S(1)} %get-tuple-element.58), channel_id=1, source_target_pairs={{0,511},{1,2},{2,1},{3,4},{4,3},{5,6},{6,5},{7,8},{8,7},{9,10},{10... | collective-permute-start | bytes 24584 | tf_op jit(solution)/shard_map/ppermute | solution.py:503
  87.6 35.6 %copy-start.1 = (f32[3,512]{1,0:T(4,128)S(1)}, f32[3,512]{1,0:T(4,128)}, u32[]{:S(2)}) copy-start(f32[3,512]{1,0:T(4,128)} %gas_ref.1) | copy-start | bytes 18436
  87.6 4.4 %collective-permute-start.8 = (f32[64,5,4,128]{3,2,1,0:T(4,128)S(1)}, f32[64,5,4,128]{3,2,1,0:T(4,128)S(1)}, u32[]{:S(2)}, u32[]{:S(2)}) collective-permute-start(f32[64,5,4,128]{3,2,1,0:T(4,128)S(1)} %get-tuple-element.64), channel_id=1, source_target_pairs={{0,1},{1,0},{2,3},{3,2},{4,5},{5,4},{6,7},{7,6},{8,9},{9,8},{10,11... | collective-permute-start | bytes 1966088 | tf_op jit(solution)/shard_map/ppermute | solution.py:529
  93.0 30.2 %all-to-all-start = ((f32[64,5,4,128]{3,2,1,0:T(4,128)}), f32[64,5,4,128]{3,2,1,0:T(4,128)S(1)}, u32[]{:S(2)}, u32[]{:S(2)}) async-start(f32[64,5,4,128]{3,2,1,0:T(4,128)} %add.3), calls=%async_computation | async-start | bytes 1310720 | tf_op jit(solution)/shard_map/all_to_all | solution.py:530
  123.8 7.3 %collective-permute-start.10 = (f32[8,128]{1,0:T(8,128)S(1)}, f32[8,128]{1,0:T(8,128)S(1)}, u32[]{:S(2)}, u32[]{:S(2)}) collective-permute-start(f32[8,128]{1,0:T(8,128)S(1)} %get-tuple-element.71), channel_id=1, source_target_pairs={{0,511},{1,2},{2,1},{3,4},{4,3},{5,6},{6,5},{7,8},{8,7},{9,10},{10... | collective-permute-start | bytes 12296 | tf_op jit(solution)/shard_map/ppermute | solution.py:503
  129.1 3.1 %collective-permute-start.9 = (f32[8,128]{1,0:T(8,128)S(1)}, f32[8,128]{1,0:T(8,128)S(1)}, u32[]{:S(2)}, u32[]{:S(2)}) collective-permute-start(f32[8,128]{1,0:T(8,128)S(1)} %get-tuple-element.72), channel_id=1, source_target_pairs={{0,1},{1,0},{2,3},{3,2},{4,5},{5,4},{6,7},{7,6},{8,9},{9,8},{10,11... | collective-permute-start | bytes 12296 | tf_op jit(solution)/shard_map/ppermute | solution.py:504
  154.8 6.8 %collective-permute-start.11 = (f32[64,3,4,128]{3,2,1,0:T(4,128)S(1)}, f32[64,3,4,128]{3,2,1,0:T(4,128)S(1)}, u32[]{:S(2)}, u32[]{:S(2)}) collective-permute-start(f32[64,3,4,128]{3,2,1,0:T(4,128)S(1)} %all_to_all.10.mine_ref), channel_id=1, source_target_pairs={{0,1},{1,0},{2,3},{3,2},{4,5},{5,4},{6,7},{7,6},{8,9},{9,8},{10,11... | collective-permute-start | bytes 1179656 | tf_op jit(solution)/shard_map/ppermute | solution.py:564
